TPU v7x, 128 devices: a whole 4x4x4 slice. The times are simulated.
128 devices in a mesh: node: 8 (over y, core), local: 16 (over x, z).
Axes of the slice: x: 4, y: 4, z: 4, core: 2. Of those that a mesh axis runs over, the one named last changes fastest.
Arguments:
- tokens: bfloat16 [8192, 3584], P(('node', 'local')), may hold values from -6 to 6
- expert_ids: int32 [8192, 8], P(('node', 'local')), may hold values from 0 to 127, as said below
- gate_values: bfloat16 [8192, 8], P(('node', 'local')), may hold values from 0.049804688 to 0.44921875
- expert_gate: bfloat16 [128, 3584, 1024], P(('node', 'local')), may hold values from -0.09375 to 0.09375
- expert_up: bfloat16 [128, 3584, 1024], P(('node', 'local')), may hold values from -0.09375 to 0.09375
- expert_down: bfloat16 [128, 1024, 3584], P(('node', 'local')), may hold values from -0.1875 to 0.1875
Outputs:
- mixed: bfloat16 [8192, 3584], P(('node', 'local'))
Inputs may be any that keep to these rules, and one draw needn't show every extreme that they name: `expert_ids`: each row names 8 different experts, the same number on each of exactly 4 nodes. Among the rows of one device, each node is named by exactly 32 rows, no expert is named more than 8 times, and on every node some expert is named exactly 8 times.
All inputs are finite; a program needn't handle non-finite values.
Results may differ from a plain program's by a relative error of at most 0.012.
Values may be sent and summed in bfloat16 or wider, within the bound.
No kernel may reach another device: no remote copies, remote signals or barrier semaphores. Data moves between devices by JAX's collectives and lax.ppermute only.
A program may use at most 128 MiB of HBM per device.

v0:
```python
import jax
import jax.numpy as jnp
from jax import lax
from jax.sharding import PartitionSpec as P


def expert_rows(rows, w_gate, w_up, w_down):
    shape = rows.shape
    flat = rows.reshape(-1, shape[-1])
    gate_rows = jnp.dot(flat, w_gate, preferred_element_type=jnp.float32)
    up_rows = jnp.dot(flat, w_up, preferred_element_type=jnp.float32)
    hidden = (jax.nn.silu(gate_rows) * up_rows).astype(jnp.bfloat16)
    output = jnp.dot(hidden, w_down, preferred_element_type=jnp.float32).astype(jnp.bfloat16)
    return output.reshape(shape)


def shards(tokens, expert_ids, gate_values, expert_gate, expert_up, expert_down):
    nodes = lax.axis_size("node")
    per_node = lax.axis_size("local")
    experts = nodes * per_node
    tok_rows, width = tokens.shape
    top = expert_ids.shape[1]
    cap = 2 * tok_rows * top // experts
    w_gate = expert_gate[0]
    w_up = expert_up[0]
    w_down = expert_down[0]
    hits = (expert_ids[:, :, None] == jnp.arange(experts, dtype=jnp.int32)[None, None, :]).astype(
        jnp.int32
    )
    flat_hits = hits.reshape(tok_rows * top, experts)
    earlier = jnp.cumsum(flat_hits, axis=0) - flat_hits
    slot = jnp.sum(earlier * flat_hits, axis=1).reshape(tok_rows, top)
    position = expert_ids * cap + slot
    places = jnp.arange(experts * cap, dtype=jnp.int32)
    chosen = places[:, None, None] == position[None, :, :]
    dispatch = jnp.any(chosen, axis=2).astype(jnp.bfloat16)
    weights = jnp.sum(
        jnp.where(chosen, gate_values[None, :, :].astype(jnp.float32), jnp.float32(0.0)), axis=2
    )
    send = jnp.dot(dispatch, tokens, preferred_element_type=jnp.float32).astype(jnp.bfloat16)
    back = lax.all_to_all(
        expert_rows(
            lax.all_to_all(
                send.reshape(experts, cap, width),
                ("node", "local"),
                split_axis=0,
                concat_axis=0,
                tiled=True,
            ),
            w_gate,
            w_up,
            w_down,
        ),
        ("node", "local"),
        split_axis=0,
        concat_axis=0,
        tiled=True,
    )
    mix = weights.astype(jnp.bfloat16).reshape(nodes, per_node * cap, tok_rows)
    node_part = jnp.einsum(
        "nct,ncd->ntd",
        mix,
        back.reshape(nodes, per_node * cap, width),
        preferred_element_type=jnp.float32,
    ).astype(jnp.bfloat16)
    return jnp.sum(node_part.astype(jnp.float32), axis=0).astype(jnp.bfloat16)


def solution(mesh):
    placed = (
        P(("node", "local"), None),
        P(("node", "local"), None),
        P(("node", "local"), None),
        P(("node", "local"), None, None),
        P(("node", "local"), None, None),
        P(("node", "local"), None, None),
    )
    return jax.shard_map(
        shards, mesh=mesh, in_specs=placed, out_specs=P(("node", "local"), None), check_vma=False
    )
```

profile of v0, /device:TPU:0, one launch (start us, length us, event | category | flops | bytes accessed | tf_op | source)
XLA Modules:
  0.0 229.6 jit_solution(6883830866495166072)
XLA Ops:
  0.0 0.0 copy-start
  0.0 0.8 copy.25
  0.8 0.1 eq.44
  0.9 0.1 eq.40
  1.0 0.1 copy.27
  1.1 0.2 fusion.19
  1.4 0.2 fusion.18
  1.7 0.1 reshape.40
  1.8 0.1 copy.29
  1.8 0.7 multiply_add_fusion
  2.5 0.1 copy.30
  2.6 0.7 fusion.15
  3.3 0.0 copy-done
  3.3 0.0 slice-start
  3.3 2.1 fusion.7
  5.5 0.0 slice-start.1
  5.5 0.0 slice-start.2
  5.5 96.6 %all_to_all.10 = bf16[128,8,3584]{2,1,0:T(8,128)(2,1)S(1)} all-to-all(bf16[128,8,3584]{2,1,0:T(8,128)(2,1)S(1)} %fusion.7), channel_id=1, replica_groups=mesh['node'=8,'local'=16] {'node','local'}, dimensions={0} | all-to-all | bytes 14680064 | tf_op jit(solution)/shard_map/all_to_all | solution.py:43
  102.0 0.0 slice-done
  102.0 0.0 slice-done.1
  102.1 0.0 slice-start.3
  102.1 7.7 %fusion.1 = f32[1024,1024]{1,0:T(8,128)S(1)} fusion(bf16[1,3584,1024]{2,1,0:T(8,128)(2,1)S(1)} %bitcast.55, bf16[128,8,3584]{2,1,0:T(8,128)(2,1)S(1)} %all_to_all.10), kind=kOutput, calls=%fused_computation.3 | convolution fusion | flops 7516192768 | bytes 18874368 | tf_op jit(solution)/shard_map/dot_general | solution.py:11
  109.8 0.0 slice-done.2
  109.8 0.0 slice-done.3
  109.8 8.6 %multiply_convert_fusion = bf16[1024,1024]{1,0:T(8,128)(2,1)S(1)} fusion(f32[1024,1024]{1,0:T(8,128)S(1)} %fusion.1, bf16[1,3584,1024]{2,1,0:T(8,128)(2,1)S(1)} %bitcast.57, bf16[128,8,3584]{2,1,0:T(8,128)(2,1)S(1)} %all_to_all.10), kind=kOutput, calls=%fused_computation.12 | convolution fusion | flops 7522484224 | bytes 20971520 | tf_op jit(solution)/shard_map/dot_general | solution.py:10
  118.4 12.8 %fusion.8 = bf16[128,8,3584]{2,1,0:T(8,128)(2,1)} fusion(bf16[1024,1024]{1,0:T(8,128)(2,1)S(1)} %multiply_convert_fusion, bf16[1,1024,3584]{2,1,0:T(8,128)(2,1)} %param.11), kind=kOutput, calls=%fused_computation.10 | convolution fusion | flops 7519862784 | bytes 16777216 | tf_op jit(solution)/shard_map/dot_general | solution.py:13
  131.2 6.0 %all-to-all-start.1 = ((bf16[128,8,3584]{2,1,0:T(8,128)(2,1)}), bf16[128,8,3584]{2,1,0:T(8,128)(2,1)}, u32[]{:S(2)}, u32[]{:S(2)}) async-start(bf16[128,8,3584]{2,1,0:T(8,128)(2,1)} %fusion.8), calls=%async_computation.1 | async-start | bytes 14680064 | tf_op jit(solution)/shard_map/all_to_all | solution.py:41
  137.2 0.0 copy-done.1
  137.2 0.1 copy.31
  137.3 0.7 select_reduce_fusion
  138.0 86.4 %all-to-all-done.1 = bf16[128,8,3584]{2,1,0:T(8,128)(2,1)} async-done(((bf16[128,8,3584]{2,1,0:T(8,128)(2,1)}), bf16[128,8,3584]{2,1,0:T(8,128)(2,1)}, u32[]{:S(2)}, u32[]{:S(2)}) %all-to-all-start.1) | async-done | bytes 7340064 | tf_op jit(solution)/shard_map/all_to_all | solution.py:41
  224.5 5.1 %fusion.16 = bf16[64,3584]{1,0:T(8,128)(2,1)} fusion(bf16[8,128,3584]{2,1,0:T(8,128)(2,1)} %bitcast.9, bf16[1024,64]{0,1:T(8,128)(2,1)S(1)} %select_reduce_fusion), kind=kOutput, calls=%fused_computation.16 | convolution fusion | flops 473202688 | bytes 7929856 | tf_op jit(solution)/shard_map/nct,ncd->ntd/dot_general | solution.py:60
  (9 shorter events, 0.1 us)
Async XLA Ops:
  0.0 3.3 %copy-start = (bf16[64,3584]{1,0:T(8,128)(2,1)S(1)}, bf16[64,3584]{1,0:T(8,128)(2,1)}, u32[]{:S(2)}) copy-start(bf16[64,3584]{1,0:T(8,128)(2,1)} %param.6) | copy-start | bytes 1376260
  3.3 98.7 %slice-start = ((s8[7340032]{0:T(1024)(128)(4,1)}), s8[4194304]{0:T(1024)(128)(4,1)S(1)}, s32[]{:S(2)}) async-start(s8[7340032]{0:T(1024)(128)(4,1)} %bitcast.54), calls=%async_computation.2 | async-start | bytes 8388608
  5.5 96.6 %slice-start.1 = ((s8[7340032]{0:T(1024)(128)(4,1)}), s8[3145728]{0:T(1024)(128)(4,1)S(1)}, s32[]{:S(2)}) async-start(s8[7340032]{0:T(1024)(128)(4,1)} %bitcast.54), calls=%async_computation.3 | async-start | bytes 6291456
  5.5 104.3 %slice-start.2 = ((s8[7340032]{0:T(1024)(128)(4,1)}), s8[4194304]{0:T(1024)(128)(4,1)S(1)}, s32[]{:S(2)}) async-start(s8[7340032]{0:T(1024)(128)(4,1)} %bitcast.56), calls=%async_computation.4 | async-start | bytes 8388608
  102.1 7.7 %slice-start.3 = ((s8[7340032]{0:T(1024)(128)(4,1)}), s8[3145728]{0:T(1024)(128)(4,1)S(1)}, s32[]{:S(2)}) async-start(s8[7340032]{0:T(1024)(128)(4,1)} %bitcast.56), calls=%async_computation.5 | async-start | bytes 6291456
  131.2 6.0 %copy-start.1 = (bf16[64,8]{0,1:T(8,128)(2,1)S(1)}, bf16[64,8]{0,1:T(8,128)(2,1)}, u32[]{:S(2)}) copy-start(bf16[64,8]{0,1:T(8,128)(2,1)} %param.8) | copy-start | bytes 3076
  131.2 93.3 %all-to-all-start.1 = ((bf16[128,8,3584]{2,1,0:T(8,128)(2,1)}), bf16[128,8,3584]{2,1,0:T(8,128)(2,1)}, u32[]{:S(2)}, u32[]{:S(2)}) async-start(bf16[128,8,3584]{2,1,0:T(8,128)(2,1)} %fusion.8), calls=%async_computation.1 | async-start | bytes 14680064 | tf_op jit(solution)/shard_map/all_to_all | solution.py:41
where the time goes:
time: 232 us; the launch traced here: 230 us
  blocking collectives  96.6 us (42%)
  waiting for transfers between devices  86.4 us (37%)
  matrix products  36.3 us (16%)
  starting transfers between devices  5.97 us (3%)
  other arithmetic  2.62 us (1%)
    all_to_all x1, blocking collectives, shards(): lax.all_to_all(send.reshape(experts, cap, width), ('node', 'local'), spli...  96.6 us
    all_to_all x1, waiting for transfers between devices, shards(): lax.all_to_all(expert_rows(lax.all_to_all(send.reshape(experts, cap, widt...  86.4 us
    dot_general x1, matrix products, expert_rows(): jnp.dot(hidden, w_down, preferred_element_type=jnp.float32)  12.8 us
    dot_general x1, matrix products, expert_rows(): gate_rows = jnp.dot(flat, w_gate, preferred_element_type=jnp.float32)  8.57 us
    dot_general x1, matrix products, expert_rows(): up_rows = jnp.dot(flat, w_up, preferred_element_type=jnp.float32)  7.72 us
    all_to_all x1, starting transfers between devices, shards(): lax.all_to_all(expert_rows(lax.all_to_all(send.reshape(experts, cap, widt...  5.97 us
    dot_general x1, matrix products, shards(): jnp.einsum('nct,ncd->ntd', mix, back.reshape(nodes, per_node * cap, width...  5.06 us
  transfers between devices with their start and end apart: 1, of which 1 were waited for; matrix products, arithmetic and copies ran while one was open for 0% of the time, Pallas kernels for 0%

commit v1 on v0

v1 whole, which is shorter than its diff:
```python
import jax
import jax.numpy as jnp
from jax import lax
from jax.sharding import PartitionSpec as P

BOTH = ("node", "local")
RING = 4
LANES = 128

OFFSETS = ((0, 1, 3, 2), (0, 3, 1, 2))

ORDERS = (("z", "x", "y"), ("y", "z", "x"), ("x", "y", "z"))
AXES = ("y", "x", "z")


def index_of(y, c, x, z):
    return ((y * 2 + c) * RING + x) * RING + z


def pairs(axis, k):
    out = []
    for y in range(RING):
        for c in range(2):
            for x in range(RING):
                for z in range(RING):
                    at = {"y": y, "x": x, "z": z}
                    at[axis] ^= OFFSETS[c][k]
                    out.append((index_of(y, c, x, z), index_of(at["y"], c, at["x"], at["z"])))
    return out


def to_partner(value, axis, k):
    return lax.ppermute(value, BOTH, pairs(axis, k))


def to_other_core(value):
    swap = [(i, i ^ 16) for i in range(128)]
    return lax.ppermute(value, BOTH, swap)


def gather_ring(block, axis):
    pair = jnp.concatenate([block, to_partner(block, axis, 1)], axis=0)
    return jnp.concatenate([pair, to_partner(pair, axis, 2)], axis=0)


def add(a, b):
    return (a.astype(jnp.float32) + b.astype(jnp.float32)).astype(jnp.bfloat16)


def reduce_ring(blocks, axis):
    half = blocks.shape[0] // 2
    pair = add(blocks[:half], to_partner(blocks[half:], axis, 2))
    half = half // 2
    return add(pair[:half], to_partner(pair[half:], axis, 1))


def column_chunks(width):
    tiles = width // LANES
    cuts = [(tiles * i + 2) // 3 * LANES for i in range(3)] + [width]
    cuts[0] = 0
    return [(cuts[i], cuts[i + 1] - cuts[i]) for i in range(3)]


def shards(tokens, expert_ids, gate_values, expert_gate, expert_up, expert_down):
    node = lax.axis_index("node")
    local = lax.axis_index("local")
    at = {"y": node // 2, "x": local // RING, "z": local % RING}
    core = node % 2
    experts = lax.axis_size("node") * lax.axis_size("local")
    tok, width = tokens.shape
    top = expert_ids.shape[1]
    cap = 2 * tok * top // experts

    hits = (expert_ids[:, :, None] == jnp.arange(experts, dtype=jnp.int32)).astype(jnp.int32)
    named = jnp.sum(hits, axis=1)
    earlier = jnp.cumsum(named, axis=0) - named
    slot = jnp.sum(hits * earlier[:, None, :], axis=2)
    place = (expert_ids * cap + slot).astype(jnp.float32)
    about = jnp.concatenate([place, gate_values.astype(jnp.float32)], axis=1)
    about = lax.all_gather(about, BOTH)

    mine = jnp.where(core == 0, jnp.array(OFFSETS[0]), jnp.array(OFFSETS[1])).astype(jnp.int32)
    ring = jnp.arange(RING)

    def selection(order):
        first, second, last = order
        coord = {last: at[last], second: at[second] ^ mine[:, None], first: at[first] ^ mine[None, :]}
        source = index_of(coord["y"], core, coord["x"], coord["z"])
        source = jnp.broadcast_to(source, (RING, RING)).reshape(-1)
        known = jnp.take(about, source, axis=0)
        place = known[:, :, :top].astype(jnp.int32)
        weight = known[:, :, top:]
        held = jnp.arange(RING * RING, dtype=jnp.int32)
        have = (held[:, None, None] * (experts * cap) + place).reshape(-1, top)
        spot = dict(at)
        spot[last] = at[last] ^ mine
        expert = index_of(spot["y"], core, spot["x"], spot["z"])
        expert = jnp.stack([expert, expert ^ 16], axis=1)
        grid = held.reshape(RING, RING)
        if AXES.index(first) < AXES.index(second):
            grid = grid.T
        grid = grid.reshape(-1)
        want = (
            grid[None, None, :, None] * (experts * cap)
            + expert[:, :, None, None] * cap
            + jnp.arange(cap, dtype=jnp.int32)
        ).reshape(RING, -1)
        same = want[:, :, None, None] == have.T[None, None, :, :]
        chosen = jnp.any(same, axis=2).astype(jnp.bfloat16)
        weights = jnp.sum(
            jnp.where(same, weight.reshape(-1, top).T[None, None], jnp.float32(0.0)), axis=2
        ).astype(jnp.bfloat16)
        return chosen, weights

    chunks = column_chunks(width)
    picks = [selection(order) for order in ORDERS]

    def arrange(pieces, last):
        return jnp.stack(pieces, axis=AXES.index(last))

    def forward(number):
        start, size = chunks[number]
        first, second, last = ORDERS[number]
        chosen = picks[number][0]
        held = gather_ring(gather_ring(tokens[:, start : start + size], first), second)
        own, other = [], []
        for k in range(RING):
            rows = jnp.dot(chosen[k], held, preferred_element_type=jnp.float32).astype(jnp.bfloat16)
            if k:
                rows = to_partner(rows, last, k)
            half = rows.shape[0] // 2
            own.append(rows[:half])
            other.append(rows[half:])
        other = to_other_core(jnp.concatenate(other, axis=0))
        other = list(other.reshape(RING, -1, size))
        shape = (RING, RING, cap, size)
        both = [arrange([p.reshape(shape) for p in part], last).reshape(-1, size) for part in (own, other)]
        return jnp.concatenate(both, axis=0)

    rows = jnp.concatenate([forward(i) for i in range(3)], axis=1)
    gate_rows = jnp.dot(rows, expert_gate[0], preferred_element_type=jnp.float32)
    up_rows = jnp.dot(rows, expert_up[0], preferred_element_type=jnp.float32)
    hidden = (jax.nn.silu(gate_rows) * up_rows).astype(jnp.bfloat16)

    def backward(number):
        start, size = chunks[number]
        first, second, last = ORDERS[number]
        weights = picks[number][1]
        out = jnp.dot(
            hidden, expert_down[0][:, start : start + size], preferred_element_type=jnp.float32
        ).astype(jnp.bfloat16)
        out = out.reshape(2, RING, RING, RING, cap, size)
        out = jnp.moveaxis(out, 1 + AXES.index(last), 1)
        own = out[0].reshape(RING, -1, size)
        other = to_other_core(out[1].reshape(RING, -1, size))
        total = 0.0
        for k in range(RING):
            rows = jnp.concatenate([own[k], other[k]], axis=0)
            if k:
                rows = to_partner(rows, last, k)
            total = total + lax.dot_general(
                weights[k], rows, (((0,), (0,)), ((), ())), preferred_element_type=jnp.float32
            )
        return reduce_ring(reduce_ring(total.astype(jnp.bfloat16), second), first)

    return jnp.concatenate([backward(i) for i in range(3)], axis=1)


def solution(mesh):
    placed = (
        P(BOTH, None),
        P(BOTH, None),
        P(BOTH, None),
        P(BOTH, None, None),
        P(BOTH, None, None),
        P(BOTH, None, None),
    )
    return jax.shard_map(
        shards, mesh=mesh, in_specs=placed, out_specs=P(BOTH, None), check_vma=False
    )
```

time: 232 us -> 433 us (1.87)
  other arithmetic: 2.62 us -> 83.3 us
  starting transfers between devices: 5.97 us -> 59.9 us
  waiting for transfers between devices: 86.4 us -> 130 us
  matrix products: 36.3 us -> 77.7 us
  blocking collectives: 96.6 us -> 60.9 us
  local copies, waits for them, and re-layouts: 1.51 us -> 14.9 us
    ppermute x0 -> x48, waiting for transfers between devices: none -> 130 us  [the longest x42 129 us: to_partner(): return lax.ppermute(value, BOTH, pairs(axis, k))]
    all_to_all x1 -> x0, blocking collectives: 96.6 us -> none  [shards(): lax.all_to_all(send.reshape(experts, cap, width), ('node', 'local'), spli...]
    all_to_all x1 -> x0, waiting for transfers between devices: 86.4 us -> none  [shards(): lax.all_to_all(expert_rows(lax.all_to_all(send.reshape(experts, cap, widt...]
    all_gather x0 -> x1, blocking collectives: none -> 60.9 us  [shards(): about = lax.all_gather(about, BOTH)]
    ppermute x0 -> x48, starting transfers between devices: none -> 59.9 us  [the longest x42 58 us: to_partner(): return lax.ppermute(value, BOTH, pairs(axis, k))]
    dot_general x5 -> x29, matrix products: 36.3 us -> 77.7 us  [the longest x1 26.4 us: shards(): jnp.dot(rows, expert_gate[0], preferred_element_type=jnp.float32)]
    reduce_sum x2 -> x5, other arithmetic: 0.96 us -> 36.6 us  [the longest x3 35.2 us: selection(): jnp.sum(jnp.where(same, weight.reshape(-1, top).T[None, None], jnp.float3...]
    reduce_or x1 -> x3, other arithmetic: 0.69 us -> 35 us  [selection(): chosen = jnp.any(same, axis=2).astype(jnp.bfloat16)]
  transfers between devices with their start and end apart: 1 -> 48, of which waited for: 1 -> 22; matrix products, arithmetic and copies ran while one was open for 0% -> 27% of each run, Pallas kernels for 0% -> 0%
where the time goes in v1:
time: 433 us; the launch traced here: 428 us
  waiting for transfers between devices  130 us (30%)
  other arithmetic  83.3 us (19%)
  matrix products  77.7 us (18%)
  blocking collectives  60.9 us (14%)
  starting transfers between devices  59.9 us (14%)
  local copies, waits for them, and re-layouts  14.9 us (3%)
    ppermute x42, waiting for transfers between devices, to_partner(): return lax.ppermute(value, BOTH, pairs(axis, k))  129 us
    all_gather x1, blocking collectives, shards(): about = lax.all_gather(about, BOTH)  60.9 us
    ppermute x42, starting transfers between devices, to_partner(): return lax.ppermute(value, BOTH, pairs(axis, k))  58 us
    reduce_sum x3, other arithmetic, selection(): jnp.sum(jnp.where(same, weight.reshape(-1, top).T[None, None], jnp.float3...  35.2 us
    reduce_or x3, other arithmetic, selection(): chosen = jnp.any(same, axis=2).astype(jnp.bfloat16)  35 us
    dot_general x1, matrix products, shards(): jnp.dot(rows, expert_gate[0], preferred_element_type=jnp.float32)  26.4 us
    dot_general x3, matrix products, backward(): jnp.dot(hidden, expert_down[0][:, start:start + size], preferred_element_...  14.9 us
    dot_general x1, matrix products, shards(): up_rows = jnp.dot(rows, expert_up[0], preferred_element_type=jnp.float32)  13.6 us
  transfers between devices with their start and end apart: 48, of which 22 were waited for; matrix products, arithmetic and copies ran while one was open for 27% of the time, Pallas kernels for 0%

profile of v1, /device:TPU:0, one launch (start us, length us, event | category | flops | bytes accessed | tf_op | source)
XLA Modules:
  0.0 428.3 jit_solution(15701905950349551372)
XLA Ops:
  13.2 60.9 %all-gather.1 = f32[128,64,16]{1,2,0:T(8,128)S(1)} all-gather(f32[1,64,16]{1,2,0:T(8,128)S(1)} %maximum_bitcast_fusion), channel_id=2, replica_groups=mesh['node'=8,'local'=16] {'node','local'}, dimensions={0}, use_global_device_ids=true | all-gather | bytes 528384 | tf_op jit(solution)/shard_map/all_gather | solution.py:80
  77.9 12.1 %compare_reduce_fusion = pred[4,256,1024]{2,1,0:T(8,128)(4,1)} fusion(s32[8,1024]{1,0:T(8,128)S(1)} %bitcast.303, s32[4,256]{1,0:T(4,128)S(1)} %get-tuple-element.82), kind=kLoop, calls=%fused_computation.4 | loop fusion | flops 15728640 | bytes 1085440 | tf_op jit(solution)/shard_map/reduce_or | solution.py:109
  90.1 12.2 %fusion.2 = bf16[4,256,1024]{2,1,0:T(8,128)(2,1)} fusion(f32[8,1024]{1,0:T(8,128)S(1)} %bitcast.309, s32[8,1024]{1,0:T(8,128)S(1)} %bitcast.304, s32[4,256]{1,0:T(4,128)S(1)} %get-tuple-element.82), kind=kLoop, calls=%fused_computation.11 | loop fusion | flops 24117248 | bytes 2166784 | tf_op jit(solution)/shard_map/reduce_sum | solution.py:110
  102.4 11.9 %compare_reduce_fusion.1 = pred[4,256,1024]{2,1,0:T(8,128)(4,1)} fusion(s32[8,1024]{1,0:T(8,128)S(1)} %bitcast.307, s32[4,256]{1,0:T(4,128)S(1)} %get-tuple-element.81), kind=kLoop, calls=%fused_computation.6 | loop fusion | flops 15728640 | bytes 1085440 | tf_op jit(solution)/shard_map/reduce_or | solution.py:109
  114.3 10.8 %fusion.1 = bf16[4,256,1024]{2,1,0:T(8,128)(2,1)S(1)} fusion(f32[8,1024]{1,0:T(8,128)S(1)} %bitcast.310, s32[8,1024]{1,0:T(8,128)S(1)} %bitcast.308, s32[4,256]{1,0:T(4,128)S(1)} %get-tuple-element.81), kind=kLoop, calls=%fused_computation.10 | loop fusion | flops 24117248 | bytes 2166784 | tf_op jit(solution)/shard_map/reduce_sum | solution.py:110
  125.3 12.2 %fusion = bf16[4,256,1024]{2,1,0:T(8,128)(2,1)} fusion(f32[8,1024]{1,0:T(8,128)S(1)} %bitcast.311, s32[8,1024]{1,0:T(8,128)S(1)} %bitcast.305, s32[4,256]{1,0:T(4,128)S(1)} %get-tuple-element.80), kind=kLoop, calls=%fused_computation.9 | loop fusion | flops 24117248 | bytes 2166784 | tf_op jit(solution)/shard_map/reduce_sum | solution.py:110
  137.5 10.9 %compare_reduce_fusion.2 = pred[4,256,1024]{2,1,0:T(8,128)(4,1)S(1)} fusion(s32[8,1024]{1,0:T(8,128)S(1)} %bitcast.306, s32[4,256]{1,0:T(4,128)S(1)} %get-tuple-element.80), kind=kLoop, calls=%fused_computation.7 | loop fusion | flops 15728640 | bytes 1085440 | tf_op jit(solution)/shard_map/reduce_or | solution.py:109
  152.9 3.5 collective-permute-done.17
  159.6 6.9 %collective-permute-done.18 = bf16[256,1152]{1,0:T(8,128)(2,1)S(1)} collective-permute-done((bf16[256,1152]{1,0:T(8,128)(2,1)S(1)}, bf16[256,1152]{1,0:T(8,128)(2,1)S(1)}, u32[]{:S(2)}, u32[]{:S(2)}) %collective-permute-start.18) | collective-permute-done | bytes 589856 | tf_op jit(solution)/shard_map/ppermute | solution.py:33
  172.2 11.9 %collective-permute-done.19 = bf16[512,1152]{1,0:T(8,128)(2,1)S(1)} collective-permute-done((bf16[512,1152]{1,0:T(8,128)(2,1)S(1)}, bf16[512,1152]{1,0:T(8,128)(2,1)S(1)}, u32[]{:S(2)}, u32[]{:S(2)}) %collective-permute-start.19) | collective-permute-done | bytes 1179680 | tf_op jit(solution)/shard_map/ppermute | solution.py:33
  201.2 7.4 %collective-permute-done.22 = bf16[256,1152]{1,0:T(8,128)(2,1)S(1)} collective-permute-done((bf16[256,1152]{1,0:T(8,128)(2,1)S(1)}, bf16[256,1152]{1,0:T(8,128)(2,1)S(1)}, u32[]{:S(2)}, u32[]{:S(2)}) %collective-permute-start.22) | collective-permute-done | bytes 589856 | tf_op jit(solution)/shard_map/ppermute | solution.py:33
  208.7 7.9 %collective-permute-done.21 = bf16[256,1152]{1,0:T(8,128)(2,1)S(1)} collective-permute-done((bf16[256,1152]{1,0:T(8,128)(2,1)S(1)}, bf16[256,1152]{1,0:T(8,128)(2,1)S(1)}, u32[]{:S(2)}, u32[]{:S(2)}) %collective-permute-start.21) | collective-permute-done | bytes 589856 | tf_op jit(solution)/shard_map/ppermute | solution.py:33
  216.5 2.7 collective-permute-start.6
  223.2 12.6 %collective-permute-done.6 = bf16[256,1280]{1,0:T(8,128)(2,1)S(1)} collective-permute-done((bf16[256,1280]{1,0:T(8,128)(2,1)S(1)}, bf16[256,1280]{1,0:T(8,128)(2,1)S(1)}, u32[]{:S(2)}, u32[]{:S(2)}) %collective-permute-start.6) | collective-permute-done | bytes 655392 | tf_op jit(solution)/shard_map/ppermute | solution.py:33
  235.8 10.3 %collective-permute-done.5 = bf16[256,1280]{1,0:T(8,128)(2,1)S(1)} collective-permute-done((bf16[256,1280]{1,0:T(8,128)(2,1)S(1)}, bf16[256,1280]{1,0:T(8,128)(2,1)S(1)}, u32[]{:S(2)}, u32[]{:S(2)}) %collective-permute-start.5) | collective-permute-done | bytes 655392 | tf_op jit(solution)/shard_map/ppermute | solution.py:33
  250.8 13.6 %fusion.3 = f32[1024,1024]{1,0:T(8,128)} fusion(bf16[1,3584,1024]{2,1,0:T(8,128)(2,1)} %param.14, bf16[512,1152]{1,0:T(8,128)(2,1)} %bitcast.298, bf16[512,1152]{1,0:T(8,128)(2,1)S(1)} %bitcast.293, bf16[512,1152]{1,0:T(8,128)(2,1)S(1)} %bitcast.302, bf16[512,1152]{1,0:T(8,128)(2,1)} %bitcast.295, bf16[512,1280]{1,0:T(8,128)(2,1)S(1)} %bitcast.267, ...), kind=kOutput, calls=%fused_computation.13 | convolution fusion | flops 7560232960 | bytes 18874368 | tf_op jit(solution)/shard_map/dot_general | solution.py:142
  264.4 26.4 %multiply_convert_fusion = bf16[1024,1024]{1,0:T(8,128)(2,1)} fusion(f32[1024,1024]{1,0:T(8,128)} %fusion.3, bf16[1,3584,1024]{2,1,0:T(8,128)(2,1)} %param.13, bf16[512,1152]{1,0:T(8,128)(2,1)} %bitcast.299, bf16[512,1152]{1,0:T(8,128)(2,1)} %bitcast.294, bf16[512,1152]{1,0:T(8,128)(2,1)} %bitcast.301, bf16[512,1152]{1,0:T(8,128)(2,1)} %bitcast.296, ...), kind=kOutput, calls=%fused_computation.24 | convolution fusion | flops 7566524416 | bytes 20971520 | tf_op jit(solution)/shard_map/dot_general | solution.py:141
  290.8 5.3 %convolution_convert_fusion = bf16[1024,1152]{1,0:T(8,128)(2,1)S(1)} fusion(bf16[1024,1024]{1,0:T(8,128)(2,1)} %multiply_convert_fusion, bf16[1024,3584]{1,0:T(8,128)(2,1)} %bitcast.312), kind=kOutput, calls=%fused_computation.27 | convolution fusion | flops 2417098752 | bytes 6815744 | tf_op jit(solution)/shard_map/dot_general | solution.py:149
  296.2 4.8 %convolution_convert_fusion.1 = bf16[1024,1152]{1,0:T(8,128)(2,1)S(1)} fusion(bf16[1024,1024]{1,0:T(8,128)(2,1)S(1)} %copy-done.10, bf16[1024,3584]{1,0:T(8,128)(2,1)} %bitcast.313), kind=kOutput, calls=%fused_computation.28 | convolution fusion | flops 2417098752 | bytes 6815744 | tf_op jit(solution)/shard_map/dot_general | solution.py:149
  300.9 4.8 %convolution_convert_fusion.2 = bf16[1024,1280]{1,0:T(8,128)(2,1)S(1)} fusion(bf16[1024,1024]{1,0:T(8,128)(2,1)S(1)} %copy-done.10, bf16[1024,3584]{1,0:T(8,128)(2,1)} %bitcast.314), kind=kOutput, calls=%fused_computation.29 | convolution fusion | flops 2685665280 | bytes 7340032 | tf_op jit(solution)/shard_map/dot_general | solution.py:149
  314.1 2.8 collective-permute-start.35
  319.9 18.4 %collective-permute-done.41 = bf16[256,1152]{1,0:T(8,128)(2,1)S(1)} collective-permute-done((bf16[256,1152]{1,0:T(8,128)(2,1)S(1)}, bf16[256,1152]{1,0:T(8,128)(2,1)S(1)}, u32[]{:S(2)}, u32[]{:S(2)}) %collective-permute-start.41) | collective-permute-done | bytes 589856 | tf_op jit(solution)/shard_map/ppermute | solution.py:33
  341.3 2.9 collective-permute-start.26
  350.4 2.6 collective-permute-start.44
  358.2 3.5 collective-permute-done.26
  363.7 13.4 %collective-permute-done.27 = bf16[256,1280]{1,0:T(8,128)(2,1)} collective-permute-done((bf16[256,1280]{1,0:T(8,128)(2,1)}, bf16[256,1280]{1,0:T(8,128)(2,1)}, u32[]{:S(2)}, u32[]{:S(2)}) %collective-permute-start.27) | collective-permute-done | bytes 655392 | tf_op jit(solution)/shard_map/ppermute | solution.py:33
  381.5 5.6 %collective-permute-done.44 = bf16[512,1152]{1,0:T(8,128)(2,1)S(1)} collective-permute-done((bf16[512,1152]{1,0:T(8,128)(2,1)S(1)}, bf16[512,1152]{1,0:T(8,128)(2,1)S(1)}, u32[]{:S(2)}, u32[]{:S(2)}) %collective-permute-start.44) | collective-permute-done | bytes 1179680 | tf_op jit(solution)/shard_map/ppermute | solution.py:33
  390.0 8.2 %collective-permute-done.28 = bf16[512,1280]{1,0:T(8,128)(2,1)S(1)} collective-permute-done((bf16[512,1280]{1,0:T(8,128)(2,1)S(1)}, bf16[512,1280]{1,0:T(8,128)(2,1)S(1)}, u32[]{:S(2)}, u32[]{:S(2)}) %collective-permute-start.28) | collective-permute-done | bytes 1310752 | tf_op jit(solution)/shard_map/ppermute | solution.py:33
  404.0 6.2 %collective-permute-done.46 = bf16[128,1152]{1,0:T(8,128)(2,1)S(1)} collective-permute-done((bf16[128,1152]{1,0:T(8,128)(2,1)S(1)}, bf16[128,1152]{1,0:T(8,128)(2,1)S(1)}, u32[]{:S(2)}, u32[]{:S(2)}) %collective-permute-start.46) | collective-permute-done | bytes 294944 | tf_op jit(solution)/shard_map/ppermute | solution.py:33
  415.6 4.2 collective-permute-done.30
  419.9 3.8 collective-permute-start.31
  423.7 3.3 collective-permute-done.31
  (282 shorter events, 102.4 us)
Async XLA Ops:
  1.7 146.7 %collective-permute-start.16 = (bf16[64,1152]{1,0:T(8,128)(2,1)S(1)}, bf16[64,1152]{1,0:T(8,128)(2,1)S(1)}, u32[]{:S(2)}, u32[]{:S(2)}) collective-permute-start(bf16[64,1152]{1,0:T(8,128)(2,1)S(1)} %get-tuple-element.79), channel_id=1, source_target_pairs={{0,4},{1,5},{2,6},{3,7},{4,0},{5,1},{6,2},{7,3},{8,12},{9,13},{10,... | collective-permute-start | bytes 442376 | tf_op jit(solution)/shard_map/ppermute | solution.py:33
  3.3 146.6 %collective-permute-start.8 = (bf16[64,1152]{1,0:T(8,128)(2,1)S(1)}, bf16[64,1152]{1,0:T(8,128)(2,1)S(1)}, u32[]{:S(2)}, u32[]{:S(2)}) collective-permute-start(bf16[64,1152]{1,0:T(8,128)(2,1)S(1)} %get-tuple-element.76), channel_id=1, source_target_pairs={{0,32},{1,33},{2,34},{3,35},{4,36},{5,37},{6,38},{7,39},{8,40},{9,... | collective-permute-start | bytes 442376 | tf_op jit(solution)/shard_map/ppermute | solution.py:33
  6.5 144.3 %collective-permute-start = (bf16[64,1280]{1,0:T(8,128)(2,1)S(1)}, bf16[64,1280]{1,0:T(8,128)(2,1)S(1)}, u32[]{:S(2)}, u32[]{:S(2)}) collective-permute-start(bf16[64,1280]{1,0:T(8,128)(2,1)S(1)} %get-tuple-element.74), channel_id=1, source_target_pairs={{0,1},{1,0},{2,3},{3,2},{4,5},{5,4},{6,7},{7,6},{8,9},{9,8},{10,11... | collective-permute-start | bytes 491528 | tf_op jit(solution)/shard_map/ppermute | solution.py:33
  166.6 17.5 %collective-permute-start.19 = (bf16[512,1152]{1,0:T(8,128)(2,1)S(1)}, bf16[512,1152]{1,0:T(8,128)(2,1)S(1)}, u32[]{:S(2)}, u32[]{:S(2)}) collective-permute-start(bf16[512,1152]{1,0:T(8,128)(2,1)S(1)} %pad_maximum_fusion.8), channel_id=1, source_target_pairs={{0,96},{1,97},{2,98},{3,99},{4,100},{5,101},{6,102},{7,103},{8,104... | collective-permute-start | bytes 3538952 | tf_op jit(solution)/shard_map/ppermute | solution.py:33
  168.1 19.7 %collective-permute-start.11 = (bf16[512,1152]{1,0:T(8,128)(2,1)S(1)}, bf16[512,1152]{1,0:T(8,128)(2,1)S(1)}, u32[]{:S(2)}, u32[]{:S(2)}) collective-permute-start(bf16[512,1152]{1,0:T(8,128)(2,1)S(1)} %pad_maximum_fusion.4), channel_id=1, source_target_pairs={{0,3},{1,2},{2,1},{3,0},{4,7},{5,6},{6,5},{7,4},{8,11},{9,10},{10,... | collective-permute-start | bytes 3538952 | tf_op jit(solution)/shard_map/ppermute | solution.py:33
  170.3 25.3 %collective-permute-start.3 = (bf16[512,1280]{1,0:T(8,128)(2,1)S(1)}, bf16[512,1280]{1,0:T(8,128)(2,1)S(1)}, u32[]{:S(2)}, u32[]{:S(2)}) collective-permute-start(bf16[512,1280]{1,0:T(8,128)(2,1)S(1)} %pad_maximum_fusion), channel_id=1, source_target_pairs={{0,12},{1,13},{2,14},{3,15},{4,8},{5,9},{6,10},{7,11},{8,4},{9,5},... | collective-permute-start | bytes 3932168 | tf_op jit(solution)/shard_map/ppermute | solution.py:33
  190.8 17.8 %collective-permute-start.22 = (bf16[256,1152]{1,0:T(8,128)(2,1)S(1)}, bf16[256,1152]{1,0:T(8,128)(2,1)S(1)}, u32[]{:S(2)}, u32[]{:S(2)}) collective-permute-start(bf16[256,1152]{1,0:T(8,128)(2,1)S(1)} %convolution_convert_fusion.3), channel_id=1, source_target_pairs={{0,2},{1,3},{2,0},{3,1},{4,6},{5,7},{6,4},{7,5},{8,10},{9,11},{10,... | collective-permute-start | bytes 1769480 | tf_op jit(solution)/shard_map/ppermute | solution.py:33
  192.7 23.8 %collective-permute-start.21 = (bf16[256,1152]{1,0:T(8,128)(2,1)S(1)}, bf16[256,1152]{1,0:T(8,128)(2,1)S(1)}, u32[]{:S(2)}, u32[]{:S(2)}) collective-permute-start(bf16[256,1152]{1,0:T(8,128)(2,1)S(1)} %convolution_convert_fusion.4), channel_id=1, source_target_pairs={{0,3},{1,2},{2,1},{3,0},{4,7},{5,6},{6,5},{7,4},{8,11},{9,10},{10,... | collective-permute-start | bytes 1769480 | tf_op jit(solution)/shard_map/ppermute | solution.py:33
  193.7 25.6 %collective-permute-start.20 = (bf16[256,1152]{1,0:T(8,128)(2,1)S(1)}, bf16[256,1152]{1,0:T(8,128)(2,1)S(1)}, u32[]{:S(2)}, u32[]{:S(2)}) collective-permute-start(bf16[256,1152]{1,0:T(8,128)(2,1)S(1)} %convolution_convert_fusion.5), channel_id=1, source_target_pairs={{0,1},{1,0},{2,3},{3,2},{4,5},{5,4},{6,7},{7,6},{8,9},{9,8},{10,11... | collective-permute-start | bytes 1769480 | tf_op jit(solution)/shard_map/ppermute | solution.py:33
  194.3 25.3 %collective-permute-start.14 = (bf16[256,1152]{1,0:T(8,128)(2,1)S(1)}, bf16[256,1152]{1,0:T(8,128)(2,1)S(1)}, u32[]{:S(2)}, u32[]{:S(2)}) collective-permute-start(bf16[256,1152]{1,0:T(8,128)(2,1)S(1)} %convolution_convert_fusion.7), channel_id=1, source_target_pairs={{0,8},{1,9},{2,10},{3,11},{4,12},{5,13},{6,14},{7,15},{8,0},{9,1},... | collective-permute-start | bytes 1769480 | tf_op jit(solution)/shard_map/ppermute | solution.py:33
  195.6 25.2 %collective-permute-start.13 = (bf16[256,1152]{1,0:T(8,128)(2,1)S(1)}, bf16[256,1152]{1,0:T(8,128)(2,1)S(1)}, u32[]{:S(2)}, u32[]{:S(2)}) collective-permute-start(bf16[256,1152]{1,0:T(8,128)(2,1)S(1)} %convolution_convert_fusion.8), channel_id=1, source_target_pairs={{0,12},{1,13},{2,14},{3,15},{4,8},{5,9},{6,10},{7,11},{8,4},{9,5},... | collective-permute-start | bytes 1769480 | tf_op jit(solution)/shard_map/ppermute | solution.py:33
  208.6 12.3 %collective-permute-start.12 = (bf16[256,1152]{1,0:T(8,128)(2,1)S(1)}, bf16[256,1152]{1,0:T(8,128)(2,1)S(1)}, u32[]{:S(2)}, u32[]{:S(2)}) collective-permute-start(bf16[256,1152]{1,0:T(8,128)(2,1)S(1)} %convolution_convert_fusion.9), channel_id=1, source_target_pairs={{0,4},{1,5},{2,6},{3,7},{4,0},{5,1},{6,2},{7,3},{8,12},{9,13},{10,... | collective-permute-start | bytes 1769480 | tf_op jit(solution)/shard_map/ppermute | solution.py:33
  216.5 19.2 %collective-permute-start.6 = (bf16[256,1280]{1,0:T(8,128)(2,1)S(1)}, bf16[256,1280]{1,0:T(8,128)(2,1)S(1)}, u32[]{:S(2)}, u32[]{:S(2)}) collective-permute-start(bf16[256,1280]{1,0:T(8,128)(2,1)S(1)} %convolution_convert_fusion.11), channel_id=1, source_target_pairs={{0,64},{1,65},{2,66},{3,67},{4,68},{5,69},{6,70},{7,71},{8,72},{9,... | collective-permute-start | bytes 1966088 | tf_op jit(solution)/shard_map/ppermute | solution.py:33
  219.3 26.8 %collective-permute-start.5 = (bf16[256,1280]{1,0:T(8,128)(2,1)S(1)}, bf16[256,1280]{1,0:T(8,128)(2,1)S(1)}, u32[]{:S(2)}, u32[]{:S(2)}) collective-permute-start(bf16[256,1280]{1,0:T(8,128)(2,1)S(1)} %convolution_convert_fusion.12), channel_id=1, source_target_pairs={{0,96},{1,97},{2,98},{3,99},{4,100},{5,101},{6,102},{7,103},{8,104... | collective-permute-start | bytes 1966088 | tf_op jit(solution)/shard_map/ppermute | solution.py:33
  219.7 26.5 %collective-permute-start.4 = (bf16[256,1280]{1,0:T(8,128)(2,1)S(1)}, bf16[256,1280]{1,0:T(8,128)(2,1)S(1)}, u32[]{:S(2)}, u32[]{:S(2)}) collective-permute-start(bf16[256,1280]{1,0:T(8,128)(2,1)S(1)} %convolution_convert_fusion.13), channel_id=1, source_target_pairs={{0,32},{1,33},{2,34},{3,35},{4,36},{5,37},{6,38},{7,39},{8,40},{9,... | collective-permute-start | bytes 1966088 | tf_op jit(solution)/shard_map/ppermute | solution.py:33
  220.8 25.8 %collective-permute-start.23 = (bf16[512,1152]{1,0:T(8,128)(2,1)S(1)}, bf16[512,1152]{1,0:T(8,128)(2,1)S(1)}, u32[]{:S(2)}, u32[]{:S(2)}) collective-permute-start(bf16[512,1152]{1,0:T(8,128)(2,1)S(1)} %pad_maximum_fusion.10), channel_id=1, source_target_pairs={{0,16},{1,17},{2,18},{3,19},{4,20},{5,21},{6,22},{7,23},{8,24},{9,... | collective-permute-start | bytes 3538952 | tf_op jit(solution)/shard_map/ppermute | solution.py:38
  221.1 26.8 %collective-permute-start.15 = (bf16[512,1152]{1,0:T(8,128)(2,1)S(1)}, bf16[512,1152]{1,0:T(8,128)(2,1)S(1)}, u32[]{:S(2)}, u32[]{:S(2)}) collective-permute-start(bf16[512,1152]{1,0:T(8,128)(2,1)S(1)} %pad_maximum_fusion.6), channel_id=1, source_target_pairs={{0,16},{1,17},{2,18},{3,19},{4,20},{5,21},{6,22},{7,23},{8,24},{9,... | collective-permute-start | bytes 3538952 | tf_op jit(solution)/shard_map/ppermute | solution.py:38
  309.2 32.1 %collective-permute-start.43 = (bf16[256,1152]{1,0:T(8,128)(2,1)S(1)}, bf16[256,1152]{1,0:T(8,128)(2,1)S(1)}, u32[]{:S(2)}, u32[]{:S(2)}) collective-permute-start(bf16[256,1152]{1,0:T(8,128)(2,1)S(1)} %pad_maximum_fusion.23), channel_id=1, source_target_pairs={{0,2},{1,3},{2,0},{3,1},{4,6},{5,7},{6,4},{7,5},{8,10},{9,11},{10,... | collective-permute-start | bytes 1769480 | tf_op jit(solution)/shard_map/ppermute | solution.py:33
  310.3 28.1 %collective-permute-start.41 = (bf16[256,1152]{1,0:T(8,128)(2,1)S(1)}, bf16[256,1152]{1,0:T(8,128)(2,1)S(1)}, u32[]{:S(2)}, u32[]{:S(2)}) collective-permute-start(bf16[256,1152]{1,0:T(8,128)(2,1)S(1)} %pad_maximum_fusion.21), channel_id=1, source_target_pairs={{0,1},{1,0},{2,3},{3,2},{4,5},{5,4},{6,7},{7,6},{8,9},{9,8},{10,11... | collective-permute-start | bytes 1769480 | tf_op jit(solution)/shard_map/ppermute | solution.py:33
  312.3 32.8 %collective-permute-start.42 = (bf16[256,1152]{1,0:T(8,128)(2,1)S(1)}, bf16[256,1152]{1,0:T(8,128)(2,1)S(1)}, u32[]{:S(2)}, u32[]{:S(2)}) collective-permute-start(bf16[256,1152]{1,0:T(8,128)(2,1)S(1)} %pad_maximum_fusion.22), channel_id=1, source_target_pairs={{0,3},{1,2},{2,1},{3,0},{4,7},{5,6},{6,5},{7,4},{8,11},{9,10},{10,... | collective-permute-start | bytes 1769480 | tf_op jit(solution)/shard_map/ppermute | solution.py:33
  314.1 36.3 %collective-permute-start.35 = (bf16[256,1152]{1,0:T(8,128)(2,1)S(1)}, bf16[256,1152]{1,0:T(8,128)(2,1)S(1)}, u32[]{:S(2)}, u32[]{:S(2)}) collective-permute-start(bf16[256,1152]{1,0:T(8,128)(2,1)S(1)} %pad_maximum_fusion.20), channel_id=1, source_target_pairs={{0,8},{1,9},{2,10},{3,11},{4,12},{5,13},{6,14},{7,15},{8,0},{9,1},... | collective-permute-start | bytes 1769480 | tf_op jit(solution)/shard_map/ppermute | solution.py:33
  317.0 29.9 %collective-permute-start.33 = (bf16[256,1152]{1,0:T(8,128)(2,1)S(1)}, bf16[256,1152]{1,0:T(8,128)(2,1)S(1)}, u32[]{:S(2)}, u32[]{:S(2)}) collective-permute-start(bf16[256,1152]{1,0:T(8,128)(2,1)S(1)} %pad_maximum_fusion.18), channel_id=1, source_target_pairs={{0,4},{1,5},{2,6},{3,7},{4,0},{5,1},{6,2},{7,3},{8,12},{9,13},{10,... | collective-permute-start | bytes 1769480 | tf_op jit(solution)/shard_map/ppermute | solution.py:33
  338.3 15.6 %collective-permute-start.34 = (bf16[256,1152]{1,0:T(8,128)(2,1)S(1)}, bf16[256,1152]{1,0:T(8,128)(2,1)S(1)}, u32[]{:S(2)}, u32[]{:S(2)}) collective-permute-start(bf16[256,1152]{1,0:T(8,128)(2,1)S(1)} %pad_maximum_fusion.19), channel_id=1, source_target_pairs={{0,12},{1,13},{2,14},{3,15},{4,8},{5,9},{6,10},{7,11},{8,4},{9,5},... | collective-permute-start | bytes 1769480 | tf_op jit(solution)/shard_map/ppermute | solution.py:33
  341.3 20.4 %collective-permute-start.26 = (bf16[256,1280]{1,0:T(8,128)(2,1)S(1)}, bf16[256,1280]{1,0:T(8,128)(2,1)S(1)}, u32[]{:S(2)}, u32[]{:S(2)}) collective-permute-start(bf16[256,1280]{1,0:T(8,128)(2,1)S(1)} %pad_maximum_fusion.14), channel_id=1, source_target_pairs={{0,96},{1,97},{2,98},{3,99},{4,100},{5,101},{6,102},{7,103},{8,104... | collective-permute-start | bytes 1966088 | tf_op jit(solution)/shard_map/ppermute | solution.py:33
  345.1 17.8 %collective-permute-start.25 = (bf16[256,1280]{1,0:T(8,128)(2,1)S(1)}, bf16[256,1280]{1,0:T(8,128)(2,1)S(1)}, u32[]{:S(2)}, u32[]{:S(2)}) collective-permute-start(bf16[256,1280]{1,0:T(8,128)(2,1)S(1)} %pad_maximum_fusion.13), channel_id=1, source_target_pairs={{0,32},{1,33},{2,34},{3,35},{4,36},{5,37},{6,38},{7,39},{8,40},{9,... | collective-permute-start | bytes 1966088 | tf_op jit(solution)/shard_map/ppermute | solution.py:33
  346.9 30.3 %collective-permute-start.27 = (bf16[256,1280]{1,0:T(8,128)(2,1)}, bf16[256,1280]{1,0:T(8,128)(2,1)}, u32[]{:S(2)}, u32[]{:S(2)}) collective-permute-start(bf16[256,1280]{1,0:T(8,128)(2,1)} %pad_maximum_fusion.15), channel_id=1, source_target_pairs={{0,64},{1,65},{2,66},{3,67},{4,68},{5,69},{6,70},{7,71},{8,72},{9,... | collective-permute-start | bytes 1966088 | tf_op jit(solution)/shard_map/ppermute | solution.py:33
  350.4 36.8 %collective-permute-start.44 = (bf16[512,1152]{1,0:T(8,128)(2,1)S(1)}, bf16[512,1152]{1,0:T(8,128)(2,1)S(1)}, u32[]{:S(2)}, u32[]{:S(2)}) collective-permute-start(bf16[512,1152]{1,0:T(8,128)(2,1)S(1)} %slice.592), channel_id=1, source_target_pairs={{0,96},{1,97},{2,98},{3,99},{4,100},{5,101},{6,102},{7,103},{8,104... | collective-permute-start | bytes 3538952 | tf_op jit(solution)/shard_map/ppermute | solution.py:33
  356.2 31.9 %collective-permute-start.36 = (bf16[512,1152]{1,0:T(8,128)(2,1)}, bf16[512,1152]{1,0:T(8,128)(2,1)S(1)}, u32[]{:S(2)}, u32[]{:S(2)}) collective-permute-start(bf16[512,1152]{1,0:T(8,128)(2,1)} %slice.569), channel_id=1, source_target_pairs={{0,3},{1,2},{2,1},{3,0},{4,7},{5,6},{6,5},{7,4},{8,11},{9,10},{10,... | collective-permute-start | bytes 3538952 | tf_op jit(solution)/shard_map/ppermute | solution.py:33
  379.4 18.9 %collective-permute-start.28 = (bf16[512,1280]{1,0:T(8,128)(2,1)S(1)}, bf16[512,1280]{1,0:T(8,128)(2,1)S(1)}, u32[]{:S(2)}, u32[]{:S(2)}) collective-permute-start(bf16[512,1280]{1,0:T(8,128)(2,1)S(1)} %slice.546), channel_id=1, source_target_pairs={{0,12},{1,13},{2,14},{3,15},{4,8},{5,9},{6,10},{7,11},{8,4},{9,5},... | collective-permute-start | bytes 3932168 | tf_op jit(solution)/shard_map/ppermute | solution.py:33
  388.4 12.8 %collective-permute-start.37 = (bf16[256,1152]{1,0:T(8,128)(2,1)S(1)}, bf16[256,1152]{1,0:T(8,128)(2,1)S(1)}, u32[]{:S(2)}, u32[]{:S(2)}) collective-permute-start(bf16[256,1152]{1,0:T(8,128)(2,1)S(1)} %slice.571), channel_id=1, source_target_pairs={{0,1},{1,0},{2,3},{3,2},{4,5},{5,4},{6,7},{7,6},{8,9},{9,8},{10,11... | collective-permute-start | bytes 1769480 | tf_op jit(solution)/shard_map/ppermute | solution.py:33
  398.7 12.6 %collective-permute-start.29 = (bf16[256,1280]{1,0:T(8,128)(2,1)S(1)}, bf16[256,1280]{1,0:T(8,128)(2,1)S(1)}, u32[]{:S(2)}, u32[]{:S(2)}) collective-permute-start(bf16[256,1280]{1,0:T(8,128)(2,1)S(1)} %slice.548), channel_id=1, source_target_pairs={{0,4},{1,5},{2,6},{3,7},{4,0},{5,1},{6,2},{7,3},{8,12},{9,13},{10,... | collective-permute-start | bytes 1966088 | tf_op jit(solution)/shard_map/ppermute | solution.py:33
  411.2 12.5 %collective-permute-start.39 = (bf16[64,1152]{1,0:T(8,128)(2,1)S(1)}, bf16[64,1152]{1,0:T(8,128)(2,1)S(1)}, u32[]{:S(2)}, u32[]{:S(2)}) collective-permute-start(bf16[64,1152]{1,0:T(8,128)(2,1)S(1)} %slice.575), channel_id=1, source_target_pairs={{0,32},{1,33},{2,34},{3,35},{4,36},{5,37},{6,38},{7,39},{8,40},{9,... | collective-permute-start | bytes 442376 | tf_op jit(solution)/shard_map/ppermute | solution.py:33
  (28 other events, 313.1 us)

commit v2 on v0

v2 whole, which is shorter than its diff:
```python
import jax
import jax.numpy as jnp
from jax import lax
from jax.sharding import PartitionSpec as P

BOTH = ("node", "local")
RING = 4
CORES = 2
LANES = 128

GATHER = (1, 3)
EXCHANGE = (3, 1)

NEAR = ((0, 0, 0), (1, 0, 0), (0, 1, 0), (0, 0, 1))
FAR = ((1, 1, 0), (0, 1, 1), (1, 0, 1), (1, 1, 1))
CORNERS = tuple((i >> 2 & 1, i >> 1 & 1, i & 1) for i in range(8))


def index_of(y, c, x, z):
    return ((y * CORES + c) * RING + x) * RING + z


def places():
    return [
        (y, c, x, z) for y in range(RING) for c in range(CORES) for x in range(RING) for z in range(RING)
    ]


def moved(place, corner, step):
    y, c, x, z = place
    return index_of(y ^ corner[0] * step, c, x ^ corner[1] * step, z ^ corner[2] * step)


def to_corner(value, corner):
    return lax.ppermute(value, BOTH, [(index_of(*p), moved(p, corner, GATHER[p[1]])) for p in places()])


def to_other_core(value):
    return lax.ppermute(
        value, BOTH, [(index_of(y, c, x, z), index_of(y, 1 - c, x, z)) for y, c, x, z in places()]
    )


def first_of(v, core):
    return (v if v < 2 else v ^ 3) if core == 0 else v & 2


def exchange(value):
    groups = [
        [moved((y, c, x, z), corner, EXCHANGE[c]) for corner in CORNERS]
        for y, c, x, z in places()
        if all(first_of(v, c) == v for v in (y, x, z))
    ]
    return lax.all_to_all(
        value, BOTH, split_axis=0, concat_axis=0, axis_index_groups=groups, tiled=True
    )


def gather_cube(block):
    y, x, z = [to_corner(block, corner) for corner in NEAR[1:]]
    far = [to_corner(x, NEAR[1]), to_corner(z, NEAR[2]), to_corner(y, NEAR[3]), to_corner(block, FAR[3])]
    return [block, y, x, z] + far


def add(a, *others):
    total = a.astype(jnp.float32)
    for b in others:
        total = total + b.astype(jnp.float32)
    return total.astype(jnp.bfloat16)


def reduce_cube(blocks):
    own, y, x, z, yx, xz, yz, yxz = blocks
    x = add(x, to_corner(yx, NEAR[1]))
    z = add(z, to_corner(xz, NEAR[2]))
    y = add(y, to_corner(yz, NEAR[3]))
    last = to_corner(yxz, FAR[3])
    return add(own, last, *[to_corner(b, corner) for b, corner in zip((y, x, z), NEAR[1:])])


def shards(tokens, expert_ids, gate_values, expert_gate, expert_up, expert_down):
    node = lax.axis_index("node")
    local = lax.axis_index("local")
    at = (node // CORES, local // RING, local % RING)
    core = node % CORES
    experts = lax.axis_size("node") * lax.axis_size("local")
    tok, width = tokens.shape
    top = expert_ids.shape[1]
    cap = 2 * tok * top // experts
    corners = len(CORNERS)
    held = corners * tok

    hits = (expert_ids[:, :, None] == jnp.arange(experts, dtype=jnp.int32)).astype(jnp.int32)
    named = jnp.sum(hits, axis=1)
    earlier = jnp.cumsum(named, axis=0) - named
    slot = jnp.sum(hits * earlier[:, None, :], axis=2)
    about = jnp.concatenate(
        [expert_ids.astype(jnp.bfloat16), slot.astype(jnp.bfloat16), gate_values], axis=1
    )
    about = jnp.pad(about, ((0, 0), (0, LANES - 3 * top)))

    blocks = gather_cube(jnp.concatenate([tokens, about], axis=1))
    rows = jnp.concatenate([b[:, :width] for b in blocks], axis=0)
    known = jnp.concatenate([b[:, width:] for b in blocks], axis=0)

    step = jnp.where(core == 0, EXCHANGE[0], EXCHANGE[1])
    base = [jnp.where(core == 0, jnp.where(v < 2, v, v ^ 3), v & 2) for v in at]
    bits = jnp.array(CORNERS, dtype=jnp.int32)
    spot = [base[i] ^ (bits[:, i] * step) for i in range(3)]
    wanted = index_of(spot[0], core, spot[1], spot[2])
    wanted = jnp.stack([wanted, wanted ^ (RING * RING)], axis=1)[:, :, None] * cap + jnp.arange(cap, dtype=jnp.int32)
    wanted = wanted.reshape(-1, 1).astype(jnp.float32)

    known = known.astype(jnp.float32).T[: 3 * top].reshape(3, top, held)
    place = known[0] * cap + known[1]
    chosen = jnp.zeros((wanted.shape[0], held), jnp.float32)
    weights = chosen
    for k in range(top):
        same = wanted == place[k][None, :]
        chosen = jnp.where(same, jnp.float32(1.0), chosen)
        weights = jnp.where(same, known[2, k][None, :], weights)

    source = jnp.repeat(jnp.arange(corners, dtype=jnp.int32), tok)
    mask = jnp.arange(corners, dtype=jnp.int32)[:, None, None] == source[None, None, :]

    def spread(small):
        small = small.reshape(corners * CORES, 1, cap, held)
        wide = jnp.where(mask[None], small, jnp.float32(0.0)).astype(jnp.bfloat16)
        return wide.reshape(corners * CORES * corners * cap, held)

    half = corners * cap
    send = jnp.dot(spread(chosen), rows, preferred_element_type=jnp.float32).astype(jnp.bfloat16)
    got = exchange(send.reshape(corners, CORES * half, width))
    theirs = to_other_core(got[:, half:].reshape(corners * half, width))
    mine = got[:, :half].reshape(corners * half, width)

    def inner(rows):
        gate_rows = jnp.dot(rows, expert_gate[0], preferred_element_type=jnp.float32)
        up_rows = jnp.dot(rows, expert_up[0], preferred_element_type=jnp.float32)
        return (jax.nn.silu(gate_rows) * up_rows).astype(jnp.bfloat16)

    def outer(hidden):
        out = jnp.dot(hidden, expert_down[0], preferred_element_type=jnp.float32).astype(jnp.bfloat16)
        return out.reshape(corners, half, width)

    hidden = inner(mine)
    theirs = to_other_core(outer(inner(theirs)))
    back = exchange(jnp.concatenate([outer(hidden), theirs], axis=1))
    total = lax.dot_general(
        spread(weights),
        back.reshape(corners * CORES * half, width),
        (((0,), (0,)), ((), ())),
        preferred_element_type=jnp.float32,
    ).astype(jnp.bfloat16)
    return reduce_cube([total[i * tok : (i + 1) * tok] for i in range(corners)])


def solution(mesh):
    placed = (
        P(("node", "local"), None),
        P(("node", "local"), None),
        P(("node", "local"), None),
        P(("node", "local"), None, None),
        P(("node", "local"), None, None),
        P(("node", "local"), None, None),
    )
    return jax.shard_map(
        shards, mesh=mesh, in_specs=placed, out_specs=P(("node", "local"), None), check_vma=False
    )
```

time: 232 us -> 251 us (1.082)
  waiting for transfers between devices: 86.4 us -> 35.5 us
  matrix products: 36.3 us -> 60.9 us
  local copies, waits for them, and re-layouts: 1.51 us -> 14.1 us
  blocking collectives: 96.6 us -> 109 us
  starting transfers between devices: 5.97 us -> 17.3 us
  other arithmetic: 2.62 us -> 13.3 us
    all_to_all x1 -> x0, waiting for transfers between devices: 86.4 us -> none  [shards(): lax.all_to_all(expert_rows(lax.all_to_all(send.reshape(experts, cap, widt...]
    ppermute x0 -> x16, waiting for transfers between devices: none -> 35.5 us  [the longest x14 29.1 us: to_corner(): lax.ppermute(value, BOTH, [(index_of(*p), moved(p, corner, GATHER[p[1]]))...]
    dot_general x5 -> x6, matrix products: 36.3 us -> 60.9 us  [the longest x2 33.3 us: outer(): jnp.dot(hidden, expert_down[0], preferred_element_type=jnp.float32)]
    ppermute x0 -> x16, starting transfers between devices: none -> 17.3 us  [the longest x14 17.2 us: to_corner(): lax.ppermute(value, BOTH, [(index_of(*p), moved(p, corner, GATHER[p[1]]))...]
    all_to_all x1 -> x2, blocking collectives: 96.6 us -> 109 us  [exchange(): lax.all_to_all(value, BOTH, split_axis=0, concat_axis=0, axis_index_group...]
    unnamed x14 -> x17, local copies, waits for them, and re-layouts: 0.86 us -> 10.1 us
    concatenate x0 -> x3, other arithmetic: none -> 8.33 us  [the longest x1 6.57 us: shards(): back = exchange(jnp.concatenate([outer(hidden), theirs], axis=1))]
    all_to_all x1 -> x0, starting transfers between devices: 5.97 us -> none  [shards(): lax.all_to_all(expert_rows(lax.all_to_all(send.reshape(experts, cap, widt...]
  transfers between devices with their start and end apart: 1 -> 16, of which waited for: 1 -> 12; matrix products, arithmetic and copies ran while one was open for 0% -> 13% of each run, Pallas kernels for 0% -> 0%
where the time goes in v2:
time: 251 us; the launch traced here: 250 us
  blocking collectives  109 us (43%)
  matrix products  60.9 us (24%)
  waiting for transfers between devices  35.5 us (14%)
  starting transfers between devices  17.3 us (7%)
  local copies, waits for them, and re-layouts  14.1 us (6%)
  other arithmetic  13.3 us (5%)
    all_to_all x2, blocking collectives, exchange(): lax.all_to_all(value, BOTH, split_axis=0, concat_axis=0, axis_index_group...  109 us
    dot_general x2, matrix products, outer(): jnp.dot(hidden, expert_down[0], preferred_element_type=jnp.float32)  33.3 us
    ppermute x14, waiting for transfers between devices, to_corner(): lax.ppermute(value, BOTH, [(index_of(*p), moved(p, corner, GATHER[p[1]]))...  29.1 us
    ppermute x14, starting transfers between devices, to_corner(): lax.ppermute(value, BOTH, [(index_of(*p), moved(p, corner, GATHER[p[1]]))...  17.2 us
    dot_general x2, matrix products, inner(): up_rows = jnp.dot(rows, expert_up[0], preferred_element_type=jnp.float32)  17.1 us
    unnamed x17, local copies, waits for them, and re-layouts  10.1 us
    concatenate x1, other arithmetic, shards(): back = exchange(jnp.concatenate([outer(hidden), theirs], axis=1))  6.57 us
    ppermute x2, waiting for transfers between devices, to_other_core(): lax.ppermute(value, BOTH, [(index_of(y, c, x, z), index_of(y, 1 - c, x, z...  6.41 us
  transfers between devices with their start and end apart: 16, of which 12 were waited for; matrix products, arithmetic and copies ran while one was open for 13% of the time, Pallas kernels for 0%

profile of v2, /device:TPU:0, one launch (start us, length us, event | category | flops | bytes accessed | tf_op | source)
XLA Modules:
  0.0 250.1 jit_solution(15492797464639659020)
XLA Ops:
  1.7 1.2 select_reduce_fusion
  3.8 1.1 pad_maximum_fusion.1
  4.9 4.0 %collective-permute-start.6 = (bf16[64,3712]{1,0:T(8,128)(2,1)S(1)}, bf16[64,3712]{1,0:T(8,128)(2,1)S(1)}, u32[]{:S(2)}, u32[]{:S(2)}) collective-permute-start(bf16[64,3712]{1,0:T(8,128)(2,1)S(1)} %pad_maximum_fusion.1), channel_id=1, source_target_pairs={{0,37},{1,36},{2,39},{3,38},{4,33},{5,32},{6,35},{7,34},{8,45},{9,... | collective-permute-start | bytes 1425416 | tf_op jit(solution)/shard_map/ppermute | solution.py:35
  11.2 1.8 constant_dynamic-update-slice_fusion
  13.0 2.7 %collective-permute-done.6 = bf16[64,3712]{1,0:T(8,128)(2,1)S(1)} collective-permute-done((bf16[64,3712]{1,0:T(8,128)(2,1)S(1)}, bf16[64,3712]{1,0:T(8,128)(2,1)S(1)}, u32[]{:S(2)}, u32[]{:S(2)}) %collective-permute-start.6) | collective-permute-done | bytes 475168 | tf_op jit(solution)/shard_map/ppermute | solution.py:35
  15.9 4.8 %collective-permute-done.2 = bf16[64,3712]{1,0:T(8,128)(2,1)S(1)} collective-permute-done((bf16[64,3712]{1,0:T(8,128)(2,1)S(1)}, bf16[64,3712]{1,0:T(8,128)(2,1)S(1)}, u32[]{:S(2)}, u32[]{:S(2)}) %collective-permute-start.2) | collective-permute-done | bytes 475168 | tf_op jit(solution)/shard_map/ppermute | solution.py:35
  21.5 1.6 collective-permute-start.4
  23.1 1.3 collective-permute-start.3
  25.3 0.8 slice_dynamic-update-slice_fusion.5
  26.9 3.4 %collective-permute-done.4 = bf16[64,3712]{1,0:T(8,128)(2,1)S(1)} collective-permute-done((bf16[64,3712]{1,0:T(8,128)(2,1)S(1)}, bf16[64,3712]{1,0:T(8,128)(2,1)S(1)}, u32[]{:S(2)}, u32[]{:S(2)}) %collective-permute-start.4) | collective-permute-done | bytes 475168 | tf_op jit(solution)/shard_map/ppermute | solution.py:35
  30.4 1.4 collective-permute-done.3
  31.9 1.2 collective-permute-done.5
  37.2 6.2 %convolution_convert_fusion = bf16[1024,3584]{1,0:T(8,128)(2,1)S(1)} fusion(bf16[1024,512]{1,0:T(8,128)(2,1)S(1)} %bitcast.70, bf16[512,3584]{1,0:T(8,128)(2,1)} %slice_dynamic-update-slice_fusion), kind=kOutput, calls=%fused_computation | convolution fusion | flops 3761766400 | bytes 12058624 | tf_op jit(solution)/shard_map/dot_general | solution.py:132
  43.4 56.5 %all_to_all.10 = bf16[8,128,3584]{2,1,0:T(8,128)(2,1)S(1)} all-to-all(bf16[8,128,3584]{2,1,0:T(8,128)(2,1)S(1)} %bitcast.64), channel_id=1, replica_groups={{0,3,12,15,96,99,108,111},{1,2,13,14,97,98,109,110},{4,7,8,11,100,103,1..., dimensions={0} | all-to-all | bytes 14680064 | tf_op jit(solution)/shard_map/all_to_all | solution.py:54
  100.0 2.5 fusion.34
  102.4 6.4 %collective-permute-done.7 = bf16[512,3584]{1,0:T(8,128)(2,1)S(1)} collective-permute-done((bf16[512,3584]{1,0:T(8,128)(2,1)S(1)}, bf16[512,3584]{1,0:T(8,128)(2,1)S(1)}, u32[]{:S(2)}, u32[]{:S(2)}) %collective-permute-start.7) | collective-permute-done | bytes 3670048 | tf_op jit(solution)/shard_map/ppermute | solution.py:39
  108.8 1.9 copy-done
  110.7 7.7 %fusion.4 = f32[512,1024]{1,0:T(8,128)} fusion(bf16[512,3584]{1,0:T(8,128)(2,1)S(1)} %collective-permute-done.7, bf16[1,3584,1024]{2,1,0:T(8,128)(2,1)} %param.11), kind=kOutput, calls=%fused_computation.6 | convolution fusion | flops 3758096384 | bytes 13107200 | tf_op jit(solution)/shard_map/dot_general | solution.py:139
  118.4 16.6 %fusion.15 = bf16[512,3584]{1,0:T(8,128)(2,1)} fusion(bf16[1,1024,3584]{2,1,0:T(8,128)(2,1)} %param.12, f32[512,1024]{1,0:T(8,128)} %fusion.4, bf16[512,3584]{1,0:T(8,128)(2,1)} %copy-done, bf16[1,3584,1024]{2,1,0:T(8,128)(2,1)} %param.10), kind=kOutput, calls=%fused_computation.15 | convolution fusion | flops 7521173504 | bytes 24117248 | tf_op jit(solution)/shard_map/dot_general | solution.py:143
  135.1 9.5 %fusion.6 = f32[512,1024]{1,0:T(8,128)} fusion(bf16[512,3584]{1,0:T(8,128)(2,1)} %bitcast.65, bf16[1,3584,1024]{2,1,0:T(8,128)(2,1)} %param.11), kind=kOutput, calls=%fused_computation.8 | convolution fusion | flops 3758096384 | bytes 13107200 | tf_op jit(solution)/shard_map/dot_general | solution.py:139
  144.6 16.7 %fusion.12 = bf16[512,3584]{1,0:T(8,128)(2,1)} fusion(bf16[1,1024,3584]{2,1,0:T(8,128)(2,1)} %param.12, f32[512,1024]{1,0:T(8,128)} %fusion.6, bf16[512,3584]{1,0:T(8,128)(2,1)} %bitcast.66, bf16[1,3584,1024]{2,1,0:T(8,128)(2,1)} %param.10), kind=kOutput, calls=%fused_computation.14 | convolution fusion | flops 7521173504 | bytes 24117248 | tf_op jit(solution)/shard_map/dot_general | solution.py:143
  161.3 6.6 %pad_maximum_fusion = bf16[8,128,3584]{2,1,0:T(8,128)(2,1)} fusion(bf16[8,64,3584]{2,1,0:T(8,128)(2,1)} %collective-permute-done.8, bf16[8,64,3584]{2,1,0:T(8,128)(2,1)} %bitcast.67), kind=kLoop, calls=%fused_computation.1 | loop fusion | flops 14680064 | bytes 14680064 | tf_op jit(solution)/shard_map/concatenate | solution.py:148
  167.8 52.3 %all_to_all.11 = bf16[8,128,3584]{2,1,0:T(8,128)(2,1)S(1)} all-to-all(bf16[8,128,3584]{2,1,0:T(8,128)(2,1)} %pad_maximum_fusion), channel_id=1, replica_groups={{0,3,12,15,96,99,108,111},{1,2,13,14,97,98,109,110},{4,7,8,11,100,103,1..., dimensions={0} | all-to-all | bytes 14680064 | tf_op jit(solution)/shard_map/all_to_all | solution.py:54
  220.1 4.3 %convolution_convert_fusion.1 = bf16[512,3584]{1,0:T(8,128)(2,1)S(1)} fusion(bf16[1024,512]{1,0:T(8,128)(2,1)S(1)} %bitcast.69, bf16[1024,3584]{1,0:T(8,128)(2,1)S(1)} %bitcast.63), kind=kOutput, calls=%fused_computation.16 | convolution fusion | flops 3759931392 | bytes 12058624 | tf_op jit(solution)/shard_map/dot_general | solution.py:149
  224.8 4.8 %collective-permute-start.9 = (bf16[64,3584]{1,0:T(8,128)(2,1)S(1)}, bf16[64,3584]{1,0:T(8,128)(2,1)S(1)}, u32[]{:S(2)}, u32[]{:S(2)}) collective-permute-start(bf16[64,3584]{1,0:T(8,128)(2,1)S(1)} %get-tuple-element.9), channel_id=1, source_target_pairs={{0,37},{1,36},{2,39},{3,38},{4,33},{5,32},{6,35},{7,34},{8,45},{9,... | collective-permute-start | bytes 1376264 | tf_op jit(solution)/shard_map/ppermute | solution.py:35
  229.6 3.5 %collective-permute-done.14 = bf16[64,3584]{1,0:T(8,128)(2,1)S(1)} collective-permute-done((bf16[64,3584]{1,0:T(8,128)(2,1)S(1)}, bf16[64,3584]{1,0:T(8,128)(2,1)S(1)}, u32[]{:S(2)}, u32[]{:S(2)}) %collective-permute-start.14) | collective-permute-done | bytes 458784 | tf_op jit(solution)/shard_map/ppermute | solution.py:35
  233.1 5.0 %collective-permute-done.12 = bf16[64,3584]{1,0:T(8,128)(2,1)S(1)} collective-permute-done((bf16[64,3584]{1,0:T(8,128)(2,1)S(1)}, bf16[64,3584]{1,0:T(8,128)(2,1)S(1)}, u32[]{:S(2)}, u32[]{:S(2)}) %collective-permute-start.12) | collective-permute-done | bytes 458784 | tf_op jit(solution)/shard_map/ppermute | solution.py:35
  238.5 2.0 collective-permute-start.11
  240.5 1.9 collective-permute-start.13
  242.5 4.6 %collective-permute-done.11 = bf16[64,3584]{1,0:T(8,128)(2,1)S(1)} collective-permute-done((bf16[64,3584]{1,0:T(8,128)(2,1)S(1)}, bf16[64,3584]{1,0:T(8,128)(2,1)S(1)}, u32[]{:S(2)}, u32[]{:S(2)}) %collective-permute-start.11) | collective-permute-done | bytes 458784 | tf_op jit(solution)/shard_map/ppermute | solution.py:35
  247.1 1.9 collective-permute-done.15
  249.0 1.1 add_convert_fusion
  (64 shorter events, 12.8 us)
Async XLA Ops:
  4.9 10.9 %collective-permute-start.6 = (bf16[64,3712]{1,0:T(8,128)(2,1)S(1)}, bf16[64,3712]{1,0:T(8,128)(2,1)S(1)}, u32[]{:S(2)}, u32[]{:S(2)}) collective-permute-start(bf16[64,3712]{1,0:T(8,128)(2,1)S(1)} %pad_maximum_fusion.1), channel_id=1, source_target_pairs={{0,37},{1,36},{2,39},{3,38},{4,33},{5,32},{6,35},{7,34},{8,45},{9,... | collective-permute-start | bytes 1425416 | tf_op jit(solution)/shard_map/ppermute | solution.py:35
  8.9 11.7 %collective-permute-start.2 = (bf16[64,3712]{1,0:T(8,128)(2,1)S(1)}, bf16[64,3712]{1,0:T(8,128)(2,1)S(1)}, u32[]{:S(2)}, u32[]{:S(2)}) collective-permute-start(bf16[64,3712]{1,0:T(8,128)(2,1)S(1)} %pad_maximum_fusion.1), channel_id=1, source_target_pairs={{0,1},{1,0},{2,3},{3,2},{4,5},{5,4},{6,7},{7,6},{8,9},{9,8},{10,11... | collective-permute-start | bytes 1425416 | tf_op jit(solution)/shard_map/ppermute | solution.py:35
  9.0 12.2 %collective-permute-start.1 = (bf16[64,3712]{1,0:T(8,128)(2,1)S(1)}, bf16[64,3712]{1,0:T(8,128)(2,1)S(1)}, u32[]{:S(2)}, u32[]{:S(2)}) collective-permute-start(bf16[64,3712]{1,0:T(8,128)(2,1)S(1)} %pad_maximum_fusion.1), channel_id=1, source_target_pairs={{0,4},{1,5},{2,6},{3,7},{4,0},{5,1},{6,2},{7,3},{8,12},{9,13},{10,... | collective-permute-start | bytes 1425416 | tf_op jit(solution)/shard_map/ppermute | solution.py:35
  9.6 11.8 %collective-permute-start = (bf16[64,3712]{1,0:T(8,128)(2,1)S(1)}, bf16[64,3712]{1,0:T(8,128)(2,1)S(1)}, u32[]{:S(2)}, u32[]{:S(2)}) collective-permute-start(bf16[64,3712]{1,0:T(8,128)(2,1)S(1)} %pad_maximum_fusion.1), channel_id=1, source_target_pairs={{0,32},{1,33},{2,34},{3,35},{4,36},{5,37},{6,38},{7,39},{8,40},{9,... | collective-permute-start | bytes 1425416 | tf_op jit(solution)/shard_map/ppermute | solution.py:35
  21.5 8.7 %collective-permute-start.4 = (bf16[64,3712]{1,0:T(8,128)(2,1)S(1)}, bf16[64,3712]{1,0:T(8,128)(2,1)S(1)}, u32[]{:S(2)}, u32[]{:S(2)}) collective-permute-start(bf16[64,3712]{1,0:T(8,128)(2,1)S(1)} %collective-permute-done.2), channel_id=1, source_target_pairs={{0,4},{1,5},{2,6},{3,7},{4,0},{5,1},{6,2},{7,3},{8,12},{9,13},{10,... | collective-permute-start | bytes 1425416 | tf_op jit(solution)/shard_map/ppermute | solution.py:35
  23.1 8.7 %collective-permute-start.3 = (bf16[64,3712]{1,0:T(8,128)(2,1)S(1)}, bf16[64,3712]{1,0:T(8,128)(2,1)S(1)}, u32[]{:S(2)}, u32[]{:S(2)}) collective-permute-start(bf16[64,3712]{1,0:T(8,128)(2,1)S(1)} %collective-permute-done.1), channel_id=1, source_target_pairs={{0,32},{1,33},{2,34},{3,35},{4,36},{5,37},{6,38},{7,39},{8,40},{9,... | collective-permute-start | bytes 1425416 | tf_op jit(solution)/shard_map/ppermute | solution.py:35
  24.4 8.7 %collective-permute-start.5 = (bf16[64,3712]{1,0:T(8,128)(2,1)S(1)}, bf16[64,3712]{1,0:T(8,128)(2,1)S(1)}, u32[]{:S(2)}, u32[]{:S(2)}) collective-permute-start(bf16[64,3712]{1,0:T(8,128)(2,1)S(1)} %collective-permute-done), channel_id=1, source_target_pairs={{0,1},{1,0},{2,3},{3,2},{4,5},{5,4},{6,7},{7,6},{8,9},{9,8},{10,11... | collective-permute-start | bytes 1425416 | tf_op jit(solution)/shard_map/ppermute | solution.py:35
  102.4 6.4 %collective-permute-start.7 = (bf16[512,3584]{1,0:T(8,128)(2,1)S(1)}, bf16[512,3584]{1,0:T(8,128)(2,1)S(1)}, u32[]{:S(2)}, u32[]{:S(2)}) collective-permute-start(bf16[512,3584]{1,0:T(8,128)(2,1)S(1)} %bitcast.68), channel_id=1, source_target_pairs={{0,16},{1,17},{2,18},{3,19},{4,20},{5,21},{6,22},{7,23},{8,24},{9,... | collective-permute-start | bytes 11010056 | tf_op jit(solution)/shard_map/ppermute | solution.py:39
  108.8 1.9 copy-start
  135.0 26.3 %collective-permute-start.8 = (bf16[8,64,3584]{2,1,0:T(8,128)(2,1)}, bf16[8,64,3584]{2,1,0:T(8,128)(2,1)}, u32[]{:S(2)}, u32[]{:S(2)}) collective-permute-start(bf16[8,64,3584]{2,1,0:T(8,128)(2,1)} %bitcast.87), channel_id=1, source_target_pairs={{0,16},{1,17},{2,18},{3,19},{4,20},{5,21},{6,22},{7,23},{8,24},{9,... | collective-permute-start | bytes 11010056 | tf_op jit(solution)/shard_map/ppermute | solution.py:39
  224.5 8.6 %collective-permute-start.14 = (bf16[64,3584]{1,0:T(8,128)(2,1)S(1)}, bf16[64,3584]{1,0:T(8,128)(2,1)S(1)}, u32[]{:S(2)}, u32[]{:S(2)}) collective-permute-start(bf16[64,3584]{1,0:T(8,128)(2,1)S(1)} %get-tuple-element.10), channel_id=1, source_target_pairs={{0,4},{1,5},{2,6},{3,7},{4,0},{5,1},{6,2},{7,3},{8,12},{9,13},{10,... | collective-permute-start | bytes 1376264 | tf_op jit(solution)/shard_map/ppermute | solution.py:35
  224.6 13.5 %collective-permute-start.12 = (bf16[64,3584]{1,0:T(8,128)(2,1)S(1)}, bf16[64,3584]{1,0:T(8,128)(2,1)S(1)}, u32[]{:S(2)}, u32[]{:S(2)}) collective-permute-start(bf16[64,3584]{1,0:T(8,128)(2,1)S(1)} %get-tuple-element.11), channel_id=1, source_target_pairs={{0,32},{1,33},{2,34},{3,35},{4,36},{5,37},{6,38},{7,39},{8,40},{9,... | collective-permute-start | bytes 1376264 | tf_op jit(solution)/shard_map/ppermute | solution.py:35
  224.7 13.5 %collective-permute-start.10 = (bf16[64,3584]{1,0:T(8,128)(2,1)S(1)}, bf16[64,3584]{1,0:T(8,128)(2,1)S(1)}, u32[]{:S(2)}, u32[]{:S(2)}) collective-permute-start(bf16[64,3584]{1,0:T(8,128)(2,1)S(1)} %get-tuple-element.12), channel_id=1, source_target_pairs={{0,1},{1,0},{2,3},{3,2},{4,5},{5,4},{6,7},{7,6},{8,9},{9,8},{10,11... | collective-permute-start | bytes 1376264 | tf_op jit(solution)/shard_map/ppermute | solution.py:35
  224.8 17.7 %collective-permute-start.9 = (bf16[64,3584]{1,0:T(8,128)(2,1)S(1)}, bf16[64,3584]{1,0:T(8,128)(2,1)S(1)}, u32[]{:S(2)}, u32[]{:S(2)}) collective-permute-start(bf16[64,3584]{1,0:T(8,128)(2,1)S(1)} %get-tuple-element.9), channel_id=1, source_target_pairs={{0,37},{1,36},{2,39},{3,38},{4,33},{5,32},{6,35},{7,34},{8,45},{9,... | collective-permute-start | bytes 1376264 | tf_op jit(solution)/shard_map/ppermute | solution.py:35
  238.5 8.6 %collective-permute-start.11 = (bf16[64,3584]{1,0:T(8,128)(2,1)S(1)}, bf16[64,3584]{1,0:T(8,128)(2,1)S(1)}, u32[]{:S(2)}, u32[]{:S(2)}) collective-permute-start(bf16[64,3584]{1,0:T(8,128)(2,1)S(1)} %get-tuple-element.13), channel_id=1, source_target_pairs={{0,32},{1,33},{2,34},{3,35},{4,36},{5,37},{6,38},{7,39},{8,40},{9,... | collective-permute-start | bytes 1376264 | tf_op jit(solution)/shard_map/ppermute | solution.py:35
  240.5 8.5 %collective-permute-start.15 = (bf16[64,3584]{1,0:T(8,128)(2,1)S(1)}, bf16[64,3584]{1,0:T(8,128)(2,1)S(1)}, u32[]{:S(2)}, u32[]{:S(2)}) collective-permute-start(bf16[64,3584]{1,0:T(8,128)(2,1)S(1)} %get-tuple-element.14), channel_id=1, source_target_pairs={{0,1},{1,0},{2,3},{3,2},{4,5},{5,4},{6,7},{7,6},{8,9},{9,8},{10,11... | collective-permute-start | bytes 1376264 | tf_op jit(solution)/shard_map/ppermute | solution.py:35
  240.5 8.5 %collective-permute-start.13 = (bf16[64,3584]{1,0:T(8,128)(2,1)S(1)}, bf16[64,3584]{1,0:T(8,128)(2,1)S(1)}, u32[]{:S(2)}, u32[]{:S(2)}) collective-permute-start(bf16[64,3584]{1,0:T(8,128)(2,1)S(1)} %get-tuple-element.15), channel_id=1, source_target_pairs={{0,4},{1,5},{2,6},{3,7},{4,0},{5,1},{6,2},{7,3},{8,12},{9,13},{10,... | collective-permute-start | bytes 1376264 | tf_op jit(solution)/shard_map/ppermute | solution.py:35

commit v3 on v2

v3 whole, which is shorter than its diff:
```python
import functools

import jax
import jax.numpy as jnp
from jax import lax
from jax.experimental import pallas as pl
from jax.experimental.pallas import tpu as pltpu
from jax.sharding import PartitionSpec as P

BOTH = ("node", "local")
RING = 4
CORES = 2
LANES = 128

GATHER = (1, 3)
EXCHANGE = (3, 1)

NEAR = ((0, 0, 0), (1, 0, 0), (0, 1, 0), (0, 0, 1))
FAR = ((1, 1, 0), (0, 1, 1), (1, 0, 1), (1, 1, 1))
CORNERS = tuple((i >> 2 & 1, i >> 1 & 1, i & 1) for i in range(8))


def index_of(y, c, x, z):
    return ((y * CORES + c) * RING + x) * RING + z


def places():
    return [
        (y, c, x, z) for y in range(RING) for c in range(CORES) for x in range(RING) for z in range(RING)
    ]


def moved(place, corner, step):
    y, c, x, z = place
    return index_of(y ^ corner[0] * step, c, x ^ corner[1] * step, z ^ corner[2] * step)


def to_corner(value, corner):
    return lax.ppermute(value, BOTH, [(index_of(*p), moved(p, corner, GATHER[p[1]])) for p in places()])


def to_other_core(value):
    return lax.ppermute(
        value, BOTH, [(index_of(y, c, x, z), index_of(y, 1 - c, x, z)) for y, c, x, z in places()]
    )


def first_of(v, core):
    return (v if v < 2 else v ^ 3) if core == 0 else v & 2


def exchange(value, flip):
    groups = [
        [moved((y, c, x, z), corner, EXCHANGE[c ^ flip]) for corner in CORNERS]
        for y, c, x, z in places()
        if all(first_of(v, c ^ flip) == v for v in (y, x, z))
    ]
    return lax.all_to_all(
        value, BOTH, split_axis=0, concat_axis=0, axis_index_groups=groups, tiled=True
    )


def gather_cube(block):
    y, x, z = [to_corner(block, corner) for corner in NEAR[1:]]
    far = [to_corner(x, NEAR[1]), to_corner(z, NEAR[2]), to_corner(y, NEAR[3]), to_corner(block, FAR[3])]
    return [block, y, x, z] + far


def add(a, *others):
    total = a.astype(jnp.float32)
    for b in others:
        total = total + b.astype(jnp.float32)
    return total.astype(jnp.bfloat16)


def reduce_cube(blocks):
    own, y, x, z, yx, xz, yz, yxz = blocks
    x = add(x, to_corner(yx, NEAR[1]))
    z = add(z, to_corner(xz, NEAR[2]))
    y = add(y, to_corner(yz, NEAR[3]))
    last = to_corner(yxz, FAR[3])
    return add(own, last, *[to_corner(b, corner) for b, corner in zip((y, x, z), NEAR[1:])])


def stack_kernel(count, *refs):
    size = refs[0].shape[0]
    rows_ref, about_ref = refs[2 * count :]
    for i in range(count):
        rows_ref[i * size : (i + 1) * size] = refs[i][...]

    @pl.when(pl.program_id(0) == 0)
    def _():
        for i in range(count):
            about_ref[i * size : (i + 1) * size] = refs[count + i][...]


def stack(blocks, width):
    count, size = len(blocks), blocks[0].shape[0]
    rest = blocks[0].shape[1] - width
    dtype = blocks[0].dtype
    wide = 896
    return pl.pallas_call(
        functools.partial(stack_kernel, count),
        grid=(width // wide,),
        in_specs=[pl.BlockSpec((size, wide), lambda i: (0, i))] * count
        + [pl.BlockSpec((size, rest), lambda i: (0, width // rest))] * count,
        out_specs=[
            pl.BlockSpec((count * size, wide), lambda i: (0, i)),
            pl.BlockSpec((count * size, rest), lambda i: (0, 0)),
        ],
        out_shape=[
            jax.ShapeDtypeStruct((count * size, width), dtype),
            jax.ShapeDtypeStruct((count * size, rest), dtype),
        ],
        compiler_params=pltpu.CompilerParams(vmem_limit_bytes=32 * 2**20),
        name="stack",
    )(*blocks, *blocks)


def follow_kernel(value_ref, after_ref, out_ref):
    del value_ref, after_ref, out_ref


def follow(value, after):
    return pl.pallas_call(
        follow_kernel,
        in_specs=[pl.BlockSpec(memory_space=pl.ANY)] * 2,
        out_specs=pl.BlockSpec(memory_space=pl.ANY),
        out_shape=jax.ShapeDtypeStruct(value.shape, value.dtype),
        input_output_aliases={0: 0},
        name="follow",
    )(value, after)


def expert_kernel(inner, tile, after_ref, rows_ref, gate_ref, up_ref, down_ref, out_ref, hidden):
    del after_ref
    step = pl.program_id(0)

    @pl.when(step < inner)
    def _():
        gate = jnp.dot(rows_ref[...], gate_ref[...], preferred_element_type=jnp.float32)
        up = jnp.dot(rows_ref[...], up_ref[...], preferred_element_type=jnp.float32)
        columns = pl.ds(pl.multiple_of(step * tile, tile), tile)
        hidden[:, columns] = (gate / (1.0 + jnp.exp(-gate)) * up).astype(hidden.dtype)

    @pl.when(step >= inner)
    def _():
        out = jnp.dot(hidden[...], down_ref[...], preferred_element_type=jnp.float32)
        out_ref[...] = out.astype(out_ref.dtype)


def expert(rows, gate, up, down, after):
    count, width = rows.shape
    hidden = gate.shape[1]
    tile = 256
    wide = 512
    inner, outer = hidden // tile, width // wide

    def of_inner(i):
        return 0, jnp.minimum(i, inner - 1)

    def of_outer(i):
        return 0, jnp.maximum(i - inner, 0)

    return pl.pallas_call(
        functools.partial(expert_kernel, inner, tile),
        grid=(inner + outer,),
        in_specs=[
            pl.BlockSpec(memory_space=pl.ANY),
            pl.BlockSpec((count, width), lambda i: (0, 0)),
            pl.BlockSpec((width, tile), of_inner),
            pl.BlockSpec((width, tile), of_inner),
            pl.BlockSpec((hidden, wide), of_outer),
        ],
        out_specs=pl.BlockSpec((count, wide), of_outer),
        out_shape=jax.ShapeDtypeStruct((count, width), rows.dtype),
        scratch_shapes=[pltpu.VMEM((count, hidden), rows.dtype)],
        compiler_params=pltpu.CompilerParams(vmem_limit_bytes=48 * 2**20),
        cost_estimate=pl.CostEstimate(
            flops=6 * count * width * hidden,
            bytes_accessed=2 * (3 * width * hidden + 2 * count * width),
            transcendentals=count * hidden,
        ),
        name="expert",
    )(after, rows, gate, up, down)


def shards(tokens, expert_ids, gate_values, expert_gate, expert_up, expert_down):
    node = lax.axis_index("node")
    local = lax.axis_index("local")
    at = (node // CORES, local // RING, local % RING)
    core = node % CORES
    experts = lax.axis_size("node") * lax.axis_size("local")
    tok, width = tokens.shape
    top = expert_ids.shape[1]
    cap = 2 * tok * top // experts
    corners = len(CORNERS)
    held = corners * tok

    about = jnp.concatenate([expert_ids.astype(jnp.bfloat16), gate_values], axis=1)
    about = jnp.pad(about, ((0, 0), (0, LANES - 2 * top)))
    own_held, own_known = stack(gather_cube(jnp.concatenate([tokens, about], axis=1)), width)
    other_held = to_other_core(own_held)
    other_known = to_other_core(own_known)

    bits = jnp.array(CORNERS, dtype=jnp.int32)
    source = jnp.repeat(jnp.arange(corners, dtype=jnp.int32), tok)
    mask = jnp.arange(corners, dtype=jnp.int32)[:, None, None] == source[None, None, :]
    order = jnp.arange(held, dtype=jnp.int32)
    earlier = (order[:, None] < order[None, :]) & (source[:, None] == source[None, :])
    earlier = earlier.astype(jnp.bfloat16)

    def selection(known, flip):
        side = core ^ flip
        step = jnp.where(side == 0, EXCHANGE[0], EXCHANGE[1])
        base = [jnp.where(side == 0, jnp.where(v < 2, v, v ^ 3), v & 2) for v in at]
        spot = [base[i] ^ (bits[:, i] * step) for i in range(3)]
        wanted = index_of(spot[0], core, spot[1], spot[2])[:, None].astype(jnp.float32)
        known = known.astype(jnp.float32).T[: 2 * top].reshape(2, top, held)
        named = jnp.zeros((corners, held), jnp.float32)
        weight = named
        for k in range(top):
            same = wanted == known[0, k][None, :]
            named = jnp.where(same, jnp.float32(1.0), named)
            weight = jnp.where(same, known[1, k][None, :], weight)
        slot = jnp.dot(named.astype(jnp.bfloat16), earlier, preferred_element_type=jnp.float32)
        slot = jnp.where(named > 0.0, slot, jnp.float32(-1.0))
        chosen = slot[:, None, :] == jnp.arange(cap, dtype=jnp.float32)[None, :, None]
        weights = jnp.where(chosen, weight[:, None, :], jnp.float32(0.0))
        wide = []
        for small in (chosen.astype(jnp.float32), weights):
            small = jnp.where(mask[None], small[:, None], jnp.float32(0.0)).astype(jnp.bfloat16)
            wide.append(small.reshape(corners * corners * cap, held))
        return wide

    flat = (corners * corners * cap, width)
    boxed = (corners, corners * cap, width)
    experts_of = (expert_gate[0], expert_up[0], expert_down[0])

    def send(held, known, flip):
        chosen, weights = selection(known, flip)
        picked = jnp.dot(chosen, held, preferred_element_type=jnp.float32).astype(jnp.bfloat16)
        return exchange(picked.reshape(boxed), flip).reshape(flat), weights

    def collect(back, weights):
        total = lax.dot_general(weights, back, (((0,), (0,)), ((), ())), preferred_element_type=jnp.float32)
        return total.astype(jnp.bfloat16)

    other_rows, other_weights = send(other_held, other_known, 1)
    own_rows, own_weights = send(own_held, own_known, 0)
    other_out = follow(expert(other_rows, *experts_of, expert_ids), own_rows)
    other_back = exchange(other_out.reshape(boxed), 1).reshape(flat)
    own_out = follow(expert(own_rows, *experts_of, other_out), other_back)
    own_back = exchange(own_out.reshape(boxed), 0).reshape(flat)
    other_total = to_other_core(follow(collect(other_back, other_weights), own_out))
    own_total = collect(own_back, own_weights)
    total = add(own_total, other_total)
    return reduce_cube([total[i * tok : (i + 1) * tok] for i in range(corners)])


def solution(mesh):
    placed = (
        P(("node", "local"), None),
        P(("node", "local"), None),
        P(("node", "local"), None),
        P(("node", "local"), None, None),
        P(("node", "local"), None, None),
        P(("node", "local"), None, None),
    )
    return jax.shard_map(
        shards, mesh=mesh, in_specs=placed, out_specs=P(("node", "local"), None), check_vma=False
    )
```

time: 251 us -> 212 us (0.84)
  blocking collectives: 109 us -> 32.4 us
  Pallas kernels: 0 us -> 42.6 us
  matrix products: 60.9 us -> 20.7 us
  waiting for transfers between devices: 35.5 us -> 73.4 us
  starting transfers between devices: 17.3 us -> 32.6 us
  local copies, waits for them, and re-layouts: 14.1 us -> 4.47 us
  other arithmetic: 13.3 us -> 4.52 us
    all_to_all x2 -> x1, blocking collectives: 109 us -> 32.4 us  [exchange(): lax.all_to_all(value, BOTH, split_axis=0, concat_axis=0, axis_index_group...]
    pallas_call x0 -> x6, Pallas kernels: none -> 42.6 us  [the longest x2 39.1 us: expert(): pl.pallas_call(functools.partial(expert_kernel, inner, tile), grid=(inner...]
    dot_general x6, matrix products: 60.9 us -> 20.7 us  [the longest x2 11.9 us: send(): jnp.dot(chosen, held, preferred_element_type=jnp.float32)]
    all_to_all x0 -> x3, waiting for transfers between devices: none -> 37 us  [exchange(): lax.all_to_all(value, BOTH, split_axis=0, concat_axis=0, axis_index_group...]
    all_to_all x0 -> x3, starting transfers between devices: none -> 13.8 us  [exchange(): lax.all_to_all(value, BOTH, split_axis=0, concat_axis=0, axis_index_group...]
    concatenate x3 -> x2, other arithmetic: 8.33 us -> 1.74 us  [the longest x1 1.05 us: shards(): jnp.concatenate([tokens, about], axis=1)]
    unnamed x17 -> x13, local copies, waits for them, and re-layouts: 10.1 us -> 3.89 us
    ppermute x2 -> x3, starting transfers between devices: 0.14 us -> 2.93 us  [to_other_core(): lax.ppermute(value, BOTH, [(index_of(y, c, x, z), index_of(y, 1 - c, x, z...]
  transfers between devices with their start and end apart: 16 -> 20, of which waited for: 12 -> 16; matrix products, arithmetic and copies ran while one was open for 13% -> 4% of each run, Pallas kernels for 0% -> 19%
where the time goes in v3:
time: 212 us; the launch traced here: 211 us
  waiting for transfers between devices  73.4 us (35%)
  Pallas kernels  42.6 us (20%)
  starting transfers between devices  32.6 us (15%)
  blocking collectives  32.4 us (15%)
  matrix products  20.7 us (10%)
  other arithmetic  4.52 us (2%)
  local copies, waits for them, and re-layouts  4.47 us (2%)
    pallas_call x2, Pallas kernels, expert(): pl.pallas_call(functools.partial(expert_kernel, inner, tile), grid=(inner...  39.1 us
    all_to_all x3, waiting for transfers between devices, exchange(): lax.all_to_all(value, BOTH, split_axis=0, concat_axis=0, axis_index_group...  37 us
    all_to_all x1, blocking collectives, exchange(): lax.all_to_all(value, BOTH, split_axis=0, concat_axis=0, axis_index_group...  32.4 us
    ppermute x14, waiting for transfers between devices, to_corner(): lax.ppermute(value, BOTH, [(index_of(*p), moved(p, corner, GATHER[p[1]]))...  31.1 us
    ppermute x14, starting transfers between devices, to_corner(): lax.ppermute(value, BOTH, [(index_of(*p), moved(p, corner, GATHER[p[1]]))...  15.9 us
    all_to_all x3, starting transfers between devices, exchange(): lax.all_to_all(value, BOTH, split_axis=0, concat_axis=0, axis_index_group...  13.8 us
    dot_general x2, matrix products, send(): jnp.dot(chosen, held, preferred_element_type=jnp.float32)  11.9 us
    dot_general x2, matrix products, collect(): lax.dot_general(weights, back, (((0,), (0,)), ((), ())), preferred_elemen...  8.08 us
  transfers between devices with their start and end apart: 20, of which 16 were waited for; matrix products, arithmetic and copies ran while one was open for 4% of the time, Pallas kernels for 19%

profile of v3, /device:TPU:0, one launch (start us, length us, event | category | flops | bytes accessed | tf_op | source)
XLA Modules:
  0.0 211.0 jit_solution(16235663700313397232)
XLA Ops:
  2.6 1.7 collective-permute-start.1
  4.2 1.9 collective-permute-start.2
  7.7 3.6 %collective-permute-done.1.refs_2_.refs_10_ = bf16[64,3712]{1,0:T(8,128)(2,1)S(1)} collective-permute-done((bf16[64,3712]{1,0:T(8,128)(2,1)S(1)}, bf16[64,3712]{1,0:T(8,128)(2,1)S(1)}, u32[]{:S(2)}, u32[]{:S(2)}) %collective-permute-start.1) | collective-permute-done | bytes 475168 | tf_op jit(solution)/shard_map/ppermute | solution.py:39
  11.3 1.7 collective-permute-start.3
  13.0 4.4 %collective-permute-done.2.refs_3_.refs_11_ = bf16[64,3712]{1,0:T(8,128)(2,1)S(1)} collective-permute-done((bf16[64,3712]{1,0:T(8,128)(2,1)S(1)}, bf16[64,3712]{1,0:T(8,128)(2,1)S(1)}, u32[]{:S(2)}, u32[]{:S(2)}) %collective-permute-start.2) | collective-permute-done | bytes 475168 | tf_op jit(solution)/shard_map/ppermute | solution.py:39
  17.4 2.5 %collective-permute-done.refs_1_.refs_9_ = bf16[64,3712]{1,0:T(8,128)(2,1)S(1)} collective-permute-done((bf16[64,3712]{1,0:T(8,128)(2,1)S(1)}, bf16[64,3712]{1,0:T(8,128)(2,1)S(1)}, u32[]{:S(2)}, u32[]{:S(2)}) %collective-permute-start) | collective-permute-done | bytes 475168 | tf_op jit(solution)/shard_map/ppermute | solution.py:39
  20.0 5.0 %collective-permute-done.3.refs_4_.refs_12_ = bf16[64,3712]{1,0:T(8,128)(2,1)S(1)} collective-permute-done((bf16[64,3712]{1,0:T(8,128)(2,1)S(1)}, bf16[64,3712]{1,0:T(8,128)(2,1)S(1)}, u32[]{:S(2)}, u32[]{:S(2)}) %collective-permute-start.3) | collective-permute-done | bytes 475168 | tf_op jit(solution)/shard_map/ppermute | solution.py:39
  26.1 2.5 %collective-permute-done.5.refs_6_.refs_14_ = bf16[64,3712]{1,0:T(8,128)(2,1)S(1)} collective-permute-done((bf16[64,3712]{1,0:T(8,128)(2,1)S(1)}, bf16[64,3712]{1,0:T(8,128)(2,1)S(1)}, u32[]{:S(2)}, u32[]{:S(2)}) %collective-permute-start.5) | collective-permute-done | bytes 475168 | tf_op jit(solution)/shard_map/ppermute | solution.py:39
  28.5 3.5 %stack.1 = (bf16[512,3584]{1,0:T(8,128)(2,1)}, bf16[512,128]{1,0:T(8,128)(2,1)S(1)}) custom-call(bf16[64,3712]{1,0:T(8,128)(2,1)S(1)} %fusion.8.refs_0_.refs_8_, bf16[64,3712]{1,0:T(8,128)(2,1)S(1)} %collective-permute-done.refs_1_.refs_9_, bf16[64,3712]{1,0:T(8,128)(2,1)S(1)} %collective-permute-done.1.refs_2_.refs_10_, ...), custom_call_target="tpu_custom_call" | custom-call | tf_op jit(solution)/shard_map/stack/pallas_call | solution.py:102
  32.0 2.8 %collective-permute-start.8 = (bf16[512,3584]{1,0:T(8,128)(2,1)}, bf16[512,3584]{1,0:T(8,128)(2,1)}, u32[]{:S(2)}, u32[]{:S(2)}) collective-permute-start(bf16[512,3584]{1,0:T(8,128)(2,1)} %get-tuple-element.8), channel_id=1, source_target_pairs={{0,16},{1,17},{2,18},{3,19},{4,20},{5,21},{6,22},{7,23},{8,24},{9,... | collective-permute-start | bytes 11010056 | tf_op jit(solution)/shard_map/ppermute | solution.py:43
  35.7 5.3 %collective-permute-done.7 = bf16[512,128]{1,0:T(8,128)(2,1)S(1)} collective-permute-done((bf16[512,128]{1,0:T(8,128)(2,1)S(1)}, bf16[512,128]{1,0:T(8,128)(2,1)S(1)}, u32[]{:S(2)}, u32[]{:S(2)}) %collective-permute-start.7) | collective-permute-done | bytes 131104 | tf_op jit(solution)/shard_map/ppermute | solution.py:43
  42.1 6.0 %convolution_convert_fusion.3 = bf16[512,3584]{1,0:T(8,128)(2,1)} fusion(bf16[512,512]{1,0:T(8,128)(2,1)S(1)} %bitcast.72, bf16[512,3584]{1,0:T(8,128)(2,1)} %collective-permute-done.8), kind=kOutput, calls=%fused_computation.4 | convolution fusion | flops 1880883200 | bytes 7864320 | tf_op jit(solution)/shard_map/dot_general | solution.py:242
  48.1 4.5 %all-to-all-start = ((bf16[8,64,3584]{2,1,0:T(8,128)(2,1)}), bf16[8,64,3584]{2,1,0:T(8,128)(2,1)}, u32[]{:S(2)}, u32[]{:S(2)}) async-start(bf16[8,64,3584]{2,1,0:T(8,128)(2,1)} %bitcast.68), calls=%async_computation | async-start | bytes 7340032 | tf_op jit(solution)/shard_map/all_to_all | solution.py:58
  52.6 5.9 %convolution_convert_fusion.2 = bf16[512,3584]{1,0:T(8,128)(2,1)} fusion(bf16[512,512]{1,0:T(8,128)(2,1)S(1)} %bitcast.71, bf16[512,3584]{1,0:T(8,128)(2,1)} %get-tuple-element.8), kind=kOutput, calls=%fused_computation.3 | convolution fusion | flops 1880883200 | bytes 7864320 | tf_op jit(solution)/shard_map/dot_general | solution.py:242
  58.5 22.4 %all-to-all-done = bf16[8,64,3584]{2,1,0:T(8,128)(2,1)} async-done(((bf16[8,64,3584]{2,1,0:T(8,128)(2,1)}), bf16[8,64,3584]{2,1,0:T(8,128)(2,1)}, u32[]{:S(2)}, u32[]{:S(2)}) %all-to-all-start) | async-done | bytes 3670048 | tf_op jit(solution)/shard_map/all_to_all | solution.py:58
  80.9 4.6 %all-to-all-start.1 = ((bf16[8,64,3584]{2,1,0:T(8,128)(2,1)}), bf16[8,64,3584]{2,1,0:T(8,128)(2,1)}, u32[]{:S(2)}, u32[]{:S(2)}) async-start(bf16[8,64,3584]{2,1,0:T(8,128)(2,1)} %bitcast.67), calls=%async_computation.1 | async-start | bytes 7340032 | tf_op jit(solution)/shard_map/all_to_all | solution.py:58
  85.6 19.6 %expert.2.value_ref = bf16[512,3584]{1,0:T(8,128)(2,1)S(1)} custom-call(s32[64,8]{1,0:T(8,128)S(1)} %copy.26.after_ref, bf16[512,3584]{1,0:T(8,128)(2,1)} %bitcast.33.rows_ref, bf16[3584,1024]{1,0:T(8,128)(2,1)} %bitcast.124, bf16[3584,1024]{1,0:T(8,128)(2,1)} %bitcast.126, bf16[1024,3584]{1,0:T(8,128)(2,1)} %bitcast.128), custom_call_target="tpu_custom_call" | custom-call | flops 11274289152 | bytes 29360128 | tf_op jit(solution)/shard_map/expert/pallas_call | solution.py:165
  105.2 1.9 copy-done.1
  107.1 7.9 %all-to-all-done.1 = bf16[8,64,3584]{2,1,0:T(8,128)(2,1)} async-done(((bf16[8,64,3584]{2,1,0:T(8,128)(2,1)}), bf16[8,64,3584]{2,1,0:T(8,128)(2,1)}, u32[]{:S(2)}, u32[]{:S(2)}) %all-to-all-start.1) | async-done | bytes 3670048 | tf_op jit(solution)/shard_map/all_to_all | solution.py:58
  115.1 4.7 %all-to-all-start.2 = ((bf16[8,64,3584]{2,1,0:T(8,128)(2,1)}), bf16[8,64,3584]{2,1,0:T(8,128)(2,1)}, u32[]{:S(2)}, u32[]{:S(2)}) async-start(bf16[8,64,3584]{2,1,0:T(8,128)(2,1)} %bitcast.64), calls=%async_computation.2 | async-start | bytes 7340032 | tf_op jit(solution)/shard_map/all_to_all | solution.py:58
  119.8 19.6 %expert.3.value_ref = bf16[512,3584]{1,0:T(8,128)(2,1)S(1)} custom-call(bf16[512,3584]{1,0:T(8,128)(2,1)} %follow.3.after_ref, bf16[512,3584]{1,0:T(8,128)(2,1)} %bitcast.39.after_ref.rows_ref, bf16[3584,1024]{1,0:T(8,128)(2,1)} %bitcast.125, bf16[3584,1024]{1,0:T(8,128)(2,1)} %bitcast.127, bf16[1024,3584]{1,0:T(8,128)(2,1)} %bitcast.129), custom_call_target="tpu_custom_call" | custom-call | flops 11274289152 | bytes 29360128 | tf_op jit(solution)/shard_map/expert/pallas_call | solution.py:165
  139.4 1.9 copy-done
  141.2 6.7 %all-to-all-done.2 = bf16[8,64,3584]{2,1,0:T(8,128)(2,1)} async-done(((bf16[8,64,3584]{2,1,0:T(8,128)(2,1)}), bf16[8,64,3584]{2,1,0:T(8,128)(2,1)}, u32[]{:S(2)}, u32[]{:S(2)}) %all-to-all-start.2) | async-done | bytes 3670048 | tf_op jit(solution)/shard_map/all_to_all | solution.py:58
  147.9 5.9 %convolution_convert_fusion.value_ref = bf16[512,3584]{1,0:T(8,128)(2,1)} fusion(bf16[512,512]{1,0:T(8,128)(2,1)S(1)} %bitcast.70, bf16[512,3584]{1,0:T(8,128)(2,1)} %bitcast.41.after_ref), kind=kOutput, calls=%fused_computation.1 | convolution fusion | flops 1880883200 | bytes 7864320 | tf_op jit(solution)/shard_map/dot_general | solution.py:246
  153.8 32.4 %all_to_all.20 = bf16[8,64,3584]{2,1,0:T(8,128)(2,1)S(1)} all-to-all(bf16[8,64,3584]{2,1,0:T(8,128)(2,1)} %bitcast.63), channel_id=1, replica_groups={{0,3,12,15,96,99,108,111},{1,2,13,14,97,98,109,110},{4,7,8,11,100,103,1..., dimensions={0} | all-to-all | bytes 7340032 | tf_op jit(solution)/shard_map/all_to_all | solution.py:58
  186.3 2.2 %add_convert_fusion = bf16[512,3584]{1,0:T(8,128)(2,1)S(1)} fusion(bf16[512,3584]{1,0:T(8,128)(2,1)S(1)} %collective-permute-done.9, bf16[512,512]{1,0:T(8,128)(2,1)S(1)} %bitcast.69, bf16[512,3584]{1,0:T(8,128)(2,1)S(1)} %bitcast.66), kind=kOutput, calls=%fused_computation | convolution fusion | flops 1888223232 | bytes 11534336 | tf_op jit(solution)/shard_map/dot_general | solution.py:246
  188.9 4.8 %collective-permute-start.10 = (bf16[64,3584]{1,0:T(8,128)(2,1)S(1)}, bf16[64,3584]{1,0:T(8,128)(2,1)S(1)}, u32[]{:S(2)}, u32[]{:S(2)}) collective-permute-start(bf16[64,3584]{1,0:T(8,128)(2,1)S(1)} %get-tuple-element.9), channel_id=1, source_target_pairs={{0,37},{1,36},{2,39},{3,38},{4,33},{5,32},{6,35},{7,34},{8,45},{9,... | collective-permute-start | bytes 1376264 | tf_op jit(solution)/shard_map/ppermute | solution.py:39
  193.6 3.5 %collective-permute-done.11 = bf16[64,3584]{1,0:T(8,128)(2,1)S(1)} collective-permute-done((bf16[64,3584]{1,0:T(8,128)(2,1)S(1)}, bf16[64,3584]{1,0:T(8,128)(2,1)S(1)}, u32[]{:S(2)}, u32[]{:S(2)}) %collective-permute-start.11) | collective-permute-done | bytes 458784 | tf_op jit(solution)/shard_map/ppermute | solution.py:39
  197.7 2.0 collective-permute-start.12
  199.7 1.9 collective-permute-start.16
  201.6 3.5 %collective-permute-done.10 = bf16[64,3584]{1,0:T(8,128)(2,1)S(1)} collective-permute-done((bf16[64,3584]{1,0:T(8,128)(2,1)S(1)}, bf16[64,3584]{1,0:T(8,128)(2,1)S(1)}, u32[]{:S(2)}, u32[]{:S(2)}) %collective-permute-start.10) | collective-permute-done | bytes 458784 | tf_op jit(solution)/shard_map/ppermute | solution.py:39
  205.2 3.4 %collective-permute-done.12 = bf16[64,3584]{1,0:T(8,128)(2,1)S(1)} collective-permute-done((bf16[64,3584]{1,0:T(8,128)(2,1)S(1)}, bf16[64,3584]{1,0:T(8,128)(2,1)S(1)}, u32[]{:S(2)}, u32[]{:S(2)}) %collective-permute-start.12) | collective-permute-done | bytes 458784 | tf_op jit(solution)/shard_map/ppermute | solution.py:39
  (56 shorter events, 10.6 us)
Async XLA Ops:
  2.5 32.4 %copy-start.3 = (s32[8,1]{0,1:T(1,128)S(1)}, s32[8,1]{0,1:T(1,128)}, u32[]{:S(2)}) copy-start(s32[8,1]{0,1:T(1,128)} %constant.76) | copy-start | bytes 100
  2.5 32.4 %copy-start.4 = (s32[8,1]{0,1:T(1,128)S(1)}, s32[8,1]{0,1:T(1,128)}, u32[]{:S(2)}) copy-start(s32[8,1]{0,1:T(1,128)} %constant.77) | copy-start | bytes 100
  2.6 32.4 %copy-start.5 = (s32[8,1]{0,1:T(1,128)S(1)}, s32[8,1]{0,1:T(1,128)}, u32[]{:S(2)}) copy-start(s32[8,1]{0,1:T(1,128)} %constant.78) | copy-start | bytes 100
  2.6 8.7 %collective-permute-start.1 = (bf16[64,3712]{1,0:T(8,128)(2,1)S(1)}, bf16[64,3712]{1,0:T(8,128)(2,1)S(1)}, u32[]{:S(2)}, u32[]{:S(2)}) collective-permute-start(bf16[64,3712]{1,0:T(8,128)(2,1)S(1)} %fusion.8.refs_0_.refs_8_), channel_id=1, source_target_pairs={{0,4},{1,5},{2,6},{3,7},{4,0},{5,1},{6,2},{7,3},{8,12},{9,13},{10,... | collective-permute-start | bytes 1425416 | tf_op jit(solution)/shard_map/ppermute | solution.py:39
  4.2 13.2 %collective-permute-start.2 = (bf16[64,3712]{1,0:T(8,128)(2,1)S(1)}, bf16[64,3712]{1,0:T(8,128)(2,1)S(1)}, u32[]{:S(2)}, u32[]{:S(2)}) collective-permute-start(bf16[64,3712]{1,0:T(8,128)(2,1)S(1)} %fusion.8.refs_0_.refs_8_), channel_id=1, source_target_pairs={{0,1},{1,0},{2,3},{3,2},{4,5},{5,4},{6,7},{7,6},{8,9},{9,8},{10,11... | collective-permute-start | bytes 1425416 | tf_op jit(solution)/shard_map/ppermute | solution.py:39
  6.1 13.7 %collective-permute-start = (bf16[64,3712]{1,0:T(8,128)(2,1)S(1)}, bf16[64,3712]{1,0:T(8,128)(2,1)S(1)}, u32[]{:S(2)}, u32[]{:S(2)}) collective-permute-start(bf16[64,3712]{1,0:T(8,128)(2,1)S(1)} %fusion.8.refs_0_.refs_8_), channel_id=1, source_target_pairs={{0,32},{1,33},{2,34},{3,35},{4,36},{5,37},{6,38},{7,39},{8,40},{9,... | collective-permute-start | bytes 1425416 | tf_op jit(solution)/shard_map/ppermute | solution.py:39
  7.7 12.3 %collective-permute-start.6 = (bf16[64,3712]{1,0:T(8,128)(2,1)S(1)}, bf16[64,3712]{1,0:T(8,128)(2,1)S(1)}, u32[]{:S(2)}, u32[]{:S(2)}) collective-permute-start(bf16[64,3712]{1,0:T(8,128)(2,1)S(1)} %fusion.8.refs_0_.refs_8_), channel_id=1, source_target_pairs={{0,37},{1,36},{2,39},{3,38},{4,33},{5,32},{6,35},{7,34},{8,45},{9,... | collective-permute-start | bytes 1425416 | tf_op jit(solution)/shard_map/ppermute | solution.py:39
  11.3 13.7 %collective-permute-start.3 = (bf16[64,3712]{1,0:T(8,128)(2,1)S(1)}, bf16[64,3712]{1,0:T(8,128)(2,1)S(1)}, u32[]{:S(2)}, u32[]{:S(2)}) collective-permute-start(bf16[64,3712]{1,0:T(8,128)(2,1)S(1)} %collective-permute-done.1.refs_2_.refs_10_), channel_id=1, source_target_pairs={{0,32},{1,33},{2,34},{3,35},{4,36},{5,37},{6,38},{7,39},{8,40},{9,... | collective-permute-start | bytes 1425416 | tf_op jit(solution)/shard_map/ppermute | solution.py:39
  17.4 8.7 %collective-permute-start.4 = (bf16[64,3712]{1,0:T(8,128)(2,1)S(1)}, bf16[64,3712]{1,0:T(8,128)(2,1)S(1)}, u32[]{:S(2)}, u32[]{:S(2)}) collective-permute-start(bf16[64,3712]{1,0:T(8,128)(2,1)S(1)} %collective-permute-done.2.refs_3_.refs_11_), channel_id=1, source_target_pairs={{0,4},{1,5},{2,6},{3,7},{4,0},{5,1},{6,2},{7,3},{8,12},{9,13},{10,... | collective-permute-start | bytes 1425416 | tf_op jit(solution)/shard_map/ppermute | solution.py:39
  19.9 8.7 %collective-permute-start.5 = (bf16[64,3712]{1,0:T(8,128)(2,1)S(1)}, bf16[64,3712]{1,0:T(8,128)(2,1)S(1)}, u32[]{:S(2)}, u32[]{:S(2)}) collective-permute-start(bf16[64,3712]{1,0:T(8,128)(2,1)S(1)} %collective-permute-done.refs_1_.refs_9_), channel_id=1, source_target_pairs={{0,1},{1,0},{2,3},{3,2},{4,5},{5,4},{6,7},{7,6},{8,9},{9,8},{10,11... | collective-permute-start | bytes 1425416 | tf_op jit(solution)/shard_map/ppermute | solution.py:39
  32.0 10.0 %collective-permute-start.8 = (bf16[512,3584]{1,0:T(8,128)(2,1)}, bf16[512,3584]{1,0:T(8,128)(2,1)}, u32[]{:S(2)}, u32[]{:S(2)}) collective-permute-start(bf16[512,3584]{1,0:T(8,128)(2,1)} %get-tuple-element.8), channel_id=1, source_target_pairs={{0,16},{1,17},{2,18},{3,19},{4,20},{5,21},{6,22},{7,23},{8,24},{9,... | collective-permute-start | bytes 11010056 | tf_op jit(solution)/shard_map/ppermute | solution.py:43
  35.0 6.0 %collective-permute-start.7 = (bf16[512,128]{1,0:T(8,128)(2,1)S(1)}, bf16[512,128]{1,0:T(8,128)(2,1)S(1)}, u32[]{:S(2)}, u32[]{:S(2)}) collective-permute-start(bf16[512,128]{1,0:T(8,128)(2,1)S(1)} %get-tuple-element.7), channel_id=1, source_target_pairs={{0,16},{1,17},{2,18},{3,19},{4,20},{5,21},{6,22},{7,23},{8,24},{9,... | collective-permute-start | bytes 393224 | tf_op jit(solution)/shard_map/ppermute | solution.py:43
  48.1 32.8 %all-to-all-start = ((bf16[8,64,3584]{2,1,0:T(8,128)(2,1)}), bf16[8,64,3584]{2,1,0:T(8,128)(2,1)}, u32[]{:S(2)}, u32[]{:S(2)}) async-start(bf16[8,64,3584]{2,1,0:T(8,128)(2,1)} %bitcast.68), calls=%async_computation | async-start | bytes 7340032 | tf_op jit(solution)/shard_map/all_to_all | solution.py:58
  80.9 4.6 %copy-start.2 = (s32[64,8]{0,1:T(8,128)S(1)}, s32[64,8]{0,1:T(8,128)}, u32[]{:S(2)}) copy-start(s32[64,8]{0,1:T(8,128)} %param.8) | copy-start | bytes 6148
  80.9 34.2 %all-to-all-start.1 = ((bf16[8,64,3584]{2,1,0:T(8,128)(2,1)}), bf16[8,64,3584]{2,1,0:T(8,128)(2,1)}, u32[]{:S(2)}, u32[]{:S(2)}) async-start(bf16[8,64,3584]{2,1,0:T(8,128)(2,1)} %bitcast.67), calls=%async_computation.1 | async-start | bytes 7340032 | tf_op jit(solution)/shard_map/all_to_all | solution.py:58
  105.2 1.9 copy-start.1
  115.1 32.8 %all-to-all-start.2 = ((bf16[8,64,3584]{2,1,0:T(8,128)(2,1)}), bf16[8,64,3584]{2,1,0:T(8,128)(2,1)}, u32[]{:S(2)}, u32[]{:S(2)}) async-start(bf16[8,64,3584]{2,1,0:T(8,128)(2,1)} %bitcast.64), calls=%async_computation.2 | async-start | bytes 7340032 | tf_op jit(solution)/shard_map/all_to_all | solution.py:58
  139.3 1.9 copy-start
  153.8 32.4 %collective-permute-start.9 = (bf16[512,3584]{1,0:T(8,128)(2,1)}, bf16[512,3584]{1,0:T(8,128)(2,1)S(1)}, u32[]{:S(2)}, u32[]{:S(2)}) collective-permute-start(bf16[512,3584]{1,0:T(8,128)(2,1)} %follow.5), channel_id=1, source_target_pairs={{0,16},{1,17},{2,18},{3,19},{4,20},{5,21},{6,22},{7,23},{8,24},{9,... | collective-permute-start | bytes 11010056 | tf_op jit(solution)/shard_map/ppermute | solution.py:43
  188.6 8.6 %collective-permute-start.11 = (bf16[64,3584]{1,0:T(8,128)(2,1)S(1)}, bf16[64,3584]{1,0:T(8,128)(2,1)S(1)}, u32[]{:S(2)}, u32[]{:S(2)}) collective-permute-start(bf16[64,3584]{1,0:T(8,128)(2,1)S(1)} %get-tuple-element.12), channel_id=1, source_target_pairs={{0,1},{1,0},{2,3},{3,2},{4,5},{5,4},{6,7},{7,6},{8,9},{9,8},{10,11... | collective-permute-start | bytes 1376264 | tf_op jit(solution)/shard_map/ppermute | solution.py:39
  188.7 8.6 %collective-permute-start.13 = (bf16[64,3584]{1,0:T(8,128)(2,1)S(1)}, bf16[64,3584]{1,0:T(8,128)(2,1)S(1)}, u32[]{:S(2)}, u32[]{:S(2)}) collective-permute-start(bf16[64,3584]{1,0:T(8,128)(2,1)S(1)} %get-tuple-element.11), channel_id=1, source_target_pairs={{0,32},{1,33},{2,34},{3,35},{4,36},{5,37},{6,38},{7,39},{8,40},{9,... | collective-permute-start | bytes 1376264 | tf_op jit(solution)/shard_map/ppermute | solution.py:39
  188.8 8.6 %collective-permute-start.15 = (bf16[64,3584]{1,0:T(8,128)(2,1)S(1)}, bf16[64,3584]{1,0:T(8,128)(2,1)S(1)}, u32[]{:S(2)}, u32[]{:S(2)}) collective-permute-start(bf16[64,3584]{1,0:T(8,128)(2,1)S(1)} %get-tuple-element.10), channel_id=1, source_target_pairs={{0,4},{1,5},{2,6},{3,7},{4,0},{5,1},{6,2},{7,3},{8,12},{9,13},{10,... | collective-permute-start | bytes 1376264 | tf_op jit(solution)/shard_map/ppermute | solution.py:39
  188.9 16.3 %collective-permute-start.10 = (bf16[64,3584]{1,0:T(8,128)(2,1)S(1)}, bf16[64,3584]{1,0:T(8,128)(2,1)S(1)}, u32[]{:S(2)}, u32[]{:S(2)}) collective-permute-start(bf16[64,3584]{1,0:T(8,128)(2,1)S(1)} %get-tuple-element.9), channel_id=1, source_target_pairs={{0,37},{1,36},{2,39},{3,38},{4,33},{5,32},{6,35},{7,34},{8,45},{9,... | collective-permute-start | bytes 1376264 | tf_op jit(solution)/shard_map/ppermute | solution.py:39
  197.7 10.9 %collective-permute-start.12 = (bf16[64,3584]{1,0:T(8,128)(2,1)S(1)}, bf16[64,3584]{1,0:T(8,128)(2,1)S(1)}, u32[]{:S(2)}, u32[]{:S(2)}) collective-permute-start(bf16[64,3584]{1,0:T(8,128)(2,1)S(1)} %get-tuple-element.13), channel_id=1, source_target_pairs={{0,32},{1,33},{2,34},{3,35},{4,36},{5,37},{6,38},{7,39},{8,40},{9,... | collective-permute-start | bytes 1376264 | tf_op jit(solution)/shard_map/ppermute | solution.py:39
  199.7 8.9 %collective-permute-start.14 = (bf16[64,3584]{1,0:T(8,128)(2,1)S(1)}, bf16[64,3584]{1,0:T(8,128)(2,1)S(1)}, u32[]{:S(2)}, u32[]{:S(2)}) collective-permute-start(bf16[64,3584]{1,0:T(8,128)(2,1)S(1)} %get-tuple-element.15), channel_id=1, source_target_pairs={{0,4},{1,5},{2,6},{3,7},{4,0},{5,1},{6,2},{7,3},{8,12},{9,13},{10,... | collective-permute-start | bytes 1376264 | tf_op jit(solution)/shard_map/ppermute | solution.py:39
  199.7 10.3 %collective-permute-start.16 = (bf16[64,3584]{1,0:T(8,128)(2,1)S(1)}, bf16[64,3584]{1,0:T(8,128)(2,1)S(1)}, u32[]{:S(2)}, u32[]{:S(2)}) collective-permute-start(bf16[64,3584]{1,0:T(8,128)(2,1)S(1)} %get-tuple-element.14), channel_id=1, source_target_pairs={{0,1},{1,0},{2,3},{3,2},{4,5},{5,4},{6,7},{7,6},{8,9},{9,8},{10,11... | collective-permute-start | bytes 1376264 | tf_op jit(solution)/shard_map/ppermute | solution.py:39

commit v4 on v3

--- a/solution.py
+++ b/solution.py
@@ -82,39 +82,78 @@
     return add(own, last, *[to_corner(b, corner) for b, corner in zip((y, x, z), NEAR[1:])])
 
 
-def stack_kernel(count, *refs):
-    size = refs[0].shape[0]
-    rows_ref, about_ref = refs[2 * count :]
-    for i in range(count):
-        rows_ref[i * size : (i + 1) * size] = refs[i][...]
+def select_kernel(count, tok, top, *refs):
+    wanted_ref, earlier_ref = refs[:2]
+    blocks, labels, outs, chosen = refs[2 : 2 + count], refs[2 + count : 2 + 2 * count], refs[2 + 2 * count : -1], refs[-1]
+    members = wanted_ref.shape[0]
+    cap = chosen.shape[0] // members**2
+
+    def whole(parts):
+        parts = [part[...] for part in parts]
+        return parts[0] if len(parts) == 1 else jnp.concatenate(parts, axis=0)
 
     @pl.when(pl.program_id(0) == 0)
     def _():
-        for i in range(count):
-            about_ref[i * size : (i + 1) * size] = refs[count + i][...]
-
-
-def stack(blocks, width):
-    count, size = len(blocks), blocks[0].shape[0]
-    rest = blocks[0].shape[1] - width
+        known = whole(labels)
+        if len(outs) > 1:
+            outs[2][...] = known
+        known = known.astype(jnp.float32).T
+        held = known.shape[1]
+        wanted = wanted_ref[...]
+        named = jnp.zeros((members, held), jnp.float32)
+        for k in range(top):
+            named = jnp.where(wanted == known[k : k + 1], jnp.float32(1.0), named)
+        slot = jnp.dot(named.astype(chosen.dtype), earlier_ref[...], preferred_element_type=jnp.float32)
+        slot = jnp.where(named > 0.0, slot, jnp.float32(-1.0))
+        rank = lax.broadcasted_iota(jnp.int32, (cap, held), 0).astype(jnp.float32)
+        lane = lax.broadcasted_iota(jnp.int32, (cap, held), 1)
+        for member in range(members):
+            same = jnp.where(slot[member : member + 1] == rank, jnp.float32(1.0), jnp.float32(0.0))
+            for source in range(0, members, 2):
+                pair = [
+                    jnp.where((lane >= i * tok) & (lane < (i + 1) * tok), same, jnp.float32(0.0))
+                    for i in (source, source + 1)
+                ]
+                first = (member * members + source) * cap
+                chosen[first : first + 2 * cap] = jnp.concatenate(pair, axis=0).astype(chosen.dtype)
+
+    rows = whole(blocks)
+    if len(outs) > 1:
+        outs[1][...] = rows
+    picked = jnp.dot(chosen[...], rows, preferred_element_type=jnp.float32)
+    outs[0][...] = picked.astype(outs[0].dtype)
+
+
+def select(wanted, earlier, blocks, labels, place, tok, top, width, keep):
+    held = earlier.shape[0]
+    members = wanted.shape[0]
+    cap = 2 * tok * top // (CORES * RING**3)
+    count = members * members * cap
+    wide = 896
     dtype = blocks[0].dtype
-    wide = 896
+    rows = jax.ShapeDtypeStruct((count, width), dtype)
+    outs = [(rows, pl.BlockSpec((count, wide), lambda i: (0, i)))]
+    if keep:
+        outs.append((jax.ShapeDtypeStruct((held, width), dtype), pl.BlockSpec((held, wide), lambda i: (0, i))))
+        outs.append((jax.ShapeDtypeStruct((held, LANES), dtype), pl.BlockSpec((held, LANES), lambda i: (0, 0))))
     return pl.pallas_call(
-        functools.partial(stack_kernel, count),
+        functools.partial(select_kernel, len(blocks), tok, top),
         grid=(width // wide,),
-        in_specs=[pl.BlockSpec((size, wide), lambda i: (0, i))] * count
-        + [pl.BlockSpec((size, rest), lambda i: (0, width // rest))] * count,
-        out_specs=[
-            pl.BlockSpec((count * size, wide), lambda i: (0, i)),
-            pl.BlockSpec((count * size, rest), lambda i: (0, 0)),
-        ],
-        out_shape=[
-            jax.ShapeDtypeStruct((count * size, width), dtype),
-            jax.ShapeDtypeStruct((count * size, rest), dtype),
-        ],
-        compiler_params=pltpu.CompilerParams(vmem_limit_bytes=32 * 2**20),
-        name="stack",
-    )(*blocks, *blocks)
+        in_specs=[
+            pl.BlockSpec(wanted.shape, lambda i: (0, 0)),
+            pl.BlockSpec(earlier.shape, lambda i: (0, 0)),
+        ]
+        + [pl.BlockSpec((block.shape[0], wide), lambda i: (0, i)) for block in blocks]
+        + [pl.BlockSpec((label.shape[0], LANES), lambda i: (0, place)) for label in labels],
+        out_specs=[spec for _, spec in outs],
+        out_shape=[shape for shape, _ in outs],
+        scratch_shapes=[pltpu.VMEM((count, held), dtype)],
+        compiler_params=pltpu.CompilerParams(vmem_limit_bytes=40 * 2**20),
+        cost_estimate=pl.CostEstimate(
+            flops=2 * count * held * width, bytes_accessed=6 * count * width, transcendentals=0
+        ),
+        name="select",
+    )(wanted, earlier, *blocks, *labels)
 
 
 def follow_kernel(value_ref, after_ref, out_ref):
@@ -132,8 +171,8 @@
     )(value, after)
 
 
-def expert_kernel(inner, tile, after_ref, rows_ref, gate_ref, up_ref, down_ref, out_ref, hidden):
-    del after_ref
+def expert_kernel(inner, tile, rows_ref, gate_ref, up_ref, down_ref, *refs):
+    out_ref, hidden = refs[-2:]
     step = pl.program_id(0)
 
     @pl.when(step < inner)
@@ -166,12 +205,12 @@
         functools.partial(expert_kernel, inner, tile),
         grid=(inner + outer,),
         in_specs=[
-            pl.BlockSpec(memory_space=pl.ANY),
             pl.BlockSpec((count, width), lambda i: (0, 0)),
             pl.BlockSpec((width, tile), of_inner),
             pl.BlockSpec((width, tile), of_inner),
             pl.BlockSpec((hidden, wide), of_outer),
-        ],
+        ]
+        + [pl.BlockSpec(memory_space=pl.ANY)] * len(after),
         out_specs=pl.BlockSpec((count, wide), of_outer),
         out_shape=jax.ShapeDtypeStruct((count, width), rows.dtype),
         scratch_shapes=[pltpu.VMEM((count, hidden), rows.dtype)],
@@ -182,7 +221,7 @@
             transcendentals=count * hidden,
         ),
         name="expert",
-    )(after, rows, gate, up, down)
+    )(rows, gate, up, down, *after)
 
 
 def shards(tokens, expert_ids, gate_values, expert_gate, expert_up, expert_down):
@@ -199,9 +238,7 @@
 
     about = jnp.concatenate([expert_ids.astype(jnp.bfloat16), gate_values], axis=1)
     about = jnp.pad(about, ((0, 0), (0, LANES - 2 * top)))
-    own_held, own_known = stack(gather_cube(jnp.concatenate([tokens, about], axis=1)), width)
-    other_held = to_other_core(own_held)
-    other_known = to_other_core(own_known)
+    blocks = gather_cube(jnp.concatenate([tokens, about], axis=1))
 
     bits = jnp.array(CORNERS, dtype=jnp.int32)
     source = jnp.repeat(jnp.arange(corners, dtype=jnp.int32), tok)
@@ -210,12 +247,14 @@
     earlier = (order[:, None] < order[None, :]) & (source[:, None] == source[None, :])
     earlier = earlier.astype(jnp.bfloat16)
 
-    def selection(known, flip):
+    def experts_for(flip):
         side = core ^ flip
         step = jnp.where(side == 0, EXCHANGE[0], EXCHANGE[1])
         base = [jnp.where(side == 0, jnp.where(v < 2, v, v ^ 3), v & 2) for v in at]
         spot = [base[i] ^ (bits[:, i] * step) for i in range(3)]
-        wanted = index_of(spot[0], core, spot[1], spot[2])[:, None].astype(jnp.float32)
+        return index_of(spot[0], core, spot[1], spot[2])[:, None].astype(jnp.float32)
+
+    def weights_of(wanted, known):
         known = known.astype(jnp.float32).T[: 2 * top].reshape(2, top, held)
         named = jnp.zeros((corners, held), jnp.float32)
         weight = named
@@ -227,35 +266,38 @@
         slot = jnp.where(named > 0.0, slot, jnp.float32(-1.0))
         chosen = slot[:, None, :] == jnp.arange(cap, dtype=jnp.float32)[None, :, None]
         weights = jnp.where(chosen, weight[:, None, :], jnp.float32(0.0))
-        wide = []
-        for small in (chosen.astype(jnp.float32), weights):
-            small = jnp.where(mask[None], small[:, None], jnp.float32(0.0)).astype(jnp.bfloat16)
-            wide.append(small.reshape(corners * corners * cap, held))
-        return wide
+        weights = jnp.where(mask[None], weights[:, None], jnp.float32(0.0)).astype(jnp.bfloat16)
+        return weights.reshape(corners * corners * cap, held)
 
     flat = (corners * corners * cap, width)
     boxed = (corners, corners * cap, width)
     experts_of = (expert_gate[0], expert_up[0], expert_down[0])
 
-    def send(held, known, flip):
-        chosen, weights = selection(known, flip)
-        picked = jnp.dot(chosen, held, preferred_element_type=jnp.float32).astype(jnp.bfloat16)
-        return exchange(picked.reshape(boxed), flip).reshape(flat), weights
-
     def collect(back, weights):
         total = lax.dot_general(weights, back, (((0,), (0,)), ((), ())), preferred_element_type=jnp.float32)
         return total.astype(jnp.bfloat16)
 
-    other_rows, other_weights = send(other_held, other_known, 1)
-    own_rows, own_weights = send(own_held, own_known, 0)
-    other_out = follow(expert(other_rows, *experts_of, expert_ids), own_rows)
+    own_experts, other_experts = experts_for(0), experts_for(1)
+    own_picked, own_held, own_known = select(
+        own_experts, earlier, blocks, blocks, width // LANES, tok, top, width, True
+    )
+    own_rows = exchange(own_picked.reshape(boxed), 0).reshape(flat)
+    other_held, other_known = to_other_core(own_held), to_other_core(own_known)
+    other_picked = select(other_experts, earlier, [other_held], [other_known], 0, tok, top, width, False)[0]
+    other_rows = exchange(other_picked.reshape(boxed), 1).reshape(flat)
+    own_weights = weights_of(own_experts, own_known)
+    other_weights = weights_of(other_experts, other_known)
+    own_out = follow(expert(own_rows, *experts_of, [own_weights, other_weights]), other_rows)
+    own_back = exchange(own_out.reshape(boxed), 0).reshape(flat)
+    other_out = follow(expert(other_rows, *experts_of, [own_out]), own_back)
     other_back = exchange(other_out.reshape(boxed), 1).reshape(flat)
-    own_out = follow(expert(own_rows, *experts_of, other_out), other_back)
-    own_back = exchange(own_out.reshape(boxed), 0).reshape(flat)
-    other_total = to_other_core(follow(collect(other_back, other_weights), own_out))
     own_total = collect(own_back, own_weights)
-    total = add(own_total, other_total)
-    return reduce_cube([total[i * tok : (i + 1) * tok] for i in range(corners)])
+    half = held // 2
+    far = to_other_core(collect(other_back, other_weights[:, half:]))
+    near = to_other_core(collect(other_back, other_weights[:, :half]))
+    total = [add(own_total[i * tok : (i + 1) * tok], near[i * tok : (i + 1) * tok]) for i in range(corners // 2)]
+    total += [add(own_total[half + i * tok :][:tok], far[i * tok : (i + 1) * tok]) for i in range(corners // 2)]
+    return reduce_cube(total)
 
 
 def solution(mesh):

time: 212 us -> 207 us (0.976)
  matrix products: 20.7 us -> 7.06 us
  Pallas kernels: 42.6 us -> 50.5 us
  waiting for transfers between devices: 73.4 us -> 69.8 us
  blocking collectives: 32.4 us -> 28.8 us
  local copies, waits for them, and re-layouts: 4.47 us -> 7.94 us
    dot_general x4 -> x2, matrix products: 12.6 us -> 0.66 us  [weights_of(): jnp.dot(named.astype(jnp.bfloat16), earlier, preferred_element_type=jnp.f...]
    pallas_call x1 -> x2, Pallas kernels: 3.49 us -> 11.4 us  [select(): pl.pallas_call(functools.partial(select_kernel, len(blocks), tok, top), g...]
    ppermute x3 -> x4, waiting for transfers between devices: 5.29 us -> 1.22 us  [to_other_core(): lax.ppermute(value, BOTH, [(index_of(y, c, x, z), index_of(y, 1 - c, x, z...]
    all_to_all x1, blocking collectives: 32.4 us -> 28.8 us  [exchange(): lax.all_to_all(value, BOTH, split_axis=0, concat_axis=0, axis_index_group...]
    unnamed x13 -> x14, local copies, waits for them, and re-layouts: 3.89 us -> 7.51 us
    ppermute x14, waiting for transfers between devices: 31.1 us -> 33.8 us  [to_corner(): lax.ppermute(value, BOTH, [(index_of(*p), moved(p, corner, GATHER[p[1]]))...]
    all_to_all x3, waiting for transfers between devices: 37 us -> 34.8 us  [exchange(): lax.all_to_all(value, BOTH, split_axis=0, concat_axis=0, axis_index_group...]
    dot_general x2 -> x3, matrix products: 8.08 us -> 6.4 us  [collect(): lax.dot_general(weights, back, (((0,), (0,)), ((), ())), preferred_elemen...]
  transfers between devices with their start and end apart: 20 -> 21, of which waited for: 16 -> 16; matrix products, arithmetic and copies ran while one was open for 4% -> 4% of each run, Pallas kernels for 19% -> 22%
where the time goes in v4:
time: 207 us; the launch traced here: 205 us
  waiting for transfers between devices  69.8 us (34%)
  Pallas kernels  50.5 us (24%)
  starting transfers between devices  34.3 us (17%)
  blocking collectives  28.8 us (14%)
  local copies, waits for them, and re-layouts  7.94 us (4%)
  matrix products  7.06 us (3%)
  other arithmetic  6.09 us (3%)
    pallas_call x2, Pallas kernels, expert(): pl.pallas_call(functools.partial(expert_kernel, inner, tile), grid=(inner...  39.1 us
    all_to_all x3, waiting for transfers between devices, exchange(): lax.all_to_all(value, BOTH, split_axis=0, concat_axis=0, axis_index_group...  34.8 us
    ppermute x14, waiting for transfers between devices, to_corner(): lax.ppermute(value, BOTH, [(index_of(*p), moved(p, corner, GATHER[p[1]]))...  33.8 us
    all_to_all x1, blocking collectives, exchange(): lax.all_to_all(value, BOTH, split_axis=0, concat_axis=0, axis_index_group...  28.8 us
    ppermute x14, starting transfers between devices, to_corner(): lax.ppermute(value, BOTH, [(index_of(*p), moved(p, corner, GATHER[p[1]]))...  16.4 us
    all_to_all x3, starting transfers between devices, exchange(): lax.all_to_all(value, BOTH, split_axis=0, concat_axis=0, axis_index_group...  14.5 us
    pallas_call x2, Pallas kernels, select(): pl.pallas_call(functools.partial(select_kernel, len(blocks), tok, top), g...  11.4 us
    unnamed x14, local copies, waits for them, and re-layouts  7.51 us
  transfers between devices with their start and end apart: 21, of which 16 were waited for; matrix products, arithmetic and copies ran while one was open for 4% of the time, Pallas kernels for 22%

profile of v4, /device:TPU:0, one launch (start us, length us, event | category | flops | bytes accessed | tf_op | source)
XLA Modules:
  0.0 204.8 jit_solution(16860545840023425523)
XLA Ops:
  2.5 2.1 %collective-permute-start.2 = (bf16[64,3712]{1,0:T(8,128)(2,1)S(1)}, bf16[64,3712]{1,0:T(8,128)(2,1)S(1)}, u32[]{:S(2)}, u32[]{:S(2)}) collective-permute-start(bf16[64,3712]{1,0:T(8,128)(2,1)S(1)} %fusion.9.refs_2_.refs_10_), channel_id=1, source_target_pairs={{0,1},{1,0},{2,3},{3,2},{4,5},{5,4},{6,7},{7,6},{8,9},{9,8},{10,11... | collective-permute-start | bytes 1425416 | tf_op jit(solution)/shard_map/ppermute | solution.py:39
  4.6 1.5 collective-permute-start.1
  6.1 1.6 collective-permute-start
  7.7 3.6 %collective-permute-done.2.refs_5_.refs_13_ = bf16[64,3712]{1,0:T(8,128)(2,1)S(1)} collective-permute-done((bf16[64,3712]{1,0:T(8,128)(2,1)S(1)}, bf16[64,3712]{1,0:T(8,128)(2,1)S(1)}, u32[]{:S(2)}, u32[]{:S(2)}) %collective-permute-start.2) | collective-permute-done | bytes 475168 | tf_op jit(solution)/shard_map/ppermute | solution.py:39
  11.3 1.6 collective-permute-start.4
  13.3 1.6 collective-permute-start.3
  14.8 5.0 %collective-permute-done.refs_3_.refs_11_ = bf16[64,3712]{1,0:T(8,128)(2,1)S(1)} collective-permute-done((bf16[64,3712]{1,0:T(8,128)(2,1)S(1)}, bf16[64,3712]{1,0:T(8,128)(2,1)S(1)}, u32[]{:S(2)}, u32[]{:S(2)}) %collective-permute-start) | collective-permute-done | bytes 475168 | tf_op jit(solution)/shard_map/ppermute | solution.py:39
  21.0 2.5 %collective-permute-done.4.refs_7_.refs_15_ = bf16[64,3712]{1,0:T(8,128)(2,1)S(1)} collective-permute-done((bf16[64,3712]{1,0:T(8,128)(2,1)S(1)}, bf16[64,3712]{1,0:T(8,128)(2,1)S(1)}, u32[]{:S(2)}, u32[]{:S(2)}) %collective-permute-start.4) | collective-permute-done | bytes 475168 | tf_op jit(solution)/shard_map/ppermute | solution.py:39
  23.5 1.5 collective-permute-done.3.refs_6_.refs_14_
  25.1 3.6 %collective-permute-done.5.refs_8_.refs_16_ = bf16[64,3712]{1,0:T(8,128)(2,1)} collective-permute-done((bf16[64,3712]{1,0:T(8,128)(2,1)S(1)}, bf16[64,3712]{1,0:T(8,128)(2,1)}, u32[]{:S(2)}, u32[]{:S(2)}) %collective-permute-start.5) | collective-permute-done | bytes 475168 | tf_op jit(solution)/shard_map/ppermute | solution.py:39
  28.6 6.3 %select.19 = (bf16[512,3584]{1,0:T(8,128)(2,1)S(1)}, bf16[512,3584]{1,0:T(8,128)(2,1)}, bf16[512,128]{1,0:T(8,128)(2,1)S(1)}) custom-call(f32[8,1]{1,0:T(8,128)S(1)} %get-tuple-element.52.refs_0_, bf16[512,512]{1,0:T(8,128)(2,1)S(1)} %fusion.4.refs_1_, bf16[64,3712]{1,0:T(8,128)(2,1)S(1)} %fusion.9.refs_2_.refs_10_, ...), custom_call_target="tpu_custom_call" | custom-call | flops 1879048192 | bytes 11010048 | tf_op jit(solution)/shard_map/select/pallas_call | solution.py:139
  34.9 1.9 copy-done.3
  36.9 2.4 %collective-permute-start.8 = (bf16[512,3584]{1,0:T(8,128)(2,1)}, bf16[512,3584]{1,0:T(8,128)(2,1)}, u32[]{:S(2)}, u32[]{:S(2)}) collective-permute-start(bf16[512,3584]{1,0:T(8,128)(2,1)} %get-tuple-element.10), channel_id=1, source_target_pairs={{0,16},{1,17},{2,18},{3,19},{4,20},{5,21},{6,22},{7,23},{8,24},{9,... | collective-permute-start | bytes 11010056 | tf_op jit(solution)/shard_map/ppermute | solution.py:43
  39.3 5.5 %all-to-all-start = ((bf16[8,64,3584]{2,1,0:T(8,128)(2,1)}), bf16[8,64,3584]{2,1,0:T(8,128)(2,1)}, u32[]{:S(2)}, u32[]{:S(2)}) async-start(bf16[8,64,3584]{2,1,0:T(8,128)(2,1)} %bitcast.56), calls=%async_computation | async-start | bytes 7340032 | tf_op jit(solution)/shard_map/all_to_all | solution.py:58
  46.4 5.0 %select.20 = bf16[512,3584]{1,0:T(8,128)(2,1)S(1)} custom-call(f32[8,1]{1,0:T(8,128)S(1)} %get-tuple-element.53.refs_0_, bf16[512,512]{1,0:T(8,128)(2,1)S(1)} %fusion.4.refs_1_, bf16[512,3584]{1,0:T(8,128)(2,1)} %collective-permute-done.8.refs_2_, bf16[512,128]{1,0:T(8,128)(2,1)S(1)} %collective-permute-done.7.refs_3_), custom_call_target="tpu_custom_call" | custom-call | flops 1879048192 | bytes 11010048 | tf_op jit(solution)/shard_map/select/pallas_call | solution.py:139
  51.5 1.9 copy-done
  53.4 21.1 %all-to-all-done = bf16[8,64,3584]{2,1,0:T(8,128)(2,1)} async-done(((bf16[8,64,3584]{2,1,0:T(8,128)(2,1)}), bf16[8,64,3584]{2,1,0:T(8,128)(2,1)}, u32[]{:S(2)}, u32[]{:S(2)}) %all-to-all-start) | async-done | bytes 3670048 | tf_op jit(solution)/shard_map/all_to_all | solution.py:58
  74.5 4.5 %all-to-all-start.1 = ((bf16[8,64,3584]{2,1,0:T(8,128)(2,1)}), bf16[8,64,3584]{2,1,0:T(8,128)(2,1)}, u32[]{:S(2)}, u32[]{:S(2)}) async-start(bf16[8,64,3584]{2,1,0:T(8,128)(2,1)} %bitcast.53), calls=%async_computation.1 | async-start | bytes 7340032 | tf_op jit(solution)/shard_map/all_to_all | solution.py:58
  80.2 19.6 %expert.2.value_ref = bf16[512,3584]{1,0:T(8,128)(2,1)S(1)} custom-call(bf16[512,3584]{1,0:T(8,128)(2,1)} %bitcast.20.rows_ref, bf16[3584,1024]{1,0:T(8,128)(2,1)} %bitcast.116, bf16[3584,1024]{1,0:T(8,128)(2,1)} %bitcast.118, bf16[1024,3584]{1,0:T(8,128)(2,1)} %bitcast.120, bf16[512,512]{1,0:T(8,128)(2,1)S(1)} %bitcast.60, bf16[512,512]{1,0:T(8,128)(2,1)S(1)} %bitcast.57), custom_call_target="tpu_custom_call" | custom-call | flops 11274289152 | bytes 29360128 | tf_op jit(solution)/shard_map/expert/pallas_call | solution.py:204
  99.8 1.9 copy-done.1
  101.8 5.5 %all-to-all-done.1 = bf16[8,64,3584]{2,1,0:T(8,128)(2,1)} async-done(((bf16[8,64,3584]{2,1,0:T(8,128)(2,1)}), bf16[8,64,3584]{2,1,0:T(8,128)(2,1)}, u32[]{:S(2)}, u32[]{:S(2)}) %all-to-all-start.1) | async-done | bytes 3670048 | tf_op jit(solution)/shard_map/all_to_all | solution.py:58
  107.3 4.5 %all-to-all-start.2 = ((bf16[8,64,3584]{2,1,0:T(8,128)(2,1)}), bf16[8,64,3584]{2,1,0:T(8,128)(2,1)}, u32[]{:S(2)}, u32[]{:S(2)}) async-start(bf16[8,64,3584]{2,1,0:T(8,128)(2,1)} %bitcast.54), calls=%async_computation.2 | async-start | bytes 7340032 | tf_op jit(solution)/shard_map/all_to_all | solution.py:58
  111.8 19.6 %expert.3.value_ref = bf16[512,3584]{1,0:T(8,128)(2,1)S(1)} custom-call(bf16[512,3584]{1,0:T(8,128)(2,1)} %bitcast.44.after_ref.rows_ref, bf16[3584,1024]{1,0:T(8,128)(2,1)} %bitcast.117, bf16[3584,1024]{1,0:T(8,128)(2,1)} %bitcast.119, bf16[1024,3584]{1,0:T(8,128)(2,1)} %bitcast.121, bf16[512,3584]{1,0:T(8,128)(2,1)} %follow.2.refs_0_), custom_call_target="tpu_custom_call" | custom-call | flops 11274289152 | bytes 29360128 | tf_op jit(solution)/shard_map/expert/pallas_call | solution.py:204
  131.4 1.8 copy-done.2
  133.1 8.2 %all-to-all-done.2 = bf16[8,64,3584]{2,1,0:T(8,128)(2,1)} async-done(((bf16[8,64,3584]{2,1,0:T(8,128)(2,1)}), bf16[8,64,3584]{2,1,0:T(8,128)(2,1)}, u32[]{:S(2)}, u32[]{:S(2)}) %all-to-all-start.2) | async-done | bytes 3670048 | tf_op jit(solution)/shard_map/all_to_all | solution.py:58
  141.3 28.8 %all_to_all.20 = bf16[8,64,3584]{2,1,0:T(8,128)(2,1)S(1)} all-to-all(bf16[8,64,3584]{2,1,0:T(8,128)(2,1)} %bitcast.55), channel_id=1, replica_groups={{0,1,4,5,32,33,36,37},{2,3,6,7,34,35,38,39},{8,9,12,13,40,41,44,45},{10..., dimensions={0} | all-to-all | bytes 7340032 | tf_op jit(solution)/shard_map/all_to_all | solution.py:58
  173.3 4.1 %convolution_convert_fusion = bf16[512,3584]{1,0:T(8,128)(2,1)S(1)} fusion(bf16[512,512]{1,0:T(8,128)(2,1)S(1)} %bitcast.61, bf16[512,3584]{1,0:T(8,128)(2,1)} %bitcast.46.after_ref), kind=kOutput, calls=%fused_computation | convolution fusion | flops 1880883200 | bytes 7864320 | tf_op jit(solution)/shard_map/dot_general | solution.py:277
  179.6 3.3 %collective-permute-start.11 = (bf16[64,3584]{1,0:T(8,128)(2,1)S(1)}, bf16[64,3584]{1,0:T(8,128)(2,1)S(1)}, u32[]{:S(2)}, u32[]{:S(2)}) collective-permute-start(bf16[64,3584]{1,0:T(8,128)(2,1)S(1)} %get-tuple-element.13), channel_id=1, source_target_pairs={{0,37},{1,36},{2,39},{3,38},{4,33},{5,32},{6,35},{7,34},{8,45},{9,... | collective-permute-start | bytes 1376264 | tf_op jit(solution)/shard_map/ppermute | solution.py:39
  182.9 3.5 %collective-permute-done.16 = bf16[64,3584]{1,0:T(8,128)(2,1)S(1)} collective-permute-done((bf16[64,3584]{1,0:T(8,128)(2,1)S(1)}, bf16[64,3584]{1,0:T(8,128)(2,1)S(1)}, u32[]{:S(2)}, u32[]{:S(2)}) %collective-permute-start.16) | collective-permute-done | bytes 458784 | tf_op jit(solution)/shard_map/ppermute | solution.py:39
  186.4 5.3 %collective-permute-done.14 = bf16[64,3584]{1,0:T(8,128)(2,1)S(1)} collective-permute-done((bf16[64,3584]{1,0:T(8,128)(2,1)S(1)}, bf16[64,3584]{1,0:T(8,128)(2,1)S(1)}, u32[]{:S(2)}, u32[]{:S(2)}) %collective-permute-start.14) | collective-permute-done | bytes 458784 | tf_op jit(solution)/shard_map/ppermute | solution.py:39
  193.0 1.3 collective-permute-start.13
  196.0 5.6 %collective-permute-done.13 = bf16[64,3584]{1,0:T(8,128)(2,1)S(1)} collective-permute-done((bf16[64,3584]{1,0:T(8,128)(2,1)S(1)}, bf16[64,3584]{1,0:T(8,128)(2,1)S(1)}, u32[]{:S(2)}, u32[]{:S(2)}) %collective-permute-start.13) | collective-permute-done | bytes 458784 | tf_op jit(solution)/shard_map/ppermute | solution.py:39
  (60 shorter events, 18.4 us)
Async XLA Ops:
  2.5 8.7 %collective-permute-start.2 = (bf16[64,3712]{1,0:T(8,128)(2,1)S(1)}, bf16[64,3712]{1,0:T(8,128)(2,1)S(1)}, u32[]{:S(2)}, u32[]{:S(2)}) collective-permute-start(bf16[64,3712]{1,0:T(8,128)(2,1)S(1)} %fusion.9.refs_2_.refs_10_), channel_id=1, source_target_pairs={{0,1},{1,0},{2,3},{3,2},{4,5},{5,4},{6,7},{7,6},{8,9},{9,8},{10,11... | collective-permute-start | bytes 1425416 | tf_op jit(solution)/shard_map/ppermute | solution.py:39
  4.6 8.7 %collective-permute-start.1 = (bf16[64,3712]{1,0:T(8,128)(2,1)S(1)}, bf16[64,3712]{1,0:T(8,128)(2,1)S(1)}, u32[]{:S(2)}, u32[]{:S(2)}) collective-permute-start(bf16[64,3712]{1,0:T(8,128)(2,1)S(1)} %fusion.9.refs_2_.refs_10_), channel_id=1, source_target_pairs={{0,4},{1,5},{2,6},{3,7},{4,0},{5,1},{6,2},{7,3},{8,12},{9,13},{10,... | collective-permute-start | bytes 1425416 | tf_op jit(solution)/shard_map/ppermute | solution.py:39
  6.1 13.7 %collective-permute-start = (bf16[64,3712]{1,0:T(8,128)(2,1)S(1)}, bf16[64,3712]{1,0:T(8,128)(2,1)S(1)}, u32[]{:S(2)}, u32[]{:S(2)}) collective-permute-start(bf16[64,3712]{1,0:T(8,128)(2,1)S(1)} %fusion.9.refs_2_.refs_10_), channel_id=1, source_target_pairs={{0,32},{1,33},{2,34},{3,35},{4,36},{5,37},{6,38},{7,39},{8,40},{9,... | collective-permute-start | bytes 1425416 | tf_op jit(solution)/shard_map/ppermute | solution.py:39
  7.7 13.3 %collective-permute-start.6 = (bf16[64,3712]{1,0:T(8,128)(2,1)S(1)}, bf16[64,3712]{1,0:T(8,128)(2,1)S(1)}, u32[]{:S(2)}, u32[]{:S(2)}) collective-permute-start(bf16[64,3712]{1,0:T(8,128)(2,1)S(1)} %fusion.9.refs_2_.refs_10_), channel_id=1, source_target_pairs={{0,37},{1,36},{2,39},{3,38},{4,33},{5,32},{6,35},{7,34},{8,45},{9,... | collective-permute-start | bytes 1425416 | tf_op jit(solution)/shard_map/ppermute | solution.py:39
  11.3 12.2 %collective-permute-start.4 = (bf16[64,3712]{1,0:T(8,128)(2,1)S(1)}, bf16[64,3712]{1,0:T(8,128)(2,1)S(1)}, u32[]{:S(2)}, u32[]{:S(2)}) collective-permute-start(bf16[64,3712]{1,0:T(8,128)(2,1)S(1)} %collective-permute-done.2.refs_5_.refs_13_), channel_id=1, source_target_pairs={{0,4},{1,5},{2,6},{3,7},{4,0},{5,1},{6,2},{7,3},{8,12},{9,13},{10,... | collective-permute-start | bytes 1425416 | tf_op jit(solution)/shard_map/ppermute | solution.py:39
  13.3 11.8 %collective-permute-start.3 = (bf16[64,3712]{1,0:T(8,128)(2,1)S(1)}, bf16[64,3712]{1,0:T(8,128)(2,1)}, u32[]{:S(2)}, u32[]{:S(2)}) collective-permute-start(bf16[64,3712]{1,0:T(8,128)(2,1)S(1)} %collective-permute-done.1.refs_4_.refs_12_), channel_id=1, source_target_pairs={{0,32},{1,33},{2,34},{3,35},{4,36},{5,37},{6,38},{7,39},{8,40},{9,... | collective-permute-start | bytes 1425416 | tf_op jit(solution)/shard_map/ppermute | solution.py:39
  19.9 8.8 %collective-permute-start.5 = (bf16[64,3712]{1,0:T(8,128)(2,1)S(1)}, bf16[64,3712]{1,0:T(8,128)(2,1)}, u32[]{:S(2)}, u32[]{:S(2)}) collective-permute-start(bf16[64,3712]{1,0:T(8,128)(2,1)S(1)} %collective-permute-done.refs_3_.refs_11_), channel_id=1, source_target_pairs={{0,1},{1,0},{2,3},{3,2},{4,5},{5,4},{6,7},{7,6},{8,9},{9,8},{10,11... | collective-permute-start | bytes 1425416 | tf_op jit(solution)/shard_map/ppermute | solution.py:39
  34.9 1.9 copy-start.3
  36.9 9.6 %collective-permute-start.8 = (bf16[512,3584]{1,0:T(8,128)(2,1)}, bf16[512,3584]{1,0:T(8,128)(2,1)}, u32[]{:S(2)}, u32[]{:S(2)}) collective-permute-start(bf16[512,3584]{1,0:T(8,128)(2,1)} %get-tuple-element.10), channel_id=1, source_target_pairs={{0,16},{1,17},{2,18},{3,19},{4,20},{5,21},{6,22},{7,23},{8,24},{9,... | collective-permute-start | bytes 11010056 | tf_op jit(solution)/shard_map/ppermute | solution.py:43
  39.3 5.5 %copy-start.4 = (s32[8,1]{1,0:T(8,128)S(1)}, s32[8,1]{1,0:T(8,128)}, u32[]{:S(2)}) copy-start(s32[8,1]{1,0:T(8,128)} %constant.78) | copy-start | bytes 100
  39.3 5.5 %copy-start.5 = (s32[8,1]{1,0:T(8,128)S(1)}, s32[8,1]{1,0:T(8,128)}, u32[]{:S(2)}) copy-start(s32[8,1]{1,0:T(8,128)} %constant.77) | copy-start | bytes 100
  39.3 5.6 %copy-start.6 = (s32[8,1]{1,0:T(8,128)S(1)}, s32[8,1]{1,0:T(8,128)}, u32[]{:S(2)}) copy-start(s32[8,1]{1,0:T(8,128)} %constant.76) | copy-start | bytes 100
  39.3 35.2 %all-to-all-start = ((bf16[8,64,3584]{2,1,0:T(8,128)(2,1)}), bf16[8,64,3584]{2,1,0:T(8,128)(2,1)}, u32[]{:S(2)}, u32[]{:S(2)}) async-start(bf16[8,64,3584]{2,1,0:T(8,128)(2,1)} %bitcast.56), calls=%async_computation | async-start | bytes 7340032 | tf_op jit(solution)/shard_map/all_to_all | solution.py:58
  45.0 1.4 collective-permute-start.7
  51.5 1.9 copy-start
  74.5 32.8 %all-to-all-start.1 = ((bf16[8,64,3584]{2,1,0:T(8,128)(2,1)}), bf16[8,64,3584]{2,1,0:T(8,128)(2,1)}, u32[]{:S(2)}, u32[]{:S(2)}) async-start(bf16[8,64,3584]{2,1,0:T(8,128)(2,1)} %bitcast.53), calls=%async_computation.1 | async-start | bytes 7340032 | tf_op jit(solution)/shard_map/all_to_all | solution.py:58
  99.8 1.9 copy-start.1
  107.3 34.0 %all-to-all-start.2 = ((bf16[8,64,3584]{2,1,0:T(8,128)(2,1)}), bf16[8,64,3584]{2,1,0:T(8,128)(2,1)}, u32[]{:S(2)}, u32[]{:S(2)}) async-start(bf16[8,64,3584]{2,1,0:T(8,128)(2,1)} %bitcast.54), calls=%async_computation.2 | async-start | bytes 7340032 | tf_op jit(solution)/shard_map/all_to_all | solution.py:58
  131.4 1.8 copy-start.2
  171.3 6.1 %collective-permute-start.10 = (bf16[256,3584]{1,0:T(8,128)(2,1)S(1)}, bf16[256,3584]{1,0:T(8,128)(2,1)S(1)}, u32[]{:S(2)}, u32[]{:S(2)}) collective-permute-start(bf16[256,3584]{1,0:T(8,128)(2,1)S(1)} %convolution_convert_fusion.1), channel_id=1, source_target_pairs={{0,16},{1,17},{2,18},{3,19},{4,20},{5,21},{6,22},{7,23},{8,24},{9,... | collective-permute-start | bytes 5505032 | tf_op jit(solution)/shard_map/ppermute | solution.py:43
  172.5 10.4 %collective-permute-start.9 = (bf16[256,3584]{1,0:T(8,128)(2,1)S(1)}, bf16[256,3584]{1,0:T(8,128)(2,1)S(1)}, u32[]{:S(2)}, u32[]{:S(2)}) collective-permute-start(bf16[256,3584]{1,0:T(8,128)(2,1)S(1)} %convolution_convert_fusion.2), channel_id=1, source_target_pairs={{0,16},{1,17},{2,18},{3,19},{4,20},{5,21},{6,22},{7,23},{8,24},{9,... | collective-permute-start | bytes 5505032 | tf_op jit(solution)/shard_map/ppermute | solution.py:43
  177.8 8.6 %collective-permute-start.16 = (bf16[64,3584]{1,0:T(8,128)(2,1)S(1)}, bf16[64,3584]{1,0:T(8,128)(2,1)S(1)}, u32[]{:S(2)}, u32[]{:S(2)}) collective-permute-start(bf16[64,3584]{1,0:T(8,128)(2,1)S(1)} %get-tuple-element.14), channel_id=1, source_target_pairs={{0,4},{1,5},{2,6},{3,7},{4,0},{5,1},{6,2},{7,3},{8,12},{9,13},{10,... | collective-permute-start | bytes 1376264 | tf_op jit(solution)/shard_map/ppermute | solution.py:39
  178.3 13.4 %collective-permute-start.14 = (bf16[64,3584]{1,0:T(8,128)(2,1)S(1)}, bf16[64,3584]{1,0:T(8,128)(2,1)S(1)}, u32[]{:S(2)}, u32[]{:S(2)}) collective-permute-start(bf16[64,3584]{1,0:T(8,128)(2,1)S(1)} %get-tuple-element.15), channel_id=1, source_target_pairs={{0,32},{1,33},{2,34},{3,35},{4,36},{5,37},{6,38},{7,39},{8,40},{9,... | collective-permute-start | bytes 1376264 | tf_op jit(solution)/shard_map/ppermute | solution.py:39
  179.1 13.4 %collective-permute-start.12 = (bf16[64,3584]{1,0:T(8,128)(2,1)S(1)}, bf16[64,3584]{1,0:T(8,128)(2,1)S(1)}, u32[]{:S(2)}, u32[]{:S(2)}) collective-permute-start(bf16[64,3584]{1,0:T(8,128)(2,1)S(1)} %get-tuple-element.16), channel_id=1, source_target_pairs={{0,1},{1,0},{2,3},{3,2},{4,5},{5,4},{6,7},{7,6},{8,9},{9,8},{10,11... | collective-permute-start | bytes 1376264 | tf_op jit(solution)/shard_map/ppermute | solution.py:39
  179.6 16.5 %collective-permute-start.11 = (bf16[64,3584]{1,0:T(8,128)(2,1)S(1)}, bf16[64,3584]{1,0:T(8,128)(2,1)S(1)}, u32[]{:S(2)}, u32[]{:S(2)}) collective-permute-start(bf16[64,3584]{1,0:T(8,128)(2,1)S(1)} %get-tuple-element.13), channel_id=1, source_target_pairs={{0,37},{1,36},{2,39},{3,38},{4,33},{5,32},{6,35},{7,34},{8,45},{9,... | collective-permute-start | bytes 1376264 | tf_op jit(solution)/shard_map/ppermute | solution.py:39
  193.0 8.6 %collective-permute-start.13 = (bf16[64,3584]{1,0:T(8,128)(2,1)S(1)}, bf16[64,3584]{1,0:T(8,128)(2,1)S(1)}, u32[]{:S(2)}, u32[]{:S(2)}) collective-permute-start(bf16[64,3584]{1,0:T(8,128)(2,1)S(1)} %get-tuple-element.17), channel_id=1, source_target_pairs={{0,32},{1,33},{2,34},{3,35},{4,36},{5,37},{6,38},{7,39},{8,40},{9,... | collective-permute-start | bytes 1376264 | tf_op jit(solution)/shard_map/ppermute | solution.py:39
  194.4 8.5 %collective-permute-start.17 = (bf16[64,3584]{1,0:T(8,128)(2,1)S(1)}, bf16[64,3584]{1,0:T(8,128)(2,1)S(1)}, u32[]{:S(2)}, u32[]{:S(2)}) collective-permute-start(bf16[64,3584]{1,0:T(8,128)(2,1)S(1)} %get-tuple-element.18), channel_id=1, source_target_pairs={{0,1},{1,0},{2,3},{3,2},{4,5},{5,4},{6,7},{7,6},{8,9},{9,8},{10,11... | collective-permute-start | bytes 1376264 | tf_op jit(solution)/shard_map/ppermute | solution.py:39
  195.1 8.5 %collective-permute-start.15 = (bf16[64,3584]{1,0:T(8,128)(2,1)S(1)}, bf16[64,3584]{1,0:T(8,128)(2,1)S(1)}, u32[]{:S(2)}, u32[]{:S(2)}) collective-permute-start(bf16[64,3584]{1,0:T(8,128)(2,1)S(1)} %get-tuple-element.19), channel_id=1, source_target_pairs={{0,4},{1,5},{2,6},{3,7},{4,0},{5,1},{6,2},{7,3},{8,12},{9,13},{10,... | collective-permute-start | bytes 1376264 | tf_op jit(solution)/shard_map/ppermute | solution.py:39

commit v5 on v4

--- a/solution.py
+++ b/solution.py
@@ -129,7 +129,7 @@
     members = wanted.shape[0]
     cap = 2 * tok * top // (CORES * RING**3)
     count = members * members * cap
-    wide = 896
+    wide = 1792
     dtype = blocks[0].dtype
     rows = jax.ShapeDtypeStruct((count, width), dtype)
     outs = [(rows, pl.BlockSpec((count, wide), lambda i: (0, i)))]
@@ -148,7 +148,7 @@
         out_specs=[spec for _, spec in outs],
         out_shape=[shape for shape, _ in outs],
         scratch_shapes=[pltpu.VMEM((count, held), dtype)],
-        compiler_params=pltpu.CompilerParams(vmem_limit_bytes=40 * 2**20),
+        compiler_params=pltpu.CompilerParams(vmem_limit_bytes=60 * 2**20),
         cost_estimate=pl.CostEstimate(
             flops=2 * count * held * width, bytes_accessed=6 * count * width, transcendentals=0
         ),
@@ -236,9 +236,8 @@
     corners = len(CORNERS)
     held = corners * tok
 
-    about = jnp.concatenate([expert_ids.astype(jnp.bfloat16), gate_values], axis=1)
-    about = jnp.pad(about, ((0, 0), (0, LANES - 2 * top)))
-    blocks = gather_cube(jnp.concatenate([tokens, about], axis=1))
+    rest = jnp.zeros((tok, LANES - 2 * top), jnp.bfloat16)
+    blocks = gather_cube(jnp.concatenate([tokens, expert_ids.astype(jnp.bfloat16), gate_values, rest], axis=1))
 
     bits = jnp.array(CORNERS, dtype=jnp.int32)
     source = jnp.repeat(jnp.arange(corners, dtype=jnp.int32), tok)

time: 207 us -> 205 us (level)
    unnamed x14 -> x31, local copies, waits for them, and re-layouts: 7.51 us -> 5.17 us
  transfers between devices with their start and end apart: 21 -> 21, of which waited for: 16 -> 16; matrix products, arithmetic and copies ran while one was open for 4% -> 5% of each run, Pallas kernels for 22% -> 22%
where the time goes in v5:
time: 205 us; the launch traced here: 203 us
  waiting for transfers between devices  69.2 us (34%)
  Pallas kernels  50.7 us (25%)
  starting transfers between devices  34.5 us (17%)
  blocking collectives  28.8 us (14%)
  matrix products  7.06 us (3%)
  local copies, waits for them, and re-layouts  6.73 us (3%)
  other arithmetic  5.74 us (3%)
    pallas_call x2, Pallas kernels, expert(): pl.pallas_call(functools.partial(expert_kernel, inner, tile), grid=(inner...  39.1 us
    all_to_all x3, waiting for transfers between devices, exchange(): lax.all_to_all(value, BOTH, split_axis=0, concat_axis=0, axis_index_group...  35.6 us
    ppermute x14, waiting for transfers between devices, to_corner(): lax.ppermute(value, BOTH, [(index_of(*p), moved(p, corner, GATHER[p[1]]))...  32.4 us
    all_to_all x1, blocking collectives, exchange(): lax.all_to_all(value, BOTH, split_axis=0, concat_axis=0, axis_index_group...  28.8 us
    ppermute x14, starting transfers between devices, to_corner(): lax.ppermute(value, BOTH, [(index_of(*p), moved(p, corner, GATHER[p[1]]))...  16.4 us
    all_to_all x3, starting transfers between devices, exchange(): lax.all_to_all(value, BOTH, split_axis=0, concat_axis=0, axis_index_group...  14.7 us
    pallas_call x2, Pallas kernels, select(): pl.pallas_call(functools.partial(select_kernel, len(blocks), tok, top), g...  11.5 us
    dot_general x3, matrix products, collect(): lax.dot_general(weights, back, (((0,), (0,)), ((), ())), preferred_elemen...  6.4 us
  transfers between devices with their start and end apart: 21, of which 16 were waited for; matrix products, arithmetic and copies ran while one was open for 5% of the time, Pallas kernels for 22%

profile of v5, /device:TPU:0, one launch (start us, length us, event | category | flops | bytes accessed | tf_op | source)
XLA Modules:
  0.0 203.1 jit_solution(7426408272128991786)
XLA Ops:
  2.7 2.1 %collective-permute-start.2 = (bf16[64,3712]{1,0:T(8,128)(2,1)S(1)}, bf16[64,3712]{1,0:T(8,128)(2,1)S(1)}, u32[]{:S(2)}, u32[]{:S(2)}) collective-permute-start(bf16[64,3712]{1,0:T(8,128)(2,1)S(1)} %concatenate.3.refs_2_.refs_10_), channel_id=1, source_target_pairs={{0,1},{1,0},{2,3},{3,2},{4,5},{5,4},{6,7},{7,6},{8,9},{9,8},{10,11... | collective-permute-start | bytes 1425416 | tf_op jit(solution)/shard_map/ppermute | solution.py:39
  4.8 1.5 collective-permute-start.1
  6.3 1.6 collective-permute-start
  7.9 3.6 %collective-permute-done.2.refs_5_.refs_13_ = bf16[64,3712]{1,0:T(8,128)(2,1)S(1)} collective-permute-done((bf16[64,3712]{1,0:T(8,128)(2,1)S(1)}, bf16[64,3712]{1,0:T(8,128)(2,1)S(1)}, u32[]{:S(2)}, u32[]{:S(2)}) %collective-permute-start.2) | collective-permute-done | bytes 475168 | tf_op jit(solution)/shard_map/ppermute | solution.py:39
  11.4 1.6 collective-permute-start.4
  13.4 1.6 collective-permute-start.3
  15.0 5.0 %collective-permute-done.refs_3_.refs_11_ = bf16[64,3712]{1,0:T(8,128)(2,1)S(1)} collective-permute-done((bf16[64,3712]{1,0:T(8,128)(2,1)S(1)}, bf16[64,3712]{1,0:T(8,128)(2,1)S(1)}, u32[]{:S(2)}, u32[]{:S(2)}) %collective-permute-start) | collective-permute-done | bytes 475168 | tf_op jit(solution)/shard_map/ppermute | solution.py:39
  20.2 1.3 add_convert_fusion.13
  23.7 1.4 collective-permute-done.3.refs_6_.refs_14_
  25.1 3.7 %collective-permute-done.5.refs_8_.refs_16_ = bf16[64,3712]{1,0:T(8,128)(2,1)} collective-permute-done((bf16[64,3712]{1,0:T(8,128)(2,1)S(1)}, bf16[64,3712]{1,0:T(8,128)(2,1)}, u32[]{:S(2)}, u32[]{:S(2)}) %collective-permute-start.5) | collective-permute-done | bytes 475168 | tf_op jit(solution)/shard_map/ppermute | solution.py:39
  28.8 6.1 %select.14 = (bf16[512,3584]{1,0:T(8,128)(2,1)}, bf16[512,3584]{1,0:T(8,128)(2,1)}, bf16[512,128]{1,0:T(8,128)(2,1)}) custom-call(f32[8,1]{1,0:T(8,128)} %get-tuple-element.52.refs_0_, bf16[512,512]{1,0:T(8,128)(2,1)} %fusion.3.refs_1_, bf16[64,3712]{1,0:T(8,128)(2,1)} %copy-done.2, bf16[64,3712]{1,0:T(8,128)(2,1)} %copy-done.5, bf16[64,3712]{1,0:T(8,128)(2,1)} %copy-done.4, ...), custom_call_target="tpu_custom_call" | custom-call | flops 1879048192 | bytes 11010048 | tf_op jit(solution)/shard_map/select/pallas_call | solution.py:139
  34.9 2.5 %collective-permute-start.8 = (bf16[512,3584]{1,0:T(8,128)(2,1)}, bf16[512,3584]{1,0:T(8,128)(2,1)}, u32[]{:S(2)}, u32[]{:S(2)}) collective-permute-start(bf16[512,3584]{1,0:T(8,128)(2,1)} %get-tuple-element.10), channel_id=1, source_target_pairs={{0,16},{1,17},{2,18},{3,19},{4,20},{5,21},{6,22},{7,23},{8,24},{9,... | collective-permute-start | bytes 11010056 | tf_op jit(solution)/shard_map/ppermute | solution.py:43
  37.4 5.6 %all-to-all-start = ((bf16[8,64,3584]{2,1,0:T(8,128)(2,1)}), bf16[8,64,3584]{2,1,0:T(8,128)(2,1)}, u32[]{:S(2)}, u32[]{:S(2)}) async-start(bf16[8,64,3584]{2,1,0:T(8,128)(2,1)} %bitcast.63), calls=%async_computation | async-start | bytes 7340032 | tf_op jit(solution)/shard_map/all_to_all | solution.py:58
  43.4 1.2 collective-permute-done.7.refs_3_
  45.3 5.5 %select.15 = bf16[512,3584]{1,0:T(8,128)(2,1)} custom-call(f32[8,1]{1,0:T(8,128)} %get-tuple-element.53.refs_0_, bf16[512,512]{1,0:T(8,128)(2,1)} %fusion.3.refs_1_, bf16[512,3584]{1,0:T(8,128)(2,1)} %collective-permute-done.8.refs_2_, bf16[512,128]{1,0:T(8,128)(2,1)} %copy-done.9), custom_call_target="tpu_custom_call" | custom-call | flops 1879048192 | bytes 11010048 | tf_op jit(solution)/shard_map/select/pallas_call | solution.py:139
  50.7 21.9 %all-to-all-done = bf16[8,64,3584]{2,1,0:T(8,128)(2,1)} async-done(((bf16[8,64,3584]{2,1,0:T(8,128)(2,1)}), bf16[8,64,3584]{2,1,0:T(8,128)(2,1)}, u32[]{:S(2)}, u32[]{:S(2)}) %all-to-all-start) | async-done | bytes 3670048 | tf_op jit(solution)/shard_map/all_to_all | solution.py:58
  72.6 4.6 %all-to-all-start.1 = ((bf16[8,64,3584]{2,1,0:T(8,128)(2,1)}), bf16[8,64,3584]{2,1,0:T(8,128)(2,1)}, u32[]{:S(2)}, u32[]{:S(2)}) async-start(bf16[8,64,3584]{2,1,0:T(8,128)(2,1)} %bitcast.62), calls=%async_computation.1 | async-start | bytes 7340032 | tf_op jit(solution)/shard_map/all_to_all | solution.py:58
  78.5 19.6 %expert.2.value_ref = bf16[512,3584]{1,0:T(8,128)(2,1)S(1)} custom-call(bf16[512,3584]{1,0:T(8,128)(2,1)} %bitcast.20.rows_ref, bf16[3584,1024]{1,0:T(8,128)(2,1)} %bitcast.116, bf16[3584,1024]{1,0:T(8,128)(2,1)} %bitcast.118, bf16[1024,3584]{1,0:T(8,128)(2,1)} %bitcast.120, bf16[512,512]{1,0:T(8,128)(2,1)S(1)} %bitcast.58, bf16[512,512]{1,0:T(8,128)(2,1)S(1)} %bitcast.55), custom_call_target="tpu_custom_call" | custom-call | flops 11274289152 | bytes 29360128 | tf_op jit(solution)/shard_map/expert/pallas_call | solution.py:204
  98.1 1.9 copy-done
  100.0 5.6 %all-to-all-done.1 = bf16[8,64,3584]{2,1,0:T(8,128)(2,1)} async-done(((bf16[8,64,3584]{2,1,0:T(8,128)(2,1)}), bf16[8,64,3584]{2,1,0:T(8,128)(2,1)}, u32[]{:S(2)}, u32[]{:S(2)}) %all-to-all-start.1) | async-done | bytes 3670048 | tf_op jit(solution)/shard_map/all_to_all | solution.py:58
  105.6 4.5 %all-to-all-start.2 = ((bf16[8,64,3584]{2,1,0:T(8,128)(2,1)}), bf16[8,64,3584]{2,1,0:T(8,128)(2,1)}, u32[]{:S(2)}, u32[]{:S(2)}) async-start(bf16[8,64,3584]{2,1,0:T(8,128)(2,1)} %bitcast.53), calls=%async_computation.2 | async-start | bytes 7340032 | tf_op jit(solution)/shard_map/all_to_all | solution.py:58
  110.1 19.6 %expert.3.value_ref = bf16[512,3584]{1,0:T(8,128)(2,1)S(1)} custom-call(bf16[512,3584]{1,0:T(8,128)(2,1)} %bitcast.44.after_ref.rows_ref, bf16[3584,1024]{1,0:T(8,128)(2,1)} %bitcast.117, bf16[3584,1024]{1,0:T(8,128)(2,1)} %bitcast.119, bf16[1024,3584]{1,0:T(8,128)(2,1)} %bitcast.121, bf16[512,3584]{1,0:T(8,128)(2,1)} %follow.2.refs_0_), custom_call_target="tpu_custom_call" | custom-call | flops 11274289152 | bytes 29360128 | tf_op jit(solution)/shard_map/expert/pallas_call | solution.py:204
  129.7 1.8 copy-done.1
  131.5 8.2 %all-to-all-done.2 = bf16[8,64,3584]{2,1,0:T(8,128)(2,1)} async-done(((bf16[8,64,3584]{2,1,0:T(8,128)(2,1)}), bf16[8,64,3584]{2,1,0:T(8,128)(2,1)}, u32[]{:S(2)}, u32[]{:S(2)}) %all-to-all-start.2) | async-done | bytes 3670048 | tf_op jit(solution)/shard_map/all_to_all | solution.py:58
  139.6 28.8 %all_to_all.20 = bf16[8,64,3584]{2,1,0:T(8,128)(2,1)S(1)} all-to-all(bf16[8,64,3584]{2,1,0:T(8,128)(2,1)} %bitcast.54), channel_id=1, replica_groups={{0,1,4,5,32,33,36,37},{2,3,6,7,34,35,38,39},{8,9,12,13,40,41,44,45},{10..., dimensions={0} | all-to-all | bytes 7340032 | tf_op jit(solution)/shard_map/all_to_all | solution.py:58
  171.6 4.1 %convolution_convert_fusion = bf16[512,3584]{1,0:T(8,128)(2,1)S(1)} fusion(bf16[512,512]{1,0:T(8,128)(2,1)S(1)} %bitcast.59, bf16[512,3584]{1,0:T(8,128)(2,1)} %bitcast.46.after_ref), kind=kOutput, calls=%fused_computation | convolution fusion | flops 1880883200 | bytes 7864320 | tf_op jit(solution)/shard_map/dot_general | solution.py:276
  177.9 3.3 %collective-permute-start.11 = (bf16[64,3584]{1,0:T(8,128)(2,1)S(1)}, bf16[64,3584]{1,0:T(8,128)(2,1)S(1)}, u32[]{:S(2)}, u32[]{:S(2)}) collective-permute-start(bf16[64,3584]{1,0:T(8,128)(2,1)S(1)} %get-tuple-element.13), channel_id=1, source_target_pairs={{0,37},{1,36},{2,39},{3,38},{4,33},{5,32},{6,35},{7,34},{8,45},{9,... | collective-permute-start | bytes 1376264 | tf_op jit(solution)/shard_map/ppermute | solution.py:39
  181.2 3.5 %collective-permute-done.16 = bf16[64,3584]{1,0:T(8,128)(2,1)S(1)} collective-permute-done((bf16[64,3584]{1,0:T(8,128)(2,1)S(1)}, bf16[64,3584]{1,0:T(8,128)(2,1)S(1)}, u32[]{:S(2)}, u32[]{:S(2)}) %collective-permute-start.16) | collective-permute-done | bytes 458784 | tf_op jit(solution)/shard_map/ppermute | solution.py:39
  184.7 5.3 %collective-permute-done.14 = bf16[64,3584]{1,0:T(8,128)(2,1)S(1)} collective-permute-done((bf16[64,3584]{1,0:T(8,128)(2,1)S(1)}, bf16[64,3584]{1,0:T(8,128)(2,1)S(1)}, u32[]{:S(2)}, u32[]{:S(2)}) %collective-permute-start.14) | collective-permute-done | bytes 458784 | tf_op jit(solution)/shard_map/ppermute | solution.py:39
  191.4 1.3 collective-permute-start.13
  194.3 5.6 %collective-permute-done.13 = bf16[64,3584]{1,0:T(8,128)(2,1)S(1)} collective-permute-done((bf16[64,3584]{1,0:T(8,128)(2,1)S(1)}, bf16[64,3584]{1,0:T(8,128)(2,1)S(1)}, u32[]{:S(2)}, u32[]{:S(2)}) %collective-permute-start.13) | collective-permute-done | bytes 458784 | tf_op jit(solution)/shard_map/ppermute | solution.py:39
  199.9 1.2 collective-permute-done.17
  (77 shorter events, 18.0 us)
Async XLA Ops:
  2.7 26.1 %copy-start.2 = (bf16[64,3712]{1,0:T(8,128)(2,1)}, bf16[64,3712]{1,0:T(8,128)(2,1)S(1)}, u32[]{:S(2)}) copy-start(bf16[64,3712]{1,0:T(8,128)(2,1)S(1)} %concatenate.3.refs_2_.refs_10_) | copy-start | bytes 1425412
  2.7 8.7 %collective-permute-start.2 = (bf16[64,3712]{1,0:T(8,128)(2,1)S(1)}, bf16[64,3712]{1,0:T(8,128)(2,1)S(1)}, u32[]{:S(2)}, u32[]{:S(2)}) collective-permute-start(bf16[64,3712]{1,0:T(8,128)(2,1)S(1)} %concatenate.3.refs_2_.refs_10_), channel_id=1, source_target_pairs={{0,1},{1,0},{2,3},{3,2},{4,5},{5,4},{6,7},{7,6},{8,9},{9,8},{10,11... | collective-permute-start | bytes 1425416 | tf_op jit(solution)/shard_map/ppermute | solution.py:39
  4.8 8.7 %collective-permute-start.1 = (bf16[64,3712]{1,0:T(8,128)(2,1)S(1)}, bf16[64,3712]{1,0:T(8,128)(2,1)S(1)}, u32[]{:S(2)}, u32[]{:S(2)}) collective-permute-start(bf16[64,3712]{1,0:T(8,128)(2,1)S(1)} %concatenate.3.refs_2_.refs_10_), channel_id=1, source_target_pairs={{0,4},{1,5},{2,6},{3,7},{4,0},{5,1},{6,2},{7,3},{8,12},{9,13},{10,... | collective-permute-start | bytes 1425416 | tf_op jit(solution)/shard_map/ppermute | solution.py:39
  6.3 13.7 %collective-permute-start = (bf16[64,3712]{1,0:T(8,128)(2,1)S(1)}, bf16[64,3712]{1,0:T(8,128)(2,1)S(1)}, u32[]{:S(2)}, u32[]{:S(2)}) collective-permute-start(bf16[64,3712]{1,0:T(8,128)(2,1)S(1)} %concatenate.3.refs_2_.refs_10_), channel_id=1, source_target_pairs={{0,32},{1,33},{2,34},{3,35},{4,36},{5,37},{6,38},{7,39},{8,40},{9,... | collective-permute-start | bytes 1425416 | tf_op jit(solution)/shard_map/ppermute | solution.py:39
  7.9 14.7 %collective-permute-start.6 = (bf16[64,3712]{1,0:T(8,128)(2,1)S(1)}, bf16[64,3712]{1,0:T(8,128)(2,1)S(1)}, u32[]{:S(2)}, u32[]{:S(2)}) collective-permute-start(bf16[64,3712]{1,0:T(8,128)(2,1)S(1)} %concatenate.3.refs_2_.refs_10_), channel_id=1, source_target_pairs={{0,37},{1,36},{2,39},{3,38},{4,33},{5,32},{6,35},{7,34},{8,45},{9,... | collective-permute-start | bytes 1425416 | tf_op jit(solution)/shard_map/ppermute | solution.py:39
  11.4 17.4 %copy-start.3 = (bf16[64,3712]{1,0:T(8,128)(2,1)}, bf16[64,3712]{1,0:T(8,128)(2,1)S(1)}, u32[]{:S(2)}) copy-start(bf16[64,3712]{1,0:T(8,128)(2,1)S(1)} %collective-permute-done.2.refs_5_.refs_13_) | copy-start | bytes 1425412
  11.4 12.2 %collective-permute-start.4 = (bf16[64,3712]{1,0:T(8,128)(2,1)S(1)}, bf16[64,3712]{1,0:T(8,128)(2,1)S(1)}, u32[]{:S(2)}, u32[]{:S(2)}) collective-permute-start(bf16[64,3712]{1,0:T(8,128)(2,1)S(1)} %collective-permute-done.2.refs_5_.refs_13_), channel_id=1, source_target_pairs={{0,4},{1,5},{2,6},{3,7},{4,0},{5,1},{6,2},{7,3},{8,12},{9,13},{10,... | collective-permute-start | bytes 1425416 | tf_op jit(solution)/shard_map/ppermute | solution.py:39
  13.4 15.4 %copy-start.4 = (bf16[64,3712]{1,0:T(8,128)(2,1)}, bf16[64,3712]{1,0:T(8,128)(2,1)S(1)}, u32[]{:S(2)}) copy-start(bf16[64,3712]{1,0:T(8,128)(2,1)S(1)} %collective-permute-done.1.refs_4_.refs_12_) | copy-start | bytes 1425412
  13.4 11.7 %collective-permute-start.3 = (bf16[64,3712]{1,0:T(8,128)(2,1)S(1)}, bf16[64,3712]{1,0:T(8,128)(2,1)S(1)}, u32[]{:S(2)}, u32[]{:S(2)}) collective-permute-start(bf16[64,3712]{1,0:T(8,128)(2,1)S(1)} %collective-permute-done.1.refs_4_.refs_12_), channel_id=1, source_target_pairs={{0,32},{1,33},{2,34},{3,35},{4,36},{5,37},{6,38},{7,39},{8,40},{9,... | collective-permute-start | bytes 1425416 | tf_op jit(solution)/shard_map/ppermute | solution.py:39
  20.0 8.8 %copy-start.5 = (bf16[64,3712]{1,0:T(8,128)(2,1)}, bf16[64,3712]{1,0:T(8,128)(2,1)S(1)}, u32[]{:S(2)}) copy-start(bf16[64,3712]{1,0:T(8,128)(2,1)S(1)} %collective-permute-done.refs_3_.refs_11_) | copy-start | bytes 1425412
  20.0 8.8 %collective-permute-start.5 = (bf16[64,3712]{1,0:T(8,128)(2,1)S(1)}, bf16[64,3712]{1,0:T(8,128)(2,1)}, u32[]{:S(2)}, u32[]{:S(2)}) collective-permute-start(bf16[64,3712]{1,0:T(8,128)(2,1)S(1)} %collective-permute-done.refs_3_.refs_11_), channel_id=1, source_target_pairs={{0,1},{1,0},{2,3},{3,2},{4,5},{5,4},{6,7},{7,6},{8,9},{9,8},{10,11... | collective-permute-start | bytes 1425416 | tf_op jit(solution)/shard_map/ppermute | solution.py:39
  22.5 6.3 %copy-start.6 = (bf16[64,3712]{1,0:T(8,128)(2,1)}, bf16[64,3712]{1,0:T(8,128)(2,1)S(1)}, u32[]{:S(2)}) copy-start(bf16[64,3712]{1,0:T(8,128)(2,1)S(1)} %collective-permute-done.6.refs_9_.refs_17_) | copy-start | bytes 1425412
  23.7 5.1 %copy-start.7 = (bf16[64,3712]{1,0:T(8,128)(2,1)}, bf16[64,3712]{1,0:T(8,128)(2,1)S(1)}, u32[]{:S(2)}) copy-start(bf16[64,3712]{1,0:T(8,128)(2,1)S(1)} %collective-permute-done.4.refs_7_.refs_15_) | copy-start | bytes 1425412
  34.9 9.7 %collective-permute-start.8 = (bf16[512,3584]{1,0:T(8,128)(2,1)}, bf16[512,3584]{1,0:T(8,128)(2,1)}, u32[]{:S(2)}, u32[]{:S(2)}) collective-permute-start(bf16[512,3584]{1,0:T(8,128)(2,1)} %get-tuple-element.10), channel_id=1, source_target_pairs={{0,16},{1,17},{2,18},{3,19},{4,20},{5,21},{6,22},{7,23},{8,24},{9,... | collective-permute-start | bytes 11010056 | tf_op jit(solution)/shard_map/ppermute | solution.py:43
  37.4 5.6 %copy-start.12 = (s32[8,1]{1,0:T(8,128)S(1)}, s32[8,1]{1,0:T(8,128)}, u32[]{:S(2)}) copy-start(s32[8,1]{1,0:T(8,128)} %constant.76) | copy-start | bytes 100
  37.4 5.6 %copy-start.13 = (s32[8,1]{1,0:T(8,128)S(1)}, s32[8,1]{1,0:T(8,128)}, u32[]{:S(2)}) copy-start(s32[8,1]{1,0:T(8,128)} %constant.75) | copy-start | bytes 100
  37.4 5.6 %copy-start.14 = (s32[8,1]{1,0:T(8,128)S(1)}, s32[8,1]{1,0:T(8,128)}, u32[]{:S(2)}) copy-start(s32[8,1]{1,0:T(8,128)} %constant.74) | copy-start | bytes 100
  37.4 5.8 %copy-start.11 = (bf16[512,128]{1,0:T(8,128)(2,1)S(1)}, bf16[512,128]{1,0:T(8,128)(2,1)}, u32[]{:S(2)}) copy-start(bf16[512,128]{1,0:T(8,128)(2,1)} %get-tuple-element.8) | copy-start | bytes 393220
  37.4 35.2 %all-to-all-start = ((bf16[8,64,3584]{2,1,0:T(8,128)(2,1)}), bf16[8,64,3584]{2,1,0:T(8,128)(2,1)}, u32[]{:S(2)}, u32[]{:S(2)}) async-start(bf16[8,64,3584]{2,1,0:T(8,128)(2,1)} %bitcast.63), calls=%async_computation | async-start | bytes 7340032 | tf_op jit(solution)/shard_map/all_to_all | solution.py:58
  43.2 1.4 collective-permute-start.7
  72.6 5.1 %copy-start.10 = (bf16[512,128]{1,0:T(8,128)(2,1)S(1)}, bf16[512,128]{1,0:T(8,128)(2,1)}, u32[]{:S(2)}) copy-start(bf16[512,128]{1,0:T(8,128)(2,1)} %copy-done.9) | copy-start | bytes 393220
  72.6 32.9 %all-to-all-start.1 = ((bf16[8,64,3584]{2,1,0:T(8,128)(2,1)}), bf16[8,64,3584]{2,1,0:T(8,128)(2,1)}, u32[]{:S(2)}, u32[]{:S(2)}) async-start(bf16[8,64,3584]{2,1,0:T(8,128)(2,1)} %bitcast.62), calls=%async_computation.1 | async-start | bytes 7340032 | tf_op jit(solution)/shard_map/all_to_all | solution.py:58
  105.6 34.0 %all-to-all-start.2 = ((bf16[8,64,3584]{2,1,0:T(8,128)(2,1)}), bf16[8,64,3584]{2,1,0:T(8,128)(2,1)}, u32[]{:S(2)}, u32[]{:S(2)}) async-start(bf16[8,64,3584]{2,1,0:T(8,128)(2,1)} %bitcast.53), calls=%async_computation.2 | async-start | bytes 7340032 | tf_op jit(solution)/shard_map/all_to_all | solution.py:58
  169.6 6.1 %collective-permute-start.10 = (bf16[256,3584]{1,0:T(8,128)(2,1)S(1)}, bf16[256,3584]{1,0:T(8,128)(2,1)S(1)}, u32[]{:S(2)}, u32[]{:S(2)}) collective-permute-start(bf16[256,3584]{1,0:T(8,128)(2,1)S(1)} %convolution_convert_fusion.1), channel_id=1, source_target_pairs={{0,16},{1,17},{2,18},{3,19},{4,20},{5,21},{6,22},{7,23},{8,24},{9,... | collective-permute-start | bytes 5505032 | tf_op jit(solution)/shard_map/ppermute | solution.py:43
  171.0 10.2 %collective-permute-start.9 = (bf16[256,3584]{1,0:T(8,128)(2,1)S(1)}, bf16[256,3584]{1,0:T(8,128)(2,1)S(1)}, u32[]{:S(2)}, u32[]{:S(2)}) collective-permute-start(bf16[256,3584]{1,0:T(8,128)(2,1)S(1)} %convolution_convert_fusion.2), channel_id=1, source_target_pairs={{0,16},{1,17},{2,18},{3,19},{4,20},{5,21},{6,22},{7,23},{8,24},{9,... | collective-permute-start | bytes 5505032 | tf_op jit(solution)/shard_map/ppermute | solution.py:43
  176.1 8.6 %collective-permute-start.16 = (bf16[64,3584]{1,0:T(8,128)(2,1)S(1)}, bf16[64,3584]{1,0:T(8,128)(2,1)S(1)}, u32[]{:S(2)}, u32[]{:S(2)}) collective-permute-start(bf16[64,3584]{1,0:T(8,128)(2,1)S(1)} %get-tuple-element.14), channel_id=1, source_target_pairs={{0,4},{1,5},{2,6},{3,7},{4,0},{5,1},{6,2},{7,3},{8,12},{9,13},{10,... | collective-permute-start | bytes 1376264 | tf_op jit(solution)/shard_map/ppermute | solution.py:39
  176.6 13.4 %collective-permute-start.14 = (bf16[64,3584]{1,0:T(8,128)(2,1)S(1)}, bf16[64,3584]{1,0:T(8,128)(2,1)S(1)}, u32[]{:S(2)}, u32[]{:S(2)}) collective-permute-start(bf16[64,3584]{1,0:T(8,128)(2,1)S(1)} %get-tuple-element.15), channel_id=1, source_target_pairs={{0,32},{1,33},{2,34},{3,35},{4,36},{5,37},{6,38},{7,39},{8,40},{9,... | collective-permute-start | bytes 1376264 | tf_op jit(solution)/shard_map/ppermute | solution.py:39
  177.4 13.4 %collective-permute-start.12 = (bf16[64,3584]{1,0:T(8,128)(2,1)S(1)}, bf16[64,3584]{1,0:T(8,128)(2,1)S(1)}, u32[]{:S(2)}, u32[]{:S(2)}) collective-permute-start(bf16[64,3584]{1,0:T(8,128)(2,1)S(1)} %get-tuple-element.16), channel_id=1, source_target_pairs={{0,1},{1,0},{2,3},{3,2},{4,5},{5,4},{6,7},{7,6},{8,9},{9,8},{10,11... | collective-permute-start | bytes 1376264 | tf_op jit(solution)/shard_map/ppermute | solution.py:39
  177.9 16.5 %collective-permute-start.11 = (bf16[64,3584]{1,0:T(8,128)(2,1)S(1)}, bf16[64,3584]{1,0:T(8,128)(2,1)S(1)}, u32[]{:S(2)}, u32[]{:S(2)}) collective-permute-start(bf16[64,3584]{1,0:T(8,128)(2,1)S(1)} %get-tuple-element.13), channel_id=1, source_target_pairs={{0,37},{1,36},{2,39},{3,38},{4,33},{5,32},{6,35},{7,34},{8,45},{9,... | collective-permute-start | bytes 1376264 | tf_op jit(solution)/shard_map/ppermute | solution.py:39
  191.4 8.6 %collective-permute-start.13 = (bf16[64,3584]{1,0:T(8,128)(2,1)S(1)}, bf16[64,3584]{1,0:T(8,128)(2,1)S(1)}, u32[]{:S(2)}, u32[]{:S(2)}) collective-permute-start(bf16[64,3584]{1,0:T(8,128)(2,1)S(1)} %get-tuple-element.17), channel_id=1, source_target_pairs={{0,32},{1,33},{2,34},{3,35},{4,36},{5,37},{6,38},{7,39},{8,40},{9,... | collective-permute-start | bytes 1376264 | tf_op jit(solution)/shard_map/ppermute | solution.py:39
  192.7 8.5 %collective-permute-start.17 = (bf16[64,3584]{1,0:T(8,128)(2,1)S(1)}, bf16[64,3584]{1,0:T(8,128)(2,1)S(1)}, u32[]{:S(2)}, u32[]{:S(2)}) collective-permute-start(bf16[64,3584]{1,0:T(8,128)(2,1)S(1)} %get-tuple-element.18), channel_id=1, source_target_pairs={{0,1},{1,0},{2,3},{3,2},{4,5},{5,4},{6,7},{7,6},{8,9},{9,8},{10,11... | collective-permute-start | bytes 1376264 | tf_op jit(solution)/shard_map/ppermute | solution.py:39
  193.4 8.5 %collective-permute-start.15 = (bf16[64,3584]{1,0:T(8,128)(2,1)S(1)}, bf16[64,3584]{1,0:T(8,128)(2,1)S(1)}, u32[]{:S(2)}, u32[]{:S(2)}) collective-permute-start(bf16[64,3584]{1,0:T(8,128)(2,1)S(1)} %get-tuple-element.19), channel_id=1, source_target_pairs={{0,4},{1,5},{2,6},{3,7},{4,0},{5,1},{6,2},{7,3},{8,12},{9,13},{10,... | collective-permute-start | bytes 1376264 | tf_op jit(solution)/shard_map/ppermute | solution.py:39
  (4 other events, 8.1 us)

commit v6 on v5

--- a/solution.py
+++ b/solution.py
@@ -285,18 +285,16 @@
     other_picked = select(other_experts, earlier, [other_held], [other_known], 0, tok, top, width, False)[0]
     other_rows = exchange(other_picked.reshape(boxed), 1).reshape(flat)
     own_weights = weights_of(own_experts, own_known)
-    other_weights = weights_of(other_experts, other_known)
+    beside = (own_experts.astype(jnp.int32) ^ (RING * RING)).astype(jnp.float32)
+    other_weights = weights_of(beside, own_known)
     own_out = follow(expert(own_rows, *experts_of, [own_weights, other_weights]), other_rows)
     own_back = exchange(own_out.reshape(boxed), 0).reshape(flat)
     other_out = follow(expert(other_rows, *experts_of, [own_out]), own_back)
-    other_back = exchange(other_out.reshape(boxed), 1).reshape(flat)
     own_total = collect(own_back, own_weights)
-    half = held // 2
-    far = to_other_core(collect(other_back, other_weights[:, half:]))
-    near = to_other_core(collect(other_back, other_weights[:, :half]))
-    total = [add(own_total[i * tok : (i + 1) * tok], near[i * tok : (i + 1) * tok]) for i in range(corners // 2)]
-    total += [add(own_total[half + i * tok :][:tok], far[i * tok : (i + 1) * tok]) for i in range(corners // 2)]
-    return reduce_cube(total)
+    other_out = follow(to_other_core(other_out), own_total)
+    other_back = exchange(other_out.reshape(boxed), 0).reshape(flat)
+    total = add(own_total, collect(other_back, other_weights))
+    return reduce_cube([total[i * tok : (i + 1) * tok] for i in range(corners)])
 
 
 def solution(mesh):

time: 205 us -> 206 us (level)
  blocking collectives: 28.8 us -> 32.7 us
  waiting for transfers between devices: 69.2 us -> 66.6 us
    all_to_all x1, blocking collectives: 28.8 us -> 32.7 us  [exchange(): lax.all_to_all(value, BOTH, split_axis=0, concat_axis=0, axis_index_group...]
    ppermute x14, waiting for transfers between devices: 32.4 us -> 28.8 us  [to_corner(): lax.ppermute(value, BOTH, [(index_of(*p), moved(p, corner, GATHER[p[1]]))...]
    dot_general x3 -> x2, matrix products: 6.4 us -> 8.1 us  [collect(): lax.dot_general(weights, back, (((0,), (0,)), ((), ())), preferred_elemen...]
  transfers between devices with their start and end apart: 21 -> 20, of which waited for: 16 -> 17; matrix products, arithmetic and copies ran while one was open for 5% -> 5% of each run, Pallas kernels for 22% -> 22%
where the time goes in v6:
time: 206 us; the launch traced here: 205 us
  waiting for transfers between devices  66.6 us (32%)
  Pallas kernels  50.7 us (25%)
  starting transfers between devices  34.5 us (17%)
  blocking collectives  32.7 us (16%)
  matrix products  8.76 us (4%)
  local copies, waits for them, and re-layouts  6.86 us (3%)
  other arithmetic  4.83 us (2%)
    pallas_call x2, Pallas kernels, expert(): pl.pallas_call(functools.partial(expert_kernel, inner, tile), grid=(inner...  39.2 us
    all_to_all x3, waiting for transfers between devices, exchange(): lax.all_to_all(value, BOTH, split_axis=0, concat_axis=0, axis_index_group...  35.6 us
    all_to_all x1, blocking collectives, exchange(): lax.all_to_all(value, BOTH, split_axis=0, concat_axis=0, axis_index_group...  32.7 us
    ppermute x14, waiting for transfers between devices, to_corner(): lax.ppermute(value, BOTH, [(index_of(*p), moved(p, corner, GATHER[p[1]]))...  28.8 us
    ppermute x14, starting transfers between devices, to_corner(): lax.ppermute(value, BOTH, [(index_of(*p), moved(p, corner, GATHER[p[1]]))...  15.9 us
    all_to_all x3, starting transfers between devices, exchange(): lax.all_to_all(value, BOTH, split_axis=0, concat_axis=0, axis_index_group...  15.6 us
    pallas_call x2, Pallas kernels, select(): pl.pallas_call(functools.partial(select_kernel, len(blocks), tok, top), g...  11.5 us
    dot_general x2, matrix products, collect(): lax.dot_general(weights, back, (((0,), (0,)), ((), ())), preferred_elemen...  8.1 us
  transfers between devices with their start and end apart: 20, of which 17 were waited for; matrix products, arithmetic and copies ran while one was open for 5% of the time, Pallas kernels for 22%

profile of v6, /device:TPU:0, one launch (start us, length us, event | category | flops | bytes accessed | tf_op | source)
XLA Modules:
  0.0 205.1 jit_solution(8162136912377846070)
XLA Ops:
  2.7 1.7 collective-permute-start.1
  4.4 1.9 collective-permute-start.2
  6.3 1.6 collective-permute-start
  7.9 3.6 %collective-permute-done.1.refs_4_.refs_12_ = bf16[64,3712]{1,0:T(8,128)(2,1)S(1)} collective-permute-done((bf16[64,3712]{1,0:T(8,128)(2,1)S(1)}, bf16[64,3712]{1,0:T(8,128)(2,1)S(1)}, u32[]{:S(2)}, u32[]{:S(2)}) %collective-permute-start.1) | collective-permute-done | bytes 475168 | tf_op jit(solution)/shard_map/ppermute | solution.py:39
  11.4 1.7 collective-permute-start.3
  13.1 4.4 %collective-permute-done.2.refs_5_.refs_13_ = bf16[64,3712]{1,0:T(8,128)(2,1)S(1)} collective-permute-done((bf16[64,3712]{1,0:T(8,128)(2,1)S(1)}, bf16[64,3712]{1,0:T(8,128)(2,1)S(1)}, u32[]{:S(2)}, u32[]{:S(2)}) %collective-permute-start.2) | collective-permute-done | bytes 475168 | tf_op jit(solution)/shard_map/ppermute | solution.py:39
  17.6 2.5 %collective-permute-done.refs_3_.refs_11_ = bf16[64,3712]{1,0:T(8,128)(2,1)S(1)} collective-permute-done((bf16[64,3712]{1,0:T(8,128)(2,1)S(1)}, bf16[64,3712]{1,0:T(8,128)(2,1)S(1)}, u32[]{:S(2)}, u32[]{:S(2)}) %collective-permute-start) | collective-permute-done | bytes 475168 | tf_op jit(solution)/shard_map/ppermute | solution.py:39
  22.5 2.6 %collective-permute-done.3.refs_6_.refs_14_ = bf16[64,3712]{1,0:T(8,128)(2,1)S(1)} collective-permute-done((bf16[64,3712]{1,0:T(8,128)(2,1)S(1)}, bf16[64,3712]{1,0:T(8,128)(2,1)S(1)}, u32[]{:S(2)}, u32[]{:S(2)}) %collective-permute-start.3) | collective-permute-done | bytes 475168 | tf_op jit(solution)/shard_map/ppermute | solution.py:39
  26.2 2.6 %collective-permute-done.5.refs_8_.refs_16_ = bf16[64,3712]{1,0:T(8,128)(2,1)} collective-permute-done((bf16[64,3712]{1,0:T(8,128)(2,1)S(1)}, bf16[64,3712]{1,0:T(8,128)(2,1)}, u32[]{:S(2)}, u32[]{:S(2)}) %collective-permute-start.5) | collective-permute-done | bytes 475168 | tf_op jit(solution)/shard_map/ppermute | solution.py:39
  28.8 6.1 %select.14 = (bf16[512,3584]{1,0:T(8,128)(2,1)}, bf16[512,3584]{1,0:T(8,128)(2,1)}, bf16[512,128]{1,0:T(8,128)(2,1)}) custom-call(f32[8,1]{1,0:T(8,128)} %get-tuple-element.39.refs_0_, bf16[512,512]{1,0:T(8,128)(2,1)} %fusion.3.refs_1_, bf16[64,3712]{1,0:T(8,128)(2,1)} %copy-done.3, bf16[64,3712]{1,0:T(8,128)(2,1)} %copy-done.6, bf16[64,3712]{1,0:T(8,128)(2,1)} %copy-done.4, ...), custom_call_target="tpu_custom_call" | custom-call | flops 1879048192 | bytes 11010048 | tf_op jit(solution)/shard_map/select/pallas_call | solution.py:139
  34.9 2.9 %collective-permute-start.7 = (bf16[512,3584]{1,0:T(8,128)(2,1)}, bf16[512,3584]{1,0:T(8,128)(2,1)}, u32[]{:S(2)}, u32[]{:S(2)}) collective-permute-start(bf16[512,3584]{1,0:T(8,128)(2,1)} %get-tuple-element.10), channel_id=1, source_target_pairs={{0,16},{1,17},{2,18},{3,19},{4,20},{5,21},{6,22},{7,23},{8,24},{9,... | collective-permute-start | bytes 11010056 | tf_op jit(solution)/shard_map/ppermute | solution.py:43
  37.8 6.5 %all-to-all-start = ((bf16[8,64,3584]{2,1,0:T(8,128)(2,1)}), bf16[8,64,3584]{2,1,0:T(8,128)(2,1)}, u32[]{:S(2)}, u32[]{:S(2)}) async-start(bf16[8,64,3584]{2,1,0:T(8,128)(2,1)} %bitcast.42), calls=%async_computation | async-start | bytes 7340032 | tf_op jit(solution)/shard_map/all_to_all | solution.py:58
  46.4 5.5 %select.15 = bf16[512,3584]{1,0:T(8,128)(2,1)} custom-call(f32[8,1]{1,0:T(8,128)} %get-tuple-element.38.refs_0_, bf16[512,512]{1,0:T(8,128)(2,1)} %fusion.3.refs_1_, bf16[512,3584]{1,0:T(8,128)(2,1)} %collective-permute-done.7.refs_2_, bf16[512,128]{1,0:T(8,128)(2,1)} %copy-done.10), custom_call_target="tpu_custom_call" | custom-call | flops 1879048192 | bytes 11010048 | tf_op jit(solution)/shard_map/select/pallas_call | solution.py:139
  51.9 22.1 %all-to-all-done = bf16[8,64,3584]{2,1,0:T(8,128)(2,1)} async-done(((bf16[8,64,3584]{2,1,0:T(8,128)(2,1)}), bf16[8,64,3584]{2,1,0:T(8,128)(2,1)}, u32[]{:S(2)}, u32[]{:S(2)}) %all-to-all-start) | async-done | bytes 3670048 | tf_op jit(solution)/shard_map/all_to_all | solution.py:58
  74.0 4.6 %all-to-all-start.1 = ((bf16[8,64,3584]{2,1,0:T(8,128)(2,1)}), bf16[8,64,3584]{2,1,0:T(8,128)(2,1)}, u32[]{:S(2)}, u32[]{:S(2)}) async-start(bf16[8,64,3584]{2,1,0:T(8,128)(2,1)} %bitcast.40), calls=%async_computation.1 | async-start | bytes 7340032 | tf_op jit(solution)/shard_map/all_to_all | solution.py:58
  79.9 19.6 %expert.2.value_ref = bf16[512,3584]{1,0:T(8,128)(2,1)S(1)} custom-call(bf16[512,3584]{1,0:T(8,128)(2,1)} %bitcast.20.rows_ref, bf16[3584,1024]{1,0:T(8,128)(2,1)} %bitcast.77, bf16[3584,1024]{1,0:T(8,128)(2,1)} %bitcast.79, bf16[1024,3584]{1,0:T(8,128)(2,1)} %bitcast.81, bf16[512,512]{1,0:T(8,128)(2,1)S(1)} %bitcast.38, bf16[512,512]{1,0:T(8,128)(2,1)S(1)} %bitcast.36), custom_call_target="tpu_custom_call" | custom-call | flops 11274289152 | bytes 29360128 | tf_op jit(solution)/shard_map/expert/pallas_call | solution.py:204
  99.5 1.9 copy-done
  101.4 5.5 %all-to-all-done.1 = bf16[8,64,3584]{2,1,0:T(8,128)(2,1)} async-done(((bf16[8,64,3584]{2,1,0:T(8,128)(2,1)}), bf16[8,64,3584]{2,1,0:T(8,128)(2,1)}, u32[]{:S(2)}, u32[]{:S(2)}) %all-to-all-start.1) | async-done | bytes 3670048 | tf_op jit(solution)/shard_map/all_to_all | solution.py:58
  106.9 4.5 %all-to-all-start.2 = ((bf16[8,64,3584]{2,1,0:T(8,128)(2,1)}), bf16[8,64,3584]{2,1,0:T(8,128)(2,1)}, u32[]{:S(2)}, u32[]{:S(2)}) async-start(bf16[8,64,3584]{2,1,0:T(8,128)(2,1)} %bitcast.35), calls=%async_computation.2 | async-start | bytes 7340032 | tf_op jit(solution)/shard_map/all_to_all | solution.py:58
  111.4 19.6 %expert.3.value_ref = bf16[512,3584]{1,0:T(8,128)(2,1)S(1)} custom-call(bf16[512,3584]{1,0:T(8,128)(2,1)} %bitcast.26.after_ref.rows_ref, bf16[3584,1024]{1,0:T(8,128)(2,1)} %bitcast.78, bf16[3584,1024]{1,0:T(8,128)(2,1)} %bitcast.80, bf16[1024,3584]{1,0:T(8,128)(2,1)} %bitcast.82, bf16[512,3584]{1,0:T(8,128)(2,1)} %follow.3.refs_0_), custom_call_target="tpu_custom_call" | custom-call | flops 11274289152 | bytes 29360128 | tf_op jit(solution)/shard_map/expert/pallas_call | solution.py:204
  131.0 1.9 copy-done.1
  132.9 8.0 %all-to-all-done.2 = bf16[8,64,3584]{2,1,0:T(8,128)(2,1)} async-done(((bf16[8,64,3584]{2,1,0:T(8,128)(2,1)}), bf16[8,64,3584]{2,1,0:T(8,128)(2,1)}, u32[]{:S(2)}, u32[]{:S(2)}) %all-to-all-start.2) | async-done | bytes 3670048 | tf_op jit(solution)/shard_map/all_to_all | solution.py:58
  140.9 5.9 %convolution_convert_fusion.1.after_ref = bf16[512,3584]{1,0:T(8,128)(2,1)} fusion(bf16[512,512]{1,0:T(8,128)(2,1)S(1)} %bitcast.39, bf16[512,3584]{1,0:T(8,128)(2,1)} %bitcast.28.after_ref), kind=kOutput, calls=%fused_computation.2 | convolution fusion | flops 1880883200 | bytes 7864320 | tf_op jit(solution)/shard_map/dot_general | solution.py:276
  147.7 32.7 %all_to_all.20 = bf16[8,64,3584]{2,1,0:T(8,128)(2,1)S(1)} all-to-all(bf16[8,64,3584]{2,1,0:T(8,128)(2,1)} %bitcast.29), channel_id=1, replica_groups={{0,3,12,15,96,99,108,111},{1,2,13,14,97,98,109,110},{4,7,8,11,100,103,1..., dimensions={0} | all-to-all | bytes 7340032 | tf_op jit(solution)/shard_map/all_to_all | solution.py:58
  180.4 2.2 %add_convert_fusion = bf16[512,3584]{1,0:T(8,128)(2,1)S(1)} fusion(bf16[512,3584]{1,0:T(8,128)(2,1)S(1)} %copy-done.2, bf16[512,512]{1,0:T(8,128)(2,1)S(1)} %bitcast.37, bf16[512,3584]{1,0:T(8,128)(2,1)S(1)} %bitcast.41), kind=kOutput, calls=%fused_computation | convolution fusion | flops 1888223232 | bytes 11534336 | tf_op jit(solution)/shard_map/dot_general | solution.py:276
  183.0 4.8 %collective-permute-start.10 = (bf16[64,3584]{1,0:T(8,128)(2,1)S(1)}, bf16[64,3584]{1,0:T(8,128)(2,1)S(1)}, u32[]{:S(2)}, u32[]{:S(2)}) collective-permute-start(bf16[64,3584]{1,0:T(8,128)(2,1)S(1)} %get-tuple-element.13), channel_id=1, source_target_pairs={{0,37},{1,36},{2,39},{3,38},{4,33},{5,32},{6,35},{7,34},{8,45},{9,... | collective-permute-start | bytes 1376264 | tf_op jit(solution)/shard_map/ppermute | solution.py:39
  187.7 3.5 %collective-permute-done.11 = bf16[64,3584]{1,0:T(8,128)(2,1)S(1)} collective-permute-done((bf16[64,3584]{1,0:T(8,128)(2,1)S(1)}, bf16[64,3584]{1,0:T(8,128)(2,1)S(1)}, u32[]{:S(2)}, u32[]{:S(2)}) %collective-permute-start.11) | collective-permute-done | bytes 458784 | tf_op jit(solution)/shard_map/ppermute | solution.py:39
  191.8 2.0 collective-permute-start.12
  193.8 1.9 collective-permute-start.16
  195.7 3.5 %collective-permute-done.10 = bf16[64,3584]{1,0:T(8,128)(2,1)S(1)} collective-permute-done((bf16[64,3584]{1,0:T(8,128)(2,1)S(1)}, bf16[64,3584]{1,0:T(8,128)(2,1)S(1)}, u32[]{:S(2)}, u32[]{:S(2)}) %collective-permute-start.10) | collective-permute-done | bytes 458784 | tf_op jit(solution)/shard_map/ppermute | solution.py:39
  199.3 3.4 %collective-permute-done.12 = bf16[64,3584]{1,0:T(8,128)(2,1)S(1)} collective-permute-done((bf16[64,3584]{1,0:T(8,128)(2,1)S(1)}, bf16[64,3584]{1,0:T(8,128)(2,1)S(1)}, u32[]{:S(2)}, u32[]{:S(2)}) %collective-permute-start.12) | collective-permute-done | bytes 458784 | tf_op jit(solution)/shard_map/ppermute | solution.py:39
  202.7 1.4 collective-permute-done.16
  (70 shorter events, 12.4 us)
Async XLA Ops:
  2.7 26.1 %copy-start.3 = (bf16[64,3712]{1,0:T(8,128)(2,1)}, bf16[64,3712]{1,0:T(8,128)(2,1)S(1)}, u32[]{:S(2)}) copy-start(bf16[64,3712]{1,0:T(8,128)(2,1)S(1)} %concatenate.3.refs_2_.refs_10_) | copy-start | bytes 1425412
  2.7 8.7 %collective-permute-start.1 = (bf16[64,3712]{1,0:T(8,128)(2,1)S(1)}, bf16[64,3712]{1,0:T(8,128)(2,1)S(1)}, u32[]{:S(2)}, u32[]{:S(2)}) collective-permute-start(bf16[64,3712]{1,0:T(8,128)(2,1)S(1)} %concatenate.3.refs_2_.refs_10_), channel_id=1, source_target_pairs={{0,4},{1,5},{2,6},{3,7},{4,0},{5,1},{6,2},{7,3},{8,12},{9,13},{10,... | collective-permute-start | bytes 1425416 | tf_op jit(solution)/shard_map/ppermute | solution.py:39
  4.4 13.2 %collective-permute-start.2 = (bf16[64,3712]{1,0:T(8,128)(2,1)S(1)}, bf16[64,3712]{1,0:T(8,128)(2,1)S(1)}, u32[]{:S(2)}, u32[]{:S(2)}) collective-permute-start(bf16[64,3712]{1,0:T(8,128)(2,1)S(1)} %concatenate.3.refs_2_.refs_10_), channel_id=1, source_target_pairs={{0,1},{1,0},{2,3},{3,2},{4,5},{5,4},{6,7},{7,6},{8,9},{9,8},{10,11... | collective-permute-start | bytes 1425416 | tf_op jit(solution)/shard_map/ppermute | solution.py:39
  6.3 13.7 %collective-permute-start = (bf16[64,3712]{1,0:T(8,128)(2,1)S(1)}, bf16[64,3712]{1,0:T(8,128)(2,1)S(1)}, u32[]{:S(2)}, u32[]{:S(2)}) collective-permute-start(bf16[64,3712]{1,0:T(8,128)(2,1)S(1)} %concatenate.3.refs_2_.refs_10_), channel_id=1, source_target_pairs={{0,32},{1,33},{2,34},{3,35},{4,36},{5,37},{6,38},{7,39},{8,40},{9,... | collective-permute-start | bytes 1425416 | tf_op jit(solution)/shard_map/ppermute | solution.py:39
  7.9 14.7 %collective-permute-start.6 = (bf16[64,3712]{1,0:T(8,128)(2,1)S(1)}, bf16[64,3712]{1,0:T(8,128)(2,1)S(1)}, u32[]{:S(2)}, u32[]{:S(2)}) collective-permute-start(bf16[64,3712]{1,0:T(8,128)(2,1)S(1)} %concatenate.3.refs_2_.refs_10_), channel_id=1, source_target_pairs={{0,37},{1,36},{2,39},{3,38},{4,33},{5,32},{6,35},{7,34},{8,45},{9,... | collective-permute-start | bytes 1425416 | tf_op jit(solution)/shard_map/ppermute | solution.py:39
  11.4 17.4 %copy-start.4 = (bf16[64,3712]{1,0:T(8,128)(2,1)}, bf16[64,3712]{1,0:T(8,128)(2,1)S(1)}, u32[]{:S(2)}) copy-start(bf16[64,3712]{1,0:T(8,128)(2,1)S(1)} %collective-permute-done.1.refs_4_.refs_12_) | copy-start | bytes 1425412
  11.4 13.7 %collective-permute-start.3 = (bf16[64,3712]{1,0:T(8,128)(2,1)S(1)}, bf16[64,3712]{1,0:T(8,128)(2,1)S(1)}, u32[]{:S(2)}, u32[]{:S(2)}) collective-permute-start(bf16[64,3712]{1,0:T(8,128)(2,1)S(1)} %collective-permute-done.1.refs_4_.refs_12_), channel_id=1, source_target_pairs={{0,32},{1,33},{2,34},{3,35},{4,36},{5,37},{6,38},{7,39},{8,40},{9,... | collective-permute-start | bytes 1425416 | tf_op jit(solution)/shard_map/ppermute | solution.py:39
  17.5 11.3 %copy-start.5 = (bf16[64,3712]{1,0:T(8,128)(2,1)}, bf16[64,3712]{1,0:T(8,128)(2,1)S(1)}, u32[]{:S(2)}) copy-start(bf16[64,3712]{1,0:T(8,128)(2,1)S(1)} %collective-permute-done.2.refs_5_.refs_13_) | copy-start | bytes 1425412
  17.6 8.7 %collective-permute-start.4 = (bf16[64,3712]{1,0:T(8,128)(2,1)S(1)}, bf16[64,3712]{1,0:T(8,128)(2,1)S(1)}, u32[]{:S(2)}, u32[]{:S(2)}) collective-permute-start(bf16[64,3712]{1,0:T(8,128)(2,1)S(1)} %collective-permute-done.2.refs_5_.refs_13_), channel_id=1, source_target_pairs={{0,4},{1,5},{2,6},{3,7},{4,0},{5,1},{6,2},{7,3},{8,12},{9,13},{10,... | collective-permute-start | bytes 1425416 | tf_op jit(solution)/shard_map/ppermute | solution.py:39
  20.0 8.8 %copy-start.6 = (bf16[64,3712]{1,0:T(8,128)(2,1)}, bf16[64,3712]{1,0:T(8,128)(2,1)S(1)}, u32[]{:S(2)}) copy-start(bf16[64,3712]{1,0:T(8,128)(2,1)S(1)} %collective-permute-done.refs_3_.refs_11_) | copy-start | bytes 1425412
  20.0 8.8 %collective-permute-start.5 = (bf16[64,3712]{1,0:T(8,128)(2,1)S(1)}, bf16[64,3712]{1,0:T(8,128)(2,1)}, u32[]{:S(2)}, u32[]{:S(2)}) collective-permute-start(bf16[64,3712]{1,0:T(8,128)(2,1)S(1)} %collective-permute-done.refs_3_.refs_11_), channel_id=1, source_target_pairs={{0,1},{1,0},{2,3},{3,2},{4,5},{5,4},{6,7},{7,6},{8,9},{9,8},{10,11... | collective-permute-start | bytes 1425416 | tf_op jit(solution)/shard_map/ppermute | solution.py:39
  22.5 6.3 %copy-start.7 = (bf16[64,3712]{1,0:T(8,128)(2,1)}, bf16[64,3712]{1,0:T(8,128)(2,1)S(1)}, u32[]{:S(2)}) copy-start(bf16[64,3712]{1,0:T(8,128)(2,1)S(1)} %collective-permute-done.6.refs_9_.refs_17_) | copy-start | bytes 1425412
  25.1 3.7 %copy-start.8 = (bf16[64,3712]{1,0:T(8,128)(2,1)}, bf16[64,3712]{1,0:T(8,128)(2,1)S(1)}, u32[]{:S(2)}) copy-start(bf16[64,3712]{1,0:T(8,128)(2,1)S(1)} %collective-permute-done.3.refs_6_.refs_14_) | copy-start | bytes 1425412
  26.2 2.6 %copy-start.9 = (bf16[64,3712]{1,0:T(8,128)(2,1)}, bf16[64,3712]{1,0:T(8,128)(2,1)S(1)}, u32[]{:S(2)}) copy-start(bf16[64,3712]{1,0:T(8,128)(2,1)S(1)} %collective-permute-done.4.refs_7_.refs_15_) | copy-start | bytes 1425412
  34.9 10.8 %collective-permute-start.7 = (bf16[512,3584]{1,0:T(8,128)(2,1)}, bf16[512,3584]{1,0:T(8,128)(2,1)}, u32[]{:S(2)}, u32[]{:S(2)}) collective-permute-start(bf16[512,3584]{1,0:T(8,128)(2,1)} %get-tuple-element.10), channel_id=1, source_target_pairs={{0,16},{1,17},{2,18},{3,19},{4,20},{5,21},{6,22},{7,23},{8,24},{9,... | collective-permute-start | bytes 11010056 | tf_op jit(solution)/shard_map/ppermute | solution.py:43
  37.8 6.5 %copy-start.11 = (bf16[512,128]{1,0:T(8,128)(2,1)S(1)}, bf16[512,128]{1,0:T(8,128)(2,1)}, u32[]{:S(2)}) copy-start(bf16[512,128]{1,0:T(8,128)(2,1)} %get-tuple-element.8) | copy-start | bytes 393220
  37.8 36.1 %all-to-all-start = ((bf16[8,64,3584]{2,1,0:T(8,128)(2,1)}), bf16[8,64,3584]{2,1,0:T(8,128)(2,1)}, u32[]{:S(2)}, u32[]{:S(2)}) async-start(bf16[8,64,3584]{2,1,0:T(8,128)(2,1)} %bitcast.42), calls=%async_computation | async-start | bytes 7340032 | tf_op jit(solution)/shard_map/all_to_all | solution.py:58
  44.3 1.4 collective-permute-start.8
  74.0 4.6 %copy-start.12 = (s32[8,1]{1,0:T(8,128)S(1)}, s32[8,1]{1,0:T(8,128)}, u32[]{:S(2)}) copy-start(s32[8,1]{1,0:T(8,128)} %constant.76) | copy-start | bytes 100
  74.0 4.6 %copy-start.13 = (s32[8,1]{1,0:T(8,128)S(1)}, s32[8,1]{1,0:T(8,128)}, u32[]{:S(2)}) copy-start(s32[8,1]{1,0:T(8,128)} %constant.77) | copy-start | bytes 100
  74.0 4.6 %copy-start.14 = (s32[8,1]{1,0:T(8,128)S(1)}, s32[8,1]{1,0:T(8,128)}, u32[]{:S(2)}) copy-start(s32[8,1]{1,0:T(8,128)} %constant.78) | copy-start | bytes 100
  74.0 32.9 %all-to-all-start.1 = ((bf16[8,64,3584]{2,1,0:T(8,128)(2,1)}), bf16[8,64,3584]{2,1,0:T(8,128)(2,1)}, u32[]{:S(2)}, u32[]{:S(2)}) async-start(bf16[8,64,3584]{2,1,0:T(8,128)(2,1)} %bitcast.40), calls=%async_computation.1 | async-start | bytes 7340032 | tf_op jit(solution)/shard_map/all_to_all | solution.py:58
  106.9 34.0 %all-to-all-start.2 = ((bf16[8,64,3584]{2,1,0:T(8,128)(2,1)}), bf16[8,64,3584]{2,1,0:T(8,128)(2,1)}, u32[]{:S(2)}, u32[]{:S(2)}) async-start(bf16[8,64,3584]{2,1,0:T(8,128)(2,1)} %bitcast.35), calls=%async_computation.2 | async-start | bytes 7340032 | tf_op jit(solution)/shard_map/all_to_all | solution.py:58
  140.9 6.8 %collective-permute-start.9 = (bf16[512,3584]{1,0:T(8,128)(2,1)}, bf16[512,3584]{1,0:T(8,128)(2,1)}, u32[]{:S(2)}, u32[]{:S(2)}) collective-permute-start(bf16[512,3584]{1,0:T(8,128)(2,1)} %follow.4), channel_id=1, source_target_pairs={{0,16},{1,17},{2,18},{3,19},{4,20},{5,21},{6,22},{7,23},{8,24},{9,... | collective-permute-start | bytes 11010056 | tf_op jit(solution)/shard_map/ppermute | solution.py:43
  147.7 32.7 %copy-start.2 = (bf16[512,3584]{1,0:T(8,128)(2,1)S(1)}, bf16[512,3584]{1,0:T(8,128)(2,1)}, u32[]{:S(2)}) copy-start(bf16[512,3584]{1,0:T(8,128)(2,1)} %convolution_convert_fusion.1.after_ref) | copy-start | bytes 11010052
  182.7 8.6 %collective-permute-start.11 = (bf16[64,3584]{1,0:T(8,128)(2,1)S(1)}, bf16[64,3584]{1,0:T(8,128)(2,1)S(1)}, u32[]{:S(2)}, u32[]{:S(2)}) collective-permute-start(bf16[64,3584]{1,0:T(8,128)(2,1)S(1)} %get-tuple-element.16), channel_id=1, source_target_pairs={{0,1},{1,0},{2,3},{3,2},{4,5},{5,4},{6,7},{7,6},{8,9},{9,8},{10,11... | collective-permute-start | bytes 1376264 | tf_op jit(solution)/shard_map/ppermute | solution.py:39
  182.8 8.6 %collective-permute-start.13 = (bf16[64,3584]{1,0:T(8,128)(2,1)S(1)}, bf16[64,3584]{1,0:T(8,128)(2,1)S(1)}, u32[]{:S(2)}, u32[]{:S(2)}) collective-permute-start(bf16[64,3584]{1,0:T(8,128)(2,1)S(1)} %get-tuple-element.15), channel_id=1, source_target_pairs={{0,32},{1,33},{2,34},{3,35},{4,36},{5,37},{6,38},{7,39},{8,40},{9,... | collective-permute-start | bytes 1376264 | tf_op jit(solution)/shard_map/ppermute | solution.py:39
  182.9 8.6 %collective-permute-start.15 = (bf16[64,3584]{1,0:T(8,128)(2,1)S(1)}, bf16[64,3584]{1,0:T(8,128)(2,1)S(1)}, u32[]{:S(2)}, u32[]{:S(2)}) collective-permute-start(bf16[64,3584]{1,0:T(8,128)(2,1)S(1)} %get-tuple-element.14), channel_id=1, source_target_pairs={{0,4},{1,5},{2,6},{3,7},{4,0},{5,1},{6,2},{7,3},{8,12},{9,13},{10,... | collective-permute-start | bytes 1376264 | tf_op jit(solution)/shard_map/ppermute | solution.py:39
  183.0 16.3 %collective-permute-start.10 = (bf16[64,3584]{1,0:T(8,128)(2,1)S(1)}, bf16[64,3584]{1,0:T(8,128)(2,1)S(1)}, u32[]{:S(2)}, u32[]{:S(2)}) collective-permute-start(bf16[64,3584]{1,0:T(8,128)(2,1)S(1)} %get-tuple-element.13), channel_id=1, source_target_pairs={{0,37},{1,36},{2,39},{3,38},{4,33},{5,32},{6,35},{7,34},{8,45},{9,... | collective-permute-start | bytes 1376264 | tf_op jit(solution)/shard_map/ppermute | solution.py:39
  191.8 10.9 %collective-permute-start.12 = (bf16[64,3584]{1,0:T(8,128)(2,1)S(1)}, bf16[64,3584]{1,0:T(8,128)(2,1)S(1)}, u32[]{:S(2)}, u32[]{:S(2)}) collective-permute-start(bf16[64,3584]{1,0:T(8,128)(2,1)S(1)} %get-tuple-element.17), channel_id=1, source_target_pairs={{0,32},{1,33},{2,34},{3,35},{4,36},{5,37},{6,38},{7,39},{8,40},{9,... | collective-permute-start | bytes 1376264 | tf_op jit(solution)/shard_map/ppermute | solution.py:39
  193.8 8.9 %collective-permute-start.14 = (bf16[64,3584]{1,0:T(8,128)(2,1)S(1)}, bf16[64,3584]{1,0:T(8,128)(2,1)S(1)}, u32[]{:S(2)}, u32[]{:S(2)}) collective-permute-start(bf16[64,3584]{1,0:T(8,128)(2,1)S(1)} %get-tuple-element.19), channel_id=1, source_target_pairs={{0,4},{1,5},{2,6},{3,7},{4,0},{5,1},{6,2},{7,3},{8,12},{9,13},{10,... | collective-permute-start | bytes 1376264 | tf_op jit(solution)/shard_map/ppermute | solution.py:39
  193.8 10.3 %collective-permute-start.16 = (bf16[64,3584]{1,0:T(8,128)(2,1)S(1)}, bf16[64,3584]{1,0:T(8,128)(2,1)S(1)}, u32[]{:S(2)}, u32[]{:S(2)}) collective-permute-start(bf16[64,3584]{1,0:T(8,128)(2,1)S(1)} %get-tuple-element.18), channel_id=1, source_target_pairs={{0,1},{1,0},{2,3},{3,2},{4,5},{5,4},{6,7},{7,6},{8,9},{9,8},{10,11... | collective-permute-start | bytes 1376264 | tf_op jit(solution)/shard_map/ppermute | solution.py:39
  (3 other events, 4.5 us)
